TPU v7x, 768 devices: a whole 4x8x12 slice. The times are simulated.
768 devices in a mesh: fsdp: 12 (over z_hi, x), tensor: 64 (over z_lo, y, core).
Axes of the slice: x: 4, y: 8, z: 12 (z_hi: 3, z_lo: 4; z = z_hi * 4 + z_lo), core: 2. Of those that a mesh axis runs over, the one named last changes fastest.
Arguments:
- hidden: bfloat16 [1536, 53248], P('fsdp', 'tensor'), may hold values from -6 to 6
- down_weight: bfloat16 [53248, 12288], P('tensor', 'fsdp'), may hold values from -0.02734375 to 0.02734375
- act_exponent: int32 [1536, 832], P('fsdp', 'tensor'), may hold values from -2 to 0
- clip_index: int32 [832], P('tensor'), may hold values from 0 to 3
- weight_exponent: int32 [12288], P('fsdp'), may hold values from -9 to -8
Outputs:
- projected: bfloat16 [1536, 12288], P('tensor', 'fsdp')
All inputs are finite; a program needn't handle non-finite values.
Results may differ from a plain program's by a relative error of at most 0.0053.
Values may be sent and summed in bfloat16 or wider, within the bound.
No kernel may reach another device: no remote copies, remote signals or barrier semaphores. Data moves between devices by JAX's collectives and lax.ppermute only.
A program may use at most 32 MiB of HBM per device.

v0:
```python
import math

import jax
import jax.numpy as jnp
from jax import lax
from jax.sharding import PartitionSpec as P


def walsh_matrix(order_size):
    indices = jnp.arange(order_size, dtype=jnp.int32)
    shared = indices[:, None] & indices[None, :]
    parity = jnp.zeros((order_size, order_size), jnp.int32)
    for bit_level in range(order_size.bit_length() - 1):
        parity = parity ^ shared >> bit_level & 1
    return (1 - 2 * parity).astype(jnp.float32)


def soft_round(values):
    return values - jnp.sin(2.0 * math.pi * values) / (2.0 * math.pi)


def quantize_rows(rotated, act_exponent, clip_index):
    row_count, unit_count = rotated.shape
    scaling = jnp.exp2(act_exponent.astype(jnp.float32))[:, :, None]
    clip_level = (7.5 - clip_index.astype(jnp.float32))[None, :, None]
    grouped = rotated.reshape(row_count, unit_count // 64, 64) / scaling
    clipped = jnp.clip(grouped, -clip_level, clip_level)
    return (soft_round(clipped) * scaling).reshape(row_count, unit_count).astype(jnp.bfloat16)


def quantize_weight(weight_matrix, weight_exponent):
    scaling = jnp.exp2(weight_exponent.astype(jnp.float32))[None, :]
    clipped = jnp.clip(weight_matrix.astype(jnp.float32) / scaling, -7.5, 7.5)
    return (soft_round(clipped) * scaling).astype(jnp.bfloat16)


def shards(hidden, down_weight, act_exponent, clip_index, weight_exponent):
    tensor_size = lax.axis_size("tensor")
    row_count, unit_count = hidden.shape
    normalizer = 1.0 / math.sqrt(64.0 * tensor_size)
    local_walsh = walsh_matrix(64).astype(jnp.bfloat16)
    arrived = lax.all_to_all(
        hidden.reshape(row_count, 1, unit_count), "tensor", split_axis=0, concat_axis=1, tiled=True
    )
    slice_rows = arrived.shape[0]
    local_mixed = jnp.dot(arrived.reshape(-1, 64), local_walsh, preferred_element_type=jnp.float32)
    local_mixed = local_mixed.reshape(slice_rows, tensor_size, unit_count // 64, 64)
    mixed = (
        jnp.einsum(
            "st,ktce->ksce", walsh_matrix(tensor_size), local_mixed, precision=lax.Precision.HIGHEST
        ).reshape(slice_rows, tensor_size, unit_count)
        * normalizer
    )
    returned = lax.all_to_all(mixed, "tensor", split_axis=1, concat_axis=0, tiled=True)
    rotated = returned.reshape(row_count, unit_count)
    quantized = quantize_rows(rotated, act_exponent, clip_index)
    weight_q = quantize_weight(down_weight, weight_exponent)
    partial_sum = jnp.dot(
        lax.all_gather(quantized, "fsdp", axis=0, tiled=True),
        weight_q,
        preferred_element_type=jnp.float32,
    )
    summed = lax.psum_scatter(partial_sum, "tensor", scatter_dimension=0, tiled=True)
    return summed.astype(jnp.bfloat16)


def solution(mesh):
    placed = (P("fsdp", "tensor"), P("tensor", "fsdp"), P("fsdp", "tensor"), P("tensor"), P("fsdp"))
    return jax.shard_map(
        shards, mesh=mesh, in_specs=placed, out_specs=P("tensor", "fsdp"), check_vma=False
    )
```

profile of v0, /device:TPU:4, one launch (start us, length us, event | category | flops | bytes accessed | tf_op | source)
XLA Modules:
  0.0 483.3 jit_solution(7542523399400070804)
XLA Ops:
  6.5 0.5 broadcast.116
  7.0 1.7 reduce.1
  8.7 0.2 copy.34
  8.9 0.1 reshape.30
  9.0 25.3 %all_to_all.30 = bf16[64,2,832]{2,1,0:T(2,128)(2,1)S(1)} all-to-all(bf16[64,2,832]{2,1,0:T(2,128)(2,1)S(1)} %reshape.30), channel_id=1, replica_groups=mesh['fsdp'=12,'tensor'=64] {'tensor'}, dimensions={0} | all-to-all | bytes 425984 | tf_op jit(solution)/shard_map/all_to_all | solution.py:42
  34.3 0.2 reshape.31
  34.5 1.4 reduce
  36.0 0.1 all_to_all.23
  36.1 0.3 reshape.26
  36.4 0.3 convolution_bitcast_fusion
  36.7 0.0 copy-start.3
  36.7 0.0 copy-start
  36.7 0.3 copy.24
  37.0 0.1 reshape.27
  37.1 0.0 copy-start.1
  37.2 1.6 convolution_multiply_fusion
  38.8 0.0 copy-start.2
  38.8 1.1 copy.26
  39.8 4.9 %all-to-all-start.1 = ((f32[2,64,832]{2,0,1:T(2,128)}), f32[2,64,832]{2,0,1:T(2,128)S(1)}, u32[]{:S(2)}, u32[]{:S(2)}) async-start(f32[2,64,832]{2,0,1:T(2,128)} %copy.26), calls=%async_computation.1 | async-start | bytes 917504 | tf_op jit(solution)/shard_map/all_to_all | solution.py:54
  44.8 0.0 all-gather.2.cloned.1.call-start
  44.8 0.0 copy-done.3
  44.8 0.1 min.25
  44.9 0.1 min.26
  45.0 0.1 max.23
  45.1 0.1 max.24
  45.1 0.0 copy-done
  45.2 0.2 copy.27
  45.4 15.2 %all-to-all-done.1 = f32[2,64,832]{2,0,1:T(2,128)S(1)} async-done(((f32[2,64,832]{2,0,1:T(2,128)}), f32[2,64,832]{2,0,1:T(2,128)S(1)}, u32[]{:S(2)}, u32[]{:S(2)}) %all-to-all-start.1) | async-done | bytes 426016 | tf_op jit(solution)/shard_map/all_to_all | solution.py:54
  60.6 0.3 reshape_reshape.3
  60.9 2.3 multiply_convert_fusion.2
  63.2 0.0 all-gather.2.cloned.1.call-update
  63.2 0.2 reduce-scatter.2.cloned.1.call-start
  63.4 0.0 copy-done.1
  63.5 98.3 %all-gather.2.cloned.1.call-done = bf16[1536,832]{1,0:T(8,128)(2,1)} async-done(((bf16[128,832]{1,0:T(8,128)(2,1)}), bf16[1536,832]{1,0:T(8,128)(2,1)}) %all-gather.2.cloned.1.call-update) | async-done | bytes 2555920 | tf_op jit(solution)/shard_map/all_gather | solution.py:59
  161.8 0.0 copy-done.2
  161.8 17.4 %fusion = f32[1536,1024]{1,0:T(8,128)} fusion(bf16[1536,832]{1,0:T(8,128)(2,1)} %all-gather.2.cloned.1.call-done, bf16[832,1024]{1,0:T(8,128)(2,1)S(1)} %copy-done.2, f32[1024]{0:T(1024)S(1)} %multiply_exponential_fusion.1), kind=kOutput, calls=%fused_computation.2 | convolution fusion | flops 2624061440 | bytes 10555392 | tf_op jit(solution)/shard_map/dot_general | solution.py:58
  179.2 0.0 reduce-scatter.2.cloned.1.call-update
  179.2 295.7 %reduce-scatter.2.cloned.1.call-done = f32[24,1024]{1,0:T(8,128)} async-done(((f32[1536,1024]{1,0:T(8,128)}), f32[24,1024]{1,0:T(8,128)}) %reduce-scatter.2.cloned.1.call-update) | async-done | bytes 98320 | tf_op jit(solution)/shard_map/reduce_scatter | solution.py:63
  474.9 1.5 convert_element_type.38
  (5 shorter events, 0.1 us)
Async XLA Ops:
  36.7 8.1 %copy-start.3 = (s32[13]{0:T(128)S(1)}, s32[13]{0:T(128)}, u32[]{:S(2)}) copy-start(s32[13]{0:T(128)} %param.8) | copy-start | bytes 160
  36.7 8.4 %copy-start = (s32[128,13]{0,1:T(8,128)S(1)}, s32[128,13]{0,1:T(8,128)}, u32[]{:S(2)}) copy-start(s32[128,13]{0,1:T(8,128)} %param.7) | copy-start | bytes 19972
  37.1 26.3 %copy-start.1 = (s32[1024]{0:T(1024)S(1)}, s32[1024]{0:T(1024)}, u32[]{:S(2)}) copy-start(s32[1024]{0:T(1024)} %param.9) | copy-start | bytes 12292
  38.8 123.0 %copy-start.2 = (bf16[832,1024]{1,0:T(8,128)(2,1)S(1)}, bf16[832,1024]{1,0:T(8,128)(2,1)}, u32[]{:S(2)}) copy-start(bf16[832,1024]{1,0:T(8,128)(2,1)} %param.6) | copy-start | bytes 5111812
  39.8 20.7 %all-to-all-start.1 = ((f32[2,64,832]{2,0,1:T(2,128)}), f32[2,64,832]{2,0,1:T(2,128)S(1)}, u32[]{:S(2)}, u32[]{:S(2)}) async-start(f32[2,64,832]{2,0,1:T(2,128)} %copy.26), calls=%async_computation.1 | async-start | bytes 917504 | tf_op jit(solution)/shard_map/all_to_all | solution.py:54
  44.8 117.0 %all-gather.2.cloned.1.call-start = ((), (), s32[]{:S(2)}) async-start(), calls=%async_computation.3 | async-start | bytes 2981888 | tf_op jit(solution)/shard_map/all_gather | solution.py:59
  63.2 411.7 %reduce-scatter.2.cloned.1.call-start = ((), (), s32[]{:S(2)}) async-start(), calls=%async_computation.4 | async-start | bytes 6389760 | tf_op jit(solution)/shard_map/reduce_scatter | solution.py:63
Sparse Core Ops, SparseCore 0:
  63.3 98.3 all-gather.1
  179.3 295.5 reduce-scatter.1
where the time goes:
time: 484 us; the launch traced here: 483 us
  waiting for transfers between devices  409 us (85%)
  blocking collectives  25.3 us (5%)
  matrix products  19.4 us (4%)
  between operations  13.5 us (3%)
  other arithmetic  6.95 us (1%)
  starting transfers between devices  5.2 us (1%)
    reduce_scatter x1, waiting for transfers between devices, shards(): lax.psum_scatter(partial_sum, 'tensor', scatter_dimension=0, tiled=True)  296 us
    all_gather x1, waiting for transfers between devices, shards(): lax.all_gather(quantized, 'fsdp', axis=0, tiled=True)  98.3 us
    all_to_all x1, blocking collectives, shards(): lax.all_to_all(hidden.reshape(row_count, 1, unit_count), 'tensor', split_...  25.3 us
    dot_general x1, matrix products, shards(): jnp.dot(lax.all_gather(quantized, 'fsdp', axis=0, tiled=True), weight_q,...  17.4 us
    all_to_all x1, waiting for transfers between devices, shards(): lax.all_to_all(mixed, 'tensor', split_axis=1, concat_axis=0, tiled=True)  15.2 us
  transfers between devices with their start and end apart: 3, of which 3 were waited for; matrix products, arithmetic and copies ran while one was open for 0% of the time, Pallas kernels for 0%

commit v1 on v0

v1 whole, which is shorter than its diff:
```python
import math

import jax
import jax.numpy as jnp
import numpy as np
from jax import lax
from jax.experimental import pallas as pl
from jax.experimental.pallas import tpu as pltpu
from jax.sharding import Mesh, PartitionSpec as P

AXES = ("h", "x", "l", "yh", "yl", "c")
SIZES = (3, 4, 4, 4, 2, 2)
TENSOR = ("l", "yh", "yl", "c")
SLOTS = (0, 1, 3, 2)
WIDTH = 896


def sine_coefficients():
    nodes = 0.25 * (1.0 + np.cos(np.pi * (np.arange(400) + 0.5) / 400)) ** 1.0
    squares = nodes**2
    target = np.sin(2.0 * np.pi * nodes) / (2.0 * np.pi)
    table = np.stack([nodes * squares**power for power in range(8)], axis=1)
    solved = np.linalg.lstsq(table, target, rcond=None)[0]
    return [float(entry) for entry in solved]


SINE = sine_coefficients()


def soft_round(values):
    rest = values - jnp.round(values)
    squares = rest * rest
    total = jnp.full_like(rest, SINE[-1])
    for entry in SINE[-2::-1]:
        total = total * squares + entry
    return values - rest * total


def walsh(order):
    indices = np.arange(order)
    shared = indices[:, None] & indices[None, :]
    parity = np.zeros((order, order), np.int64)
    for bit_level in range(order.bit_length() - 1):
        parity ^= shared >> bit_level & 1
    return (1 - 2 * parity).astype(np.float32)


def rotate_kernel(x_ref, rows_ref, lanes_ref, spread_ref, out_ref):
    arrived = x_ref[...]
    mixed = jnp.dot(rows_ref[...], arrived, preferred_element_type=jnp.float32)
    extra = arrived[:, 768:896]
    lanes = lanes_ref[...]
    for piece in range(7):
        width = 128 if piece < 6 else 64
        rest = mixed[:, piece * 128 : piece * 128 + 128]
        rotated = None
        for _ in range(3):
            part = rest.astype(jnp.bfloat16)
            rest = rest - part.astype(jnp.float32)
            term = jnp.dot(part, lanes, preferred_element_type=jnp.float32)
            rotated = term if rotated is None else rotated + term
        scale, inverse, level = (
            jnp.dot(
                extra,
                spread_ref[kind, :, piece * 128 : piece * 128 + 128],
                preferred_element_type=jnp.float32,
            )
            for kind in range(3)
        )
        scaled = rotated * (1.0 / 64.0) * inverse
        clipped = jnp.maximum(jnp.minimum(scaled, level), -level)
        quantized = (soft_round(clipped) * scale).astype(jnp.bfloat16)
        out_ref[:, piece * 128 : piece * 128 + width] = quantized[:, :width]


def rotate_and_quantize(arrived):
    rows = np.kron(walsh(64), np.eye(2, dtype=np.float32))
    lanes = np.kron(np.eye(2, dtype=np.float32), walsh(64))
    spread = np.zeros((3, 128, WIDTH), np.float32)
    for kind in range(3):
        for group in range(13):
            spread[kind, 64 + 13 * kind + group, 64 * group : 64 * group + 64] = 1.0
    return pl.pallas_call(
        rotate_kernel,
        out_shape=jax.ShapeDtypeStruct((128, 832), jnp.bfloat16),
        in_specs=[pl.BlockSpec(memory_space=pltpu.VMEM)] * 4,
        out_specs=pl.BlockSpec(memory_space=pltpu.VMEM),
        compiler_params=pltpu.CompilerParams(vmem_limit_bytes=24 * 1024 * 1024),
        cost_estimate=pl.CostEstimate(flops=400_000_000, bytes_accessed=1_500_000, transcendentals=0),
    )(
        arrived,
        jnp.asarray(rows, jnp.bfloat16),
        jnp.asarray(lanes, jnp.bfloat16),
        jnp.asarray(spread, jnp.bfloat16),
    )


def quantize_weight(weight_matrix, weight_exponent):
    scaling = jnp.exp2(weight_exponent.astype(jnp.float32)).astype(jnp.bfloat16).astype(jnp.float32)[None, :]
    clipped = jnp.clip(weight_matrix.astype(jnp.float32) / scaling, -7.5, 7.5)
    return (soft_round(clipped) * scaling).astype(jnp.bfloat16)


def ring(size, shift):
    return [(at, (at + shift) % size) for at in range(size)]


def final_pairs(which):
    pairs = []
    for x in range(4):
        for slot in range(4):
            for y in range(8):
                for c in range(2):
                    first = 3 * (2 * y + c)
                    if which == "main":
                        k = (first + 1) // 16
                    elif first // 16 != (first + 1) // 16:
                        k = first // 16
                    elif (first + 2) // 16 != (first + 1) // 16:
                        k = (first + 2) // 16
                    else:
                        continue
                    owner_l = (4 * ((k - x) % 3) + x) // 3
                    owner_x = (x + SLOTS[slot]) % 4
                    source = ((x * 4 + slot) * 8 + y) * 2 + c
                    pairs.append((source, ((owner_x * 4 + owner_l) * 8 + y) * 2 + c))
    return pairs


def row_order(h, x, y_low, c):
    at = lax.broadcasted_iota(jnp.int32, (384, 384), 0)
    source = lax.broadcasted_iota(jnp.int32, (384, 384), 1)
    core = jnp.where(at < 192, 1 - c, c)
    rest = at % 192
    parity = jnp.where(rest < 96, 1 - y_low, y_low)
    rest = rest % 96
    y = 2 * (rest // 24) + parity
    row = (2 * y + core) * 24 + rest % 24
    shifted = (row - 128 * ((h + x) % 3) + 384) % 384
    return (source == shifted).astype(jnp.bfloat16)


def shards(hidden, down_weight, act_exponent, clip_index, weight_exponent):
    h, x, y_low, c = (lax.axis_index(name) for name in ("h", "x", "yl", "c"))
    y_high = lax.axis_index("yh")

    weight_0 = quantize_weight(down_weight, weight_exponent)
    weight_1 = lax.ppermute(weight_0, "x", ring(4, -1))
    weight_3 = lax.ppermute(weight_0, "x", ring(4, 1))
    weight_2 = jnp.concatenate(
        [
            lax.ppermute(weight_3[:416], "x", ring(4, 1)),
            lax.ppermute(weight_1[416:], "x", ring(4, -1)),
        ],
        axis=0,
    )

    scaling = jnp.exp2(act_exponent.astype(jnp.float32)).astype(jnp.bfloat16)
    inverse = (1.0 / scaling.astype(jnp.float32)).astype(jnp.bfloat16)
    level = jnp.broadcast_to((7.5 - clip_index.astype(jnp.float32)).astype(jnp.bfloat16)[None, :], (128, 13))
    packed = jnp.concatenate([hidden, scaling, inverse, level, jnp.zeros((128, 25), jnp.bfloat16)], axis=1)
    arrived = lax.all_to_all(packed.reshape(64, 2, WIDTH), TENSOR, split_axis=0, concat_axis=0, tiled=True)
    quantized = rotate_and_quantize(arrived.reshape(128, WIDTH))
    returned = lax.all_to_all(quantized.reshape(64, 2, 832), TENSOR, split_axis=0, concat_axis=0, tiled=True)
    own = returned.reshape(128, 832)
    next_1 = lax.ppermute(own, "h", ring(3, -1))
    next_2 = lax.ppermute(own, "h", ring(3, 1))
    gathered = jnp.concatenate([own, next_1, next_2], axis=0)
    acts = jnp.dot(row_order(h, x, y_low, c), gathered, preferred_element_type=jnp.float32).astype(jnp.bfloat16)

    y_pairs_near = [(y, y ^ 1) for y in range(8)]
    y_pairs_far = [(y, (y - 1) % 8 if y % 2 == 0 else (y + 1) % 8) for y in range(8)]
    parts = []
    for weights, y_pairs in (((weight_0, weight_1), y_pairs_near), ((weight_3, weight_2), y_pairs_far)):
        products = [jnp.dot(acts, weight, preferred_element_type=jnp.float32) for weight in weights]
        other = jnp.stack([product[:192] for product in products]).astype(jnp.bfloat16)
        from_core = lax.ppermute(other, "c", [(0, 1), (1, 0)])
        mine = jnp.stack([product[192:] for product in products]) + from_core.astype(jnp.float32)
        from_y = lax.ppermute(mine[:, :96].astype(jnp.bfloat16), ("yh", "yl"), y_pairs)
        parts.append((mine[:, 96:] + from_y.astype(jnp.float32)).astype(jnp.bfloat16))
    sums = jnp.concatenate(parts, axis=0).reshape(16, 24, 1024)
    crossed = lax.all_to_all(sums, ("l", "yh"), split_axis=0, concat_axis=0, tiled=True)
    total = jnp.sum(crossed.astype(jnp.float32), axis=0).astype(jnp.bfloat16)

    y = 2 * y_high + y_low
    early = jnp.logical_and(y == 2, c == 1)
    late = jnp.logical_and(y == 5, c == 0)
    moved = lax.ppermute(total, ("x", "l", "yh", "yl", "c"), final_pairs("main"))
    fixed = lax.ppermute(
        jnp.where(early, total[:8], total[16:]), ("x", "l", "yh", "yl", "c"), final_pairs("fix")
    )
    return jnp.concatenate(
        [jnp.where(early, fixed, moved[:8]), moved[8:16], jnp.where(late, fixed, moved[16:])], axis=0
    )


def solution(mesh):
    fine = Mesh(mesh.devices.reshape(SIZES), AXES)
    rows, columns = ("h", "x"), TENSOR
    placed = (P(rows, columns), P(columns, rows), P(rows, columns), P(columns), P(rows))
    return jax.shard_map(
        shards, mesh=fine, in_specs=placed, out_specs=P(columns, rows), check_vma=False
    )
```

time: 484 us -> 183 us (0.38)
  the two profiles are of different devices: /device:TPU:4 before, /device:TPU:21 now
where the time goes in v1:
time: 183 us; the launch traced here: 182 us
  waiting for transfers between devices  88 us (48%)
  starting transfers between devices  71.4 us (39%)
  matrix products  7.56 us (4%)
  local copies, waits for them, and re-layouts  6.88 us (4%)
  other arithmetic  6.6 us (4%)
    all_to_all x1, waiting for transfers between devices, shards(): lax.all_to_all(sums, ('l', 'yh'), split_axis=0, concat_axis=0, tiled=True)  18.6 us
    ppermute x1, waiting for transfers between devices, shards(): next_1 = lax.ppermute(own, 'h', ring(3, -1))  16.7 us
    all_to_all x1, starting transfers between devices, shards(): lax.all_to_all(packed.reshape(64, 2, WIDTH), TENSOR, split_axis=0, concat...  13.9 us
    all_to_all x1, waiting for transfers between devices, shards(): lax.all_to_all(packed.reshape(64, 2, WIDTH), TENSOR, split_axis=0, concat...  10.6 us
    ppermute x1, starting transfers between devices, shards(): next_2 = lax.ppermute(own, 'h', ring(3, 1))  10.3 us
    ppermute x2, waiting for transfers between devices, shards(): lax.ppermute(mine[:, :96].astype(jnp.bfloat16), ('yh', 'yl'), y_pairs)  10.3 us
    ppermute x1, waiting for transfers between devices, shards(): lax.ppermute(weight_3[:416], 'x', ring(4, 1))  8.46 us
    ppermute x1, waiting for transfers between devices, shards(): next_2 = lax.ppermute(own, 'h', ring(3, 1))  8.26 us
  transfers between devices with their start and end apart: 15, of which 10 were waited for; matrix products, arithmetic and copies ran while one was open for 8% of the time, Pallas kernels for 0%

profile of v1, /device:TPU:21, one launch (start us, length us, event | category | flops | bytes accessed | tf_op | source)
XLA Modules:
  0.0 181.7 jit_solution(14929969982555529814)
XLA Ops:
  0.0 0.7 subtract_convert_fusion
  0.8 0.7 divide_convert_fusion
  1.5 1.4 concatenate.15
  2.9 0.2 copy.10
  3.1 0.8 reshape.17
  3.9 13.9 %all-to-all-start = ((bf16[64,2,896]{2,1,0:T(2,128)(2,1)}), bf16[64,2,896]{2,1,0:T(2,128)(2,1)S(1)}, u32[]{:S(2)}, u32[]{:S(2)}) async-start(bf16[64,2,896]{2,1,0:T(2,128)(2,1)} %reshape.17), calls=%async_computation | async-start | bytes 458752 | tf_op jit(solution)/shard_map/all_to_all | solution.py:162
  17.8 10.6 %all-to-all-done = bf16[64,2,896]{2,1,0:T(2,128)(2,1)S(1)} async-done(((bf16[64,2,896]{2,1,0:T(2,128)(2,1)}), bf16[64,2,896]{2,1,0:T(2,128)(2,1)S(1)}, u32[]{:S(2)}, u32[]{:S(2)}) %all-to-all-start) | async-done | bytes 229408 | tf_op jit(solution)/shard_map/all_to_all | solution.py:162
  28.3 0.1 reshape.18.x_ref
  28.5 0.7 shard_map.82
  29.2 0.8 reshape.19
  30.0 6.7 %all-to-all-start.1 = ((bf16[64,2,832]{2,1,0:T(2,128)(2,1)}), bf16[64,2,832]{2,1,0:T(2,128)(2,1)}, u32[]{:S(2)}, u32[]{:S(2)}) async-start(bf16[64,2,832]{2,1,0:T(2,128)(2,1)} %reshape.19), calls=%async_computation.1 | async-start | bytes 458752 | tf_op jit(solution)/shard_map/all_to_all | solution.py:164
  36.6 2.7 %multiply_convert_fusion = bf16[832,1024]{1,0:T(8,128)(2,1)S(1)} fusion(bf16[832,1024]{1,0:T(8,128)(2,1)S(1)} %copy-done.3, f32[1024]{0:T(1024)S(1)} %fusion.57), kind=kLoop, calls=%fused_computation.1 | loop fusion | flops 20447232 | bytes 3411968 | tf_op jit(solution)/shard_map/convert_element_type | solution.py:101
  39.3 2.8 %collective-permute-start.5 = (bf16[832,1024]{1,0:T(8,128)(2,1)S(1)}, bf16[832,1024]{1,0:T(8,128)(2,1)S(1)}, u32[]{:S(2)}, u32[]{:S(2)}) collective-permute-start(bf16[832,1024]{1,0:T(8,128)(2,1)S(1)} %multiply_convert_fusion), channel_id=1, source_target_pairs={{0,64},{64,128},{128,192},{192,0},{1,65},{65,129},{129,193},{193,1... | collective-permute-start | bytes 5111816 | tf_op jit(solution)/shard_map/ppermute | solution.py:149
  42.2 2.5 %collective-permute-start.2 = (bf16[832,1024]{1,0:T(8,128)(2,1)S(1)}, bf16[832,1024]{1,0:T(8,128)(2,1)}, u32[]{:S(2)}, u32[]{:S(2)}) collective-permute-start(bf16[832,1024]{1,0:T(8,128)(2,1)S(1)} %multiply_convert_fusion), channel_id=1, source_target_pairs={{0,192},{64,0},{128,64},{192,128},{1,193},{65,1},{129,65},{193,129... | collective-permute-start | bytes 5111816 | tf_op jit(solution)/shard_map/ppermute | solution.py:148
  44.7 2.6 %all-to-all-done.1 = bf16[64,2,832]{2,1,0:T(2,128)(2,1)} async-done(((bf16[64,2,832]{2,1,0:T(2,128)(2,1)}), bf16[64,2,832]{2,1,0:T(2,128)(2,1)}, u32[]{:S(2)}, u32[]{:S(2)}) %all-to-all-start.1) | async-done | bytes 213024 | tf_op jit(solution)/shard_map/all_to_all | solution.py:164
  47.3 1.8 reshape.20
  49.1 10.3 %collective-permute-start.1 = (bf16[128,832]{1,0:T(8,128)(2,1)}, bf16[128,832]{1,0:T(8,128)(2,1)S(1)}, u32[]{:S(2)}, u32[]{:S(2)}) collective-permute-start(bf16[128,832]{1,0:T(8,128)(2,1)} %reshape.20), channel_id=1, source_target_pairs={{0,256},{256,512},{512,0},{1,257},{257,513},{513,1},{2,258},{258,5... | collective-permute-start | bytes 638984 | tf_op jit(solution)/shard_map/ppermute | solution.py:167
  59.4 3.2 %collective-permute-start = (bf16[128,832]{1,0:T(8,128)(2,1)}, bf16[128,832]{1,0:T(8,128)(2,1)S(1)}, u32[]{:S(2)}, u32[]{:S(2)}) collective-permute-start(bf16[128,832]{1,0:T(8,128)(2,1)} %reshape.20), channel_id=1, source_target_pairs={{0,512},{256,0},{512,256},{1,513},{257,1},{513,257},{2,514},{258,2... | collective-permute-start | bytes 638984 | tf_op jit(solution)/shard_map/ppermute | solution.py:166
  62.6 8.3 %collective-permute-done.1 = bf16[128,832]{1,0:T(8,128)(2,1)S(1)} collective-permute-done((bf16[128,832]{1,0:T(8,128)(2,1)}, bf16[128,832]{1,0:T(8,128)(2,1)S(1)}, u32[]{:S(2)}, u32[]{:S(2)}) %collective-permute-start.1) | collective-permute-done | bytes 213024 | tf_op jit(solution)/shard_map/ppermute | solution.py:167
  70.8 16.7 %collective-permute-done = bf16[128,832]{1,0:T(8,128)(2,1)S(1)} collective-permute-done((bf16[128,832]{1,0:T(8,128)(2,1)}, bf16[128,832]{1,0:T(8,128)(2,1)S(1)}, u32[]{:S(2)}, u32[]{:S(2)}) %collective-permute-start) | collective-permute-done | bytes 213024 | tf_op jit(solution)/shard_map/ppermute | solution.py:166
  87.6 2.1 %convolution_convert_fusion = bf16[384,832]{0,1:T(8,128)(2,1)S(1)} fusion(bf16[128,832]{1,0:T(8,128)(2,1)S(1)} %collective-permute-done.1, bf16[128,832]{1,0:T(8,128)(2,1)S(1)} %collective-permute-done, bf16[128,832]{1,0:T(8,128)(2,1)} %reshape.20, s32[]{:T(128)S(6)} %mul_shard_map.3, s32[384]{0:T(512)S(1)} %fusion.62, s32[]{:T(128)S(6)} %axis_index.56, ...), kind=kOutput, calls=%fused_computation.18 | convolution fusion | flops 252911616 | bytes 1282956 | tf_op jit(solution)/shard_map/dot_general | solution.py:169
  89.7 1.0 fusion.72
  90.9 2.8 %collective-permute-start.6 = (bf16[416,1024]{1,0:T(8,128)(2,1)S(1)}, bf16[416,1024]{1,0:T(8,128)(2,1)S(1)}, u32[]{:S(2)}, u32[]{:S(2)}) collective-permute-start(bf16[416,1024]{1,0:T(8,128)(2,1)S(1)} %slice.89), channel_id=1, source_target_pairs={{0,64},{64,128},{128,192},{192,0},{1,65},{65,129},{129,193},{193,1... | collective-permute-start | bytes 2555912 | tf_op jit(solution)/shard_map/ppermute | solution.py:152
  93.7 2.5 %fusion.73 = f32[384,1024]{1,0:T(8,128)S(1)} fusion(bf16[384,832]{0,1:T(8,128)(2,1)S(1)} %convolution_convert_fusion, bf16[832,1024]{1,0:T(8,128)(2,1)} %collective-permute-done.2), kind=kOutput, calls=%fused_computation.112 | convolution fusion | flops 654311424 | bytes 3915776 | tf_op jit(solution)/shard_map/dot_general | solution.py:175
  96.2 1.2 slice.90
  97.5 2.4 %collective-permute-start.7 = (bf16[416,1024]{1,0:T(8,128)(2,1)S(1)}, bf16[416,1024]{1,0:T(8,128)(2,1)S(1)}, u32[]{:S(2)}, u32[]{:S(2)}) collective-permute-start(bf16[416,1024]{1,0:T(8,128)(2,1)S(1)} %slice.90), channel_id=1, source_target_pairs={{0,192},{64,0},{128,64},{192,128},{1,193},{65,1},{129,65},{193,129... | collective-permute-start | bytes 2555912 | tf_op jit(solution)/shard_map/ppermute | solution.py:153
  100.0 3.1 %collective-permute-start.3 = (bf16[2,192,1024]{2,1,0:T(8,128)(2,1)S(1)}, bf16[2,192,1024]{2,1,0:T(8,128)(2,1)S(1)}, u32[]{:S(2)}, u32[]{:S(2)}) collective-permute-start(bf16[2,192,1024]{2,1,0:T(8,128)(2,1)S(1)} %pad_maximum_fusion), channel_id=1, source_target_pairs={{0,1},{1,0},{2,3},{3,2},{4,5},{5,4},{6,7},{7,6},{8,9},{9,8},{10,11... | collective-permute-start | bytes 2359304 | tf_op jit(solution)/shard_map/ppermute | solution.py:177
  103.1 1.0 fusion.74
  104.2 8.5 %collective-permute-done.6 = bf16[416,1024]{1,0:T(8,128)(2,1)S(1)} collective-permute-done((bf16[416,1024]{1,0:T(8,128)(2,1)S(1)}, bf16[416,1024]{1,0:T(8,128)(2,1)S(1)}, u32[]{:S(2)}, u32[]{:S(2)}) %collective-permute-start.6) | collective-permute-done | bytes 852000 | tf_op jit(solution)/shard_map/ppermute | solution.py:152
  112.7 6.3 %collective-permute-done.7 = bf16[416,1024]{1,0:T(8,128)(2,1)S(1)} collective-permute-done((bf16[416,1024]{1,0:T(8,128)(2,1)S(1)}, bf16[416,1024]{1,0:T(8,128)(2,1)S(1)}, u32[]{:S(2)}, u32[]{:S(2)}) %collective-permute-start.7) | collective-permute-done | bytes 852000 | tf_op jit(solution)/shard_map/ppermute | solution.py:153
  118.9 1.0 fusion.5
  120.1 3.7 %collective-permute-start.8 = (bf16[2,192,1024]{2,1,0:T(8,128)(2,1)S(1)}, bf16[2,192,1024]{2,1,0:T(8,128)(2,1)S(1)}, u32[]{:S(2)}, u32[]{:S(2)}) collective-permute-start(bf16[2,192,1024]{2,1,0:T(8,128)(2,1)S(1)} %pad_maximum_fusion.1), channel_id=1, source_target_pairs={{0,1},{1,0},{2,3},{3,2},{4,5},{5,4},{6,7},{7,6},{8,9},{9,8},{10,11... | collective-permute-start | bytes 2359304 | tf_op jit(solution)/shard_map/ppermute | solution.py:177
  123.9 0.2 maximum_add_fusion
  124.1 2.7 %collective-permute-start.4 = (bf16[2,96,1024]{2,1,0:T(8,128)(2,1)S(1)}, bf16[2,96,1024]{2,1,0:T(8,128)(2,1)S(1)}, u32[]{:S(2)}, u32[]{:S(2)}) collective-permute-start(bf16[2,96,1024]{2,1,0:T(8,128)(2,1)S(1)} %slice.130), channel_id=1, source_target_pairs={{0,2},{2,0},{4,6},{6,4},{8,10},{10,8},{12,14},{14,12},{1,3},{3,1},... | collective-permute-start | bytes 1179656 | tf_op jit(solution)/shard_map/ppermute | solution.py:179
  126.9 0.2 maximum_add_fusion.1
  127.1 1.9 %collective-permute-start.9 = (bf16[2,96,1024]{2,1,0:T(8,128)(2,1)S(1)}, bf16[2,96,1024]{2,1,0:T(8,128)(2,1)S(1)}, u32[]{:S(2)}, u32[]{:S(2)}) collective-permute-start(bf16[2,96,1024]{2,1,0:T(8,128)(2,1)S(1)} %slice.129), channel_id=1, source_target_pairs={{0,14},{2,4},{4,2},{6,8},{8,6},{10,12},{12,10},{14,0},{1,15},{3,5}... | collective-permute-start | bytes 1179656 | tf_op jit(solution)/shard_map/ppermute | solution.py:179
  129.1 7.7 %collective-permute-done.4 = bf16[2,96,1024]{2,1,0:T(8,128)(2,1)S(1)} collective-permute-done((bf16[2,96,1024]{2,1,0:T(8,128)(2,1)S(1)}, bf16[2,96,1024]{2,1,0:T(8,128)(2,1)S(1)}, u32[]{:S(2)}, u32[]{:S(2)}) %collective-permute-start.4) | collective-permute-done | bytes 393248 | tf_op jit(solution)/shard_map/ppermute | solution.py:179
  136.8 0.1 fusion.12
  136.8 2.6 %collective-permute-done.9 = bf16[2,96,1024]{2,1,0:T(8,128)(2,1)S(1)} collective-permute-done((bf16[2,96,1024]{2,1,0:T(8,128)(2,1)S(1)}, bf16[2,96,1024]{2,1,0:T(8,128)(2,1)S(1)}, u32[]{:S(2)}, u32[]{:S(2)}) %collective-permute-start.9) | collective-permute-done | bytes 393248 | tf_op jit(solution)/shard_map/ppermute | solution.py:179
  139.5 0.1 fusion.11
  139.6 1.0 pad_maximum_fusion.2
  140.5 5.4 %all-to-all-start.2 = ((bf16[16,24,1024]{2,1,0:T(8,128)(2,1)}), bf16[16,24,1024]{2,1,0:T(8,128)(2,1)S(1)}, u32[]{:S(2)}, u32[]{:S(2)}) async-start(bf16[16,24,1024]{2,1,0:T(8,128)(2,1)} %bitcast.8), calls=%async_computation.2 | async-start | bytes 1572864 | tf_op jit(solution)/shard_map/all_to_all | solution.py:182
  145.9 18.6 %all-to-all-done.2 = bf16[16,24,1024]{2,1,0:T(8,128)(2,1)S(1)} async-done(((bf16[16,24,1024]{2,1,0:T(8,128)(2,1)}), bf16[16,24,1024]{2,1,0:T(8,128)(2,1)S(1)}, u32[]{:S(2)}, u32[]{:S(2)}) %all-to-all-start.2) | async-done | bytes 786464 | tf_op jit(solution)/shard_map/all_to_all | solution.py:182
  164.6 0.1 reduce_sum.12
  164.7 7.6 %collective-permute-start.11 = (bf16[24,1024]{1,0:T(8,128)(2,1)S(1)}, bf16[24,1024]{1,0:T(8,128)(2,1)S(1)}, u32[]{:S(2)}, u32[]{:S(2)}) collective-permute-start(bf16[24,1024]{1,0:T(8,128)(2,1)S(1)} %reduce_sum.12), channel_id=1, source_target_pairs={{0,0},{1,1},{2,2},{3,3},{4,4},{5,21},{6,22},{7,23},{8,24},{9,25},{... | collective-permute-start | bytes 147464 | tf_op jit(solution)/shard_map/ppermute | solution.py:188
  172.4 2.5 %collective-permute-start.10 = (bf16[8,1024]{1,0:T(8,128)(2,1)S(1)}, bf16[8,1024]{1,0:T(8,128)(2,1)S(1)}, u32[]{:S(2)}, u32[]{:S(2)}) collective-permute-start(bf16[8,1024]{1,0:T(8,128)(2,1)S(1)} %slice_select_fusion.2), channel_id=1, source_target_pairs={{5,5},{10,42},{21,69},{26,106},{37,197},{42,234},{53,133},{58,170}... | collective-permute-start | bytes 49160 | tf_op jit(solution)/shard_map/ppermute | solution.py:189
  174.8 6.2 %collective-permute-done.10 = bf16[8,1024]{1,0:T(8,128)(2,1)S(1)} collective-permute-done((bf16[8,1024]{1,0:T(8,128)(2,1)S(1)}, bf16[8,1024]{1,0:T(8,128)(2,1)S(1)}, u32[]{:S(2)}, u32[]{:S(2)}) %collective-permute-start.10) | collective-permute-done | bytes 16416 | tf_op jit(solution)/shard_map/ppermute | solution.py:189
  181.1 0.6 pad_maximum_fusion.3
  (36 shorter events, 0.9 us)
Async XLA Ops:
  0.0 28.4 %copy-start = (bf16[3,128,896]{2,1,0:T(8,128)(2,1)S(1)}, bf16[3,128,896]{2,1,0:T(8,128)(2,1)}, u32[]{:S(2)}) copy-start(bf16[3,128,896]{2,1,0:T(8,128)(2,1)} %constant.122.clone.spread_ref) | copy-start | bytes 2064388
  0.0 28.4 %copy-start.1 = (bf16[128,128]{1,0:T(8,128)(2,1)S(1)}, bf16[128,128]{1,0:T(8,128)(2,1)}, u32[]{:S(2)}) copy-start(bf16[128,128]{1,0:T(8,128)(2,1)} %constant.121.clone.lanes_ref) | copy-start | bytes 98308
  0.0 28.5 %copy-start.2 = (bf16[128,128]{1,0:T(8,128)(2,1)S(1)}, bf16[128,128]{1,0:T(8,128)(2,1)}, u32[]{:S(2)}) copy-start(bf16[128,128]{1,0:T(8,128)(2,1)} %constant.120.clone.rows_ref) | copy-start | bytes 98308
  0.0 17.7 %copy-start.4 = (s32[1024]{0:T(1024)S(1)}, s32[1024]{0:T(1024)}, u32[]{:S(2)}) copy-start(s32[1024]{0:T(1024)} %param.12) | copy-start | bytes 12292
  3.9 32.8 %copy-start.3 = (bf16[832,1024]{1,0:T(8,128)(2,1)S(1)}, bf16[832,1024]{1,0:T(8,128)(2,1)}, u32[]{:S(2)}) copy-start(bf16[832,1024]{1,0:T(8,128)(2,1)} %param.9) | copy-start | bytes 5111812
  3.9 24.5 %all-to-all-start = ((bf16[64,2,896]{2,1,0:T(2,128)(2,1)}), bf16[64,2,896]{2,1,0:T(2,128)(2,1)S(1)}, u32[]{:S(2)}, u32[]{:S(2)}) async-start(bf16[64,2,896]{2,1,0:T(2,128)(2,1)} %reshape.17), calls=%async_computation | async-start | bytes 458752 | tf_op jit(solution)/shard_map/all_to_all | solution.py:162
  30.0 17.3 %all-to-all-start.1 = ((bf16[64,2,832]{2,1,0:T(2,128)(2,1)}), bf16[64,2,832]{2,1,0:T(2,128)(2,1)}, u32[]{:S(2)}, u32[]{:S(2)}) async-start(bf16[64,2,832]{2,1,0:T(2,128)(2,1)} %reshape.19), calls=%async_computation.1 | async-start | bytes 458752 | tf_op jit(solution)/shard_map/all_to_all | solution.py:164
  39.3 51.5 %collective-permute-start.5 = (bf16[832,1024]{1,0:T(8,128)(2,1)S(1)}, bf16[832,1024]{1,0:T(8,128)(2,1)S(1)}, u32[]{:S(2)}, u32[]{:S(2)}) collective-permute-start(bf16[832,1024]{1,0:T(8,128)(2,1)S(1)} %multiply_convert_fusion), channel_id=1, source_target_pairs={{0,64},{64,128},{128,192},{192,0},{1,65},{65,129},{129,193},{193,1... | collective-permute-start | bytes 5111816 | tf_op jit(solution)/shard_map/ppermute | solution.py:149
  42.2 51.6 %collective-permute-start.2 = (bf16[832,1024]{1,0:T(8,128)(2,1)S(1)}, bf16[832,1024]{1,0:T(8,128)(2,1)}, u32[]{:S(2)}, u32[]{:S(2)}) collective-permute-start(bf16[832,1024]{1,0:T(8,128)(2,1)S(1)} %multiply_convert_fusion), channel_id=1, source_target_pairs={{0,192},{64,0},{128,64},{192,128},{1,193},{65,1},{129,65},{193,129... | collective-permute-start | bytes 5111816 | tf_op jit(solution)/shard_map/ppermute | solution.py:148
  49.1 21.8 %collective-permute-start.1 = (bf16[128,832]{1,0:T(8,128)(2,1)}, bf16[128,832]{1,0:T(8,128)(2,1)S(1)}, u32[]{:S(2)}, u32[]{:S(2)}) collective-permute-start(bf16[128,832]{1,0:T(8,128)(2,1)} %reshape.20), channel_id=1, source_target_pairs={{0,256},{256,512},{512,0},{1,257},{257,513},{513,1},{2,258},{258,5... | collective-permute-start | bytes 638984 | tf_op jit(solution)/shard_map/ppermute | solution.py:167
  59.4 28.2 %collective-permute-start = (bf16[128,832]{1,0:T(8,128)(2,1)}, bf16[128,832]{1,0:T(8,128)(2,1)S(1)}, u32[]{:S(2)}, u32[]{:S(2)}) collective-permute-start(bf16[128,832]{1,0:T(8,128)(2,1)} %reshape.20), channel_id=1, source_target_pairs={{0,512},{256,0},{512,256},{1,513},{257,1},{513,257},{2,514},{258,2... | collective-permute-start | bytes 638984 | tf_op jit(solution)/shard_map/ppermute | solution.py:166
  90.9 21.8 %collective-permute-start.6 = (bf16[416,1024]{1,0:T(8,128)(2,1)S(1)}, bf16[416,1024]{1,0:T(8,128)(2,1)S(1)}, u32[]{:S(2)}, u32[]{:S(2)}) collective-permute-start(bf16[416,1024]{1,0:T(8,128)(2,1)S(1)} %slice.89), channel_id=1, source_target_pairs={{0,64},{64,128},{128,192},{192,0},{1,65},{65,129},{129,193},{193,1... | collective-permute-start | bytes 2555912 | tf_op jit(solution)/shard_map/ppermute | solution.py:152
  97.5 21.5 %collective-permute-start.7 = (bf16[416,1024]{1,0:T(8,128)(2,1)S(1)}, bf16[416,1024]{1,0:T(8,128)(2,1)S(1)}, u32[]{:S(2)}, u32[]{:S(2)}) collective-permute-start(bf16[416,1024]{1,0:T(8,128)(2,1)S(1)} %slice.90), channel_id=1, source_target_pairs={{0,192},{64,0},{128,64},{192,128},{1,193},{65,1},{129,65},{193,129... | collective-permute-start | bytes 2555912 | tf_op jit(solution)/shard_map/ppermute | solution.py:153
  100.0 23.8 %collective-permute-start.3 = (bf16[2,192,1024]{2,1,0:T(8,128)(2,1)S(1)}, bf16[2,192,1024]{2,1,0:T(8,128)(2,1)S(1)}, u32[]{:S(2)}, u32[]{:S(2)}) collective-permute-start(bf16[2,192,1024]{2,1,0:T(8,128)(2,1)S(1)} %pad_maximum_fusion), channel_id=1, source_target_pairs={{0,1},{1,0},{2,3},{3,2},{4,5},{5,4},{6,7},{7,6},{8,9},{9,8},{10,11... | collective-permute-start | bytes 2359304 | tf_op jit(solution)/shard_map/ppermute | solution.py:177
  120.1 6.8 %collective-permute-start.8 = (bf16[2,192,1024]{2,1,0:T(8,128)(2,1)S(1)}, bf16[2,192,1024]{2,1,0:T(8,128)(2,1)S(1)}, u32[]{:S(2)}, u32[]{:S(2)}) collective-permute-start(bf16[2,192,1024]{2,1,0:T(8,128)(2,1)S(1)} %pad_maximum_fusion.1), channel_id=1, source_target_pairs={{0,1},{1,0},{2,3},{3,2},{4,5},{5,4},{6,7},{7,6},{8,9},{9,8},{10,11... | collective-permute-start | bytes 2359304 | tf_op jit(solution)/shard_map/ppermute | solution.py:177
  124.1 12.6 %collective-permute-start.4 = (bf16[2,96,1024]{2,1,0:T(8,128)(2,1)S(1)}, bf16[2,96,1024]{2,1,0:T(8,128)(2,1)S(1)}, u32[]{:S(2)}, u32[]{:S(2)}) collective-permute-start(bf16[2,96,1024]{2,1,0:T(8,128)(2,1)S(1)} %slice.130), channel_id=1, source_target_pairs={{0,2},{2,0},{4,6},{6,4},{8,10},{10,8},{12,14},{14,12},{1,3},{3,1},... | collective-permute-start | bytes 1179656 | tf_op jit(solution)/shard_map/ppermute | solution.py:179
  127.1 12.3 %collective-permute-start.9 = (bf16[2,96,1024]{2,1,0:T(8,128)(2,1)S(1)}, bf16[2,96,1024]{2,1,0:T(8,128)(2,1)S(1)}, u32[]{:S(2)}, u32[]{:S(2)}) collective-permute-start(bf16[2,96,1024]{2,1,0:T(8,128)(2,1)S(1)} %slice.129), channel_id=1, source_target_pairs={{0,14},{2,4},{4,2},{6,8},{8,6},{10,12},{12,10},{14,0},{1,15},{3,5}... | collective-permute-start | bytes 1179656 | tf_op jit(solution)/shard_map/ppermute | solution.py:179
  140.5 24.0 %all-to-all-start.2 = ((bf16[16,24,1024]{2,1,0:T(8,128)(2,1)}), bf16[16,24,1024]{2,1,0:T(8,128)(2,1)S(1)}, u32[]{:S(2)}, u32[]{:S(2)}) async-start(bf16[16,24,1024]{2,1,0:T(8,128)(2,1)} %bitcast.8), calls=%async_computation.2 | async-start | bytes 1572864 | tf_op jit(solution)/shard_map/all_to_all | solution.py:182
  164.7 16.3 %collective-permute-start.11 = (bf16[24,1024]{1,0:T(8,128)(2,1)S(1)}, bf16[24,1024]{1,0:T(8,128)(2,1)S(1)}, u32[]{:S(2)}, u32[]{:S(2)}) collective-permute-start(bf16[24,1024]{1,0:T(8,128)(2,1)S(1)} %reduce_sum.12), channel_id=1, source_target_pairs={{0,0},{1,1},{2,2},{3,3},{4,4},{5,21},{6,22},{7,23},{8,24},{9,25},{... | collective-permute-start | bytes 147464 | tf_op jit(solution)/shard_map/ppermute | solution.py:188
  172.4 8.7 %collective-permute-start.10 = (bf16[8,1024]{1,0:T(8,128)(2,1)S(1)}, bf16[8,1024]{1,0:T(8,128)(2,1)S(1)}, u32[]{:S(2)}, u32[]{:S(2)}) collective-permute-start(bf16[8,1024]{1,0:T(8,128)(2,1)S(1)} %slice_select_fusion.2), channel_id=1, source_target_pairs={{5,5},{10,42},{21,69},{26,106},{37,197},{42,234},{53,133},{58,170}... | collective-permute-start | bytes 49160 | tf_op jit(solution)/shard_map/ppermute | solution.py:189

commit v2 on v1

--- a/solution.py
+++ b/solution.py
@@ -13,6 +13,7 @@
 TENSOR = ("l", "yh", "yl", "c")
 SLOTS = (0, 1, 3, 2)
 WIDTH = 896
+SPLIT = 416
 
 
 def sine_coefficients():
@@ -144,24 +145,28 @@
     h, x, y_low, c = (lax.axis_index(name) for name in ("h", "x", "yl", "c"))
     y_high = lax.axis_index("yh")
 
-    weight_0 = quantize_weight(down_weight, weight_exponent)
-    weight_1 = lax.ppermute(weight_0, "x", ring(4, -1))
-    weight_3 = lax.ppermute(weight_0, "x", ring(4, 1))
-    weight_2 = jnp.concatenate(
-        [
-            lax.ppermute(weight_3[:416], "x", ring(4, 1)),
-            lax.ppermute(weight_1[416:], "x", ring(4, -1)),
-        ],
-        axis=0,
-    )
+    top_0 = quantize_weight(down_weight[:SPLIT], weight_exponent)
+    top_1 = lax.ppermute(top_0, "x", ring(4, -1))
+    top_3 = lax.ppermute(top_0, "x", ring(4, 1))
+    low_0 = quantize_weight(down_weight[SPLIT:], weight_exponent)
 
     scaling = jnp.exp2(act_exponent.astype(jnp.float32)).astype(jnp.bfloat16)
     inverse = (1.0 / scaling.astype(jnp.float32)).astype(jnp.bfloat16)
     level = jnp.broadcast_to((7.5 - clip_index.astype(jnp.float32)).astype(jnp.bfloat16)[None, :], (128, 13))
     packed = jnp.concatenate([hidden, scaling, inverse, level, jnp.zeros((128, 25), jnp.bfloat16)], axis=1)
     arrived = lax.all_to_all(packed.reshape(64, 2, WIDTH), TENSOR, split_axis=0, concat_axis=0, tiled=True)
+    arrived, top_1, top_3, low_0 = lax.optimization_barrier((arrived, top_1, top_3, low_0))
+    low_1 = lax.ppermute(low_0, "x", ring(4, -1))
+    low_3 = lax.ppermute(low_0, "x", ring(4, 1))
     quantized = rotate_and_quantize(arrived.reshape(128, WIDTH))
     returned = lax.all_to_all(quantized.reshape(64, 2, 832), TENSOR, split_axis=0, concat_axis=0, tiled=True)
+    returned, low_1, low_3 = lax.optimization_barrier((returned, low_1, low_3))
+    top_2 = lax.ppermute(top_3, "x", ring(4, 1))
+    low_2 = lax.ppermute(low_1, "x", ring(4, -1))
+    weight_0, weight_1, weight_2, weight_3 = (
+        jnp.concatenate(pair, axis=0)
+        for pair in ((top_0, low_0), (top_1, low_1), (top_2, low_2), (top_3, low_3))
+    )
     own = returned.reshape(128, 832)
     next_1 = lax.ppermute(own, "h", ring(3, -1))
     next_2 = lax.ppermute(own, "h", ring(3, 1))

time: 183 us -> 172 us (0.940)
  blocking collectives: 0 us -> 24.7 us
  waiting for transfers between devices: 88 us -> 64.3 us
  starting transfers between devices: 71.4 us -> 63.3 us
  local copies, waits for them, and re-layouts: 6.88 us -> 2.48 us
    all_to_all x0 -> x1, blocking collectives: none -> 24.7 us  [shards(): lax.all_to_all(packed.reshape(64, 2, WIDTH), TENSOR, split_axis=0, concat...]
    ppermute x4 -> x6, waiting for transfers between devices: 14.7 us -> 0.02 us  [the longest x1 0.01 us: shards(): top_3 = lax.ppermute(top_0, 'x', ring(4, 1))]
    all_to_all x1 -> x0, starting transfers between devices: 13.9 us -> none  [shards(): lax.all_to_all(packed.reshape(64, 2, WIDTH), TENSOR, split_axis=0, concat...]
    all_to_all x1 -> x0, waiting for transfers between devices: 10.6 us -> none  [shards(): lax.all_to_all(packed.reshape(64, 2, WIDTH), TENSOR, split_axis=0, concat...]
    all_to_all x1, waiting for transfers between devices: 2.6 us -> 10.6 us  [shards(): lax.all_to_all(quantized.reshape(64, 2, 832), TENSOR, split_axis=0, conca...]
    ppermute x1, waiting for transfers between devices: 8.26 us -> 2.76 us  [shards(): next_2 = lax.ppermute(own, 'h', ring(3, 1))]
    ppermute x4 -> x6, starting transfers between devices: 10.6 us -> 16 us  [the longest x1 3.32 us: shards(): top_2 = lax.ppermute(top_3, 'x', ring(4, 1))]
    ppermute x2, starting transfers between devices: 6.75 us -> 4.43 us  [shards(): from_core = lax.ppermute(other, 'c', [(0, 1), (1, 0)])]
  transfers between devices with their start and end apart: 15 -> 16, of which waited for: 10 -> 7; matrix products, arithmetic and copies ran while one was open for 8% -> 6% of each run, Pallas kernels for 0% -> 0%
where the time goes in v2:
time: 172 us; the launch traced here: 171 us
  waiting for transfers between devices  64.3 us (37%)
  starting transfers between devices  63.3 us (37%)
  blocking collectives  24.7 us (14%)
  matrix products  8 us (5%)
  other arithmetic  7.07 us (4%)
  local copies, waits for them, and re-layouts  2.48 us (1%)
    all_to_all x1, blocking collectives, shards(): lax.all_to_all(packed.reshape(64, 2, WIDTH), TENSOR, split_axis=0, concat...  24.7 us
    all_to_all x1, waiting for transfers between devices, shards(): lax.all_to_all(sums, ('l', 'yh'), split_axis=0, concat_axis=0, tiled=True)  18.2 us
    ppermute x1, waiting for transfers between devices, shards(): next_1 = lax.ppermute(own, 'h', ring(3, -1))  16.7 us
    all_to_all x1, waiting for transfers between devices, shards(): lax.all_to_all(quantized.reshape(64, 2, 832), TENSOR, split_axis=0, conca...  10.6 us
    ppermute x1, starting transfers between devices, shards(): next_2 = lax.ppermute(own, 'h', ring(3, 1))  10.3 us
    ppermute x2, waiting for transfers between devices, shards(): lax.ppermute(mine[:, :96].astype(jnp.bfloat16), ('yh', 'yl'), y_pairs)  9.75 us
    all_to_all x1, starting transfers between devices, shards(): lax.all_to_all(quantized.reshape(64, 2, 832), TENSOR, split_axis=0, conca...  8.91 us
    ppermute x1, starting transfers between devices, shards(): lax.ppermute(total, ('x', 'l', 'yh', 'yl', 'c'), final_pairs('main'))  7.9 us
  transfers between devices with their start and end apart: 16, of which 7 were waited for; matrix products, arithmetic and copies ran while one was open for 6% of the time, Pallas kernels for 0%

profile of v2, /device:TPU:21, one launch (start us, length us, event | category | flops | bytes accessed | tf_op | source)
XLA Modules:
  0.0 171.0 jit_solution(6558550632707834419)
XLA Ops:
  0.0 0.7 fusion.74
  0.7 3.9 %multiply_convert_fusion = (bf16[416,1024]{1,0:T(8,128)(2,1)S(1)}, bf16[416,1024]{1,0:T(8,128)(2,1)S(1)}) fusion(bf16[832,1024]{1,0:T(8,128)(2,1)} %param.9, f32[1024]{0:T(1024)S(1)} %fusion.74), kind=kLoop, calls=%fused_computation.18 | loop fusion | flops 20447232 | bytes 3411968 | tf_op jit(solution)/shard_map/convert_element_type | solution.py:102
  4.6 3.0 %collective-permute-start.1 = (bf16[416,1024]{1,0:T(8,128)(2,1)S(1)}, bf16[416,1024]{1,0:T(8,128)(2,1)}, u32[]{:S(2)}, u32[]{:S(2)}) collective-permute-start(bf16[416,1024]{1,0:T(8,128)(2,1)S(1)} %get-tuple-element.22), channel_id=1, source_target_pairs={{0,64},{64,128},{128,192},{192,0},{1,65},{65,129},{129,193},{193,1... | collective-permute-start | bytes 2555912 | tf_op jit(solution)/shard_map/ppermute | solution.py:150
  7.6 2.5 %collective-permute-start = (bf16[416,1024]{1,0:T(8,128)(2,1)S(1)}, bf16[416,1024]{1,0:T(8,128)(2,1)}, u32[]{:S(2)}, u32[]{:S(2)}) collective-permute-start(bf16[416,1024]{1,0:T(8,128)(2,1)S(1)} %get-tuple-element.22), channel_id=1, source_target_pairs={{0,192},{64,0},{128,64},{192,128},{1,193},{65,1},{129,65},{193,129... | collective-permute-start | bytes 2555912 | tf_op jit(solution)/shard_map/ppermute | solution.py:149
  10.1 0.1 broadcast_in_dim.29
  10.2 0.5 concatenate.24
  10.7 0.2 copy.10
  10.9 0.1 reshape.17
  11.0 24.7 %all_to_all.15 = bf16[64,2,896]{2,1,0:T(2,128)(2,1)S(1)} all-to-all(bf16[64,2,896]{2,1,0:T(2,128)(2,1)S(1)} %reshape.17), channel_id=1, replica_groups=mesh['h'=3,'x'=4,'l'=4,'yh'=4,'yl'=2,'c'=2] {'l','yh','yl','c'}, dimensions={0} | all-to-all | bytes 458752 | tf_op jit(solution)/shard_map/all_to_all | solution.py:157
  35.7 2.8 %collective-permute-start.3 = (bf16[416,1024]{1,0:T(8,128)(2,1)S(1)}, bf16[416,1024]{1,0:T(8,128)(2,1)}, u32[]{:S(2)}, u32[]{:S(2)}) collective-permute-start(bf16[416,1024]{1,0:T(8,128)(2,1)S(1)} %get-tuple-element.13), channel_id=1, source_target_pairs={{0,64},{64,128},{128,192},{192,0},{1,65},{65,129},{129,193},{193,1... | collective-permute-start | bytes 2555912 | tf_op jit(solution)/shard_map/ppermute | solution.py:160
  38.5 2.5 %collective-permute-start.2 = (bf16[416,1024]{1,0:T(8,128)(2,1)S(1)}, bf16[416,1024]{1,0:T(8,128)(2,1)}, u32[]{:S(2)}, u32[]{:S(2)}) collective-permute-start(bf16[416,1024]{1,0:T(8,128)(2,1)S(1)} %get-tuple-element.13), channel_id=1, source_target_pairs={{0,192},{64,0},{128,64},{192,128},{1,193},{65,1},{129,65},{193,129... | collective-permute-start | bytes 2555912 | tf_op jit(solution)/shard_map/ppermute | solution.py:159
  41.0 0.1 reshape.18.x_ref
  41.1 0.7 shard_map.82
  41.8 0.8 reshape.19
  42.6 8.9 %all-to-all-start.1 = ((bf16[64,2,832]{2,1,0:T(2,128)(2,1)}), bf16[64,2,832]{2,1,0:T(2,128)(2,1)S(1)}, u32[]{:S(2)}, u32[]{:S(2)}) async-start(bf16[64,2,832]{2,1,0:T(2,128)(2,1)} %reshape.19), calls=%async_computation.1 | async-start | bytes 458752 | tf_op jit(solution)/shard_map/all_to_all | solution.py:162
  51.5 10.6 %all-to-all-done.1 = bf16[64,2,832]{2,1,0:T(2,128)(2,1)S(1)} async-done(((bf16[64,2,832]{2,1,0:T(2,128)(2,1)}), bf16[64,2,832]{2,1,0:T(2,128)(2,1)S(1)}, u32[]{:S(2)}, u32[]{:S(2)}) %all-to-all-start.1) | async-done | bytes 213024 | tf_op jit(solution)/shard_map/all_to_all | solution.py:162
  62.1 0.2 reshape.20
  62.3 10.3 %collective-permute-start.5 = (bf16[128,832]{1,0:T(8,128)(2,1)S(1)}, bf16[128,832]{1,0:T(8,128)(2,1)S(1)}, u32[]{:S(2)}, u32[]{:S(2)}) collective-permute-start(bf16[128,832]{1,0:T(8,128)(2,1)S(1)} %reshape.20), channel_id=1, source_target_pairs={{0,256},{256,512},{512,0},{1,257},{257,513},{513,1},{2,258},{258,5... | collective-permute-start | bytes 638984 | tf_op jit(solution)/shard_map/ppermute | solution.py:172
  72.6 3.2 %collective-permute-start.4 = (bf16[128,832]{1,0:T(8,128)(2,1)S(1)}, bf16[128,832]{1,0:T(8,128)(2,1)S(1)}, u32[]{:S(2)}, u32[]{:S(2)}) collective-permute-start(bf16[128,832]{1,0:T(8,128)(2,1)S(1)} %reshape.20), channel_id=1, source_target_pairs={{0,512},{256,0},{512,256},{1,513},{257,1},{513,257},{2,514},{258,2... | collective-permute-start | bytes 638984 | tf_op jit(solution)/shard_map/ppermute | solution.py:171
  75.8 3.3 %collective-permute-start.8 = (bf16[416,1024]{1,0:T(8,128)(2,1)}, bf16[416,1024]{1,0:T(8,128)(2,1)S(1)}, u32[]{:S(2)}, u32[]{:S(2)}) collective-permute-start(bf16[416,1024]{1,0:T(8,128)(2,1)} %collective-permute-done.1), channel_id=1, source_target_pairs={{0,64},{64,128},{128,192},{192,0},{1,65},{65,129},{129,193},{193,1... | collective-permute-start | bytes 2555912 | tf_op jit(solution)/shard_map/ppermute | solution.py:164
  79.1 2.0 %collective-permute-start.9 = (bf16[416,1024]{1,0:T(8,128)(2,1)}, bf16[416,1024]{1,0:T(8,128)(2,1)S(1)}, u32[]{:S(2)}, u32[]{:S(2)}) collective-permute-start(bf16[416,1024]{1,0:T(8,128)(2,1)} %collective-permute-done.2), channel_id=1, source_target_pairs={{0,192},{64,0},{128,64},{192,128},{1,193},{65,1},{129,65},{193,129... | collective-permute-start | bytes 2555912 | tf_op jit(solution)/shard_map/ppermute | solution.py:165
  81.1 2.8 %collective-permute-done.5 = bf16[128,832]{1,0:T(8,128)(2,1)S(1)} collective-permute-done((bf16[128,832]{1,0:T(8,128)(2,1)S(1)}, bf16[128,832]{1,0:T(8,128)(2,1)S(1)}, u32[]{:S(2)}, u32[]{:S(2)}) %collective-permute-start.5) | collective-permute-done | bytes 213024 | tf_op jit(solution)/shard_map/ppermute | solution.py:172
  83.9 16.7 %collective-permute-done.4 = bf16[128,832]{1,0:T(8,128)(2,1)S(1)} collective-permute-done((bf16[128,832]{1,0:T(8,128)(2,1)S(1)}, bf16[128,832]{1,0:T(8,128)(2,1)S(1)}, u32[]{:S(2)}, u32[]{:S(2)}) %collective-permute-start.4) | collective-permute-done | bytes 213024 | tf_op jit(solution)/shard_map/ppermute | solution.py:171
  100.6 1.1 convolution_convert_fusion
  101.8 1.0 fusion
  102.8 2.4 %fusion.8 = f32[384,1024]{1,0:T(8,128)S(1)} fusion(bf16[384,832]{0,1:T(8,128)(2,1)S(1)} %convolution_convert_fusion, bf16[416,1024]{1,0:T(8,128)(2,1)} %collective-permute-done.3, bf16[416,1024]{1,0:T(8,128)(2,1)} %collective-permute-done.1), kind=kOutput, calls=%fused_computation.10 | convolution fusion | flops 657719296 | bytes 3915776 | tf_op jit(solution)/shard_map/dot_general | solution.py:180
  105.3 2.4 %fusion.4 = f32[384,1024]{1,0:T(8,128)S(1)} fusion(bf16[384,832]{0,1:T(8,128)(2,1)S(1)} %convolution_convert_fusion, bf16[416,1024]{1,0:T(8,128)(2,1)} %collective-permute-done.2, bf16[416,1024]{1,0:T(8,128)(2,1)} %collective-permute-done), kind=kOutput, calls=%fused_computation.6 | convolution fusion | flops 657719296 | bytes 3915776 | tf_op jit(solution)/shard_map/dot_general | solution.py:180
  107.7 0.1 pad_maximum_fusion
  107.8 2.5 %collective-permute-start.6 = (bf16[2,192,1024]{2,1,0:T(8,128)(2,1)S(1)}, bf16[2,192,1024]{2,1,0:T(8,128)(2,1)S(1)}, u32[]{:S(2)}, u32[]{:S(2)}) collective-permute-start(bf16[2,192,1024]{2,1,0:T(8,128)(2,1)S(1)} %pad_maximum_fusion), channel_id=1, source_target_pairs={{0,1},{1,0},{2,3},{3,2},{4,5},{5,4},{6,7},{7,6},{8,9},{9,8},{10,11... | collective-permute-start | bytes 2359304 | tf_op jit(solution)/shard_map/ppermute | solution.py:182
  110.6 1.0 fusion.12
  111.6 0.1 pad_maximum_fusion.1
  111.7 1.9 %collective-permute-start.10 = (bf16[2,192,1024]{2,1,0:T(8,128)(2,1)S(1)}, bf16[2,192,1024]{2,1,0:T(8,128)(2,1)S(1)}, u32[]{:S(2)}, u32[]{:S(2)}) collective-permute-start(bf16[2,192,1024]{2,1,0:T(8,128)(2,1)S(1)} %pad_maximum_fusion.1), channel_id=1, source_target_pairs={{0,1},{1,0},{2,3},{3,2},{4,5},{5,4},{6,7},{7,6},{8,9},{9,8},{10,11... | collective-permute-start | bytes 2359304 | tf_op jit(solution)/shard_map/ppermute | solution.py:182
  113.8 0.2 maximum_add_fusion
  114.1 2.6 %collective-permute-start.7 = (bf16[2,96,1024]{2,1,0:T(8,128)(2,1)S(1)}, bf16[2,96,1024]{2,1,0:T(8,128)(2,1)S(1)}, u32[]{:S(2)}, u32[]{:S(2)}) collective-permute-start(bf16[2,96,1024]{2,1,0:T(8,128)(2,1)S(1)} %slice.130), channel_id=1, source_target_pairs={{0,2},{2,0},{4,6},{6,4},{8,10},{10,8},{12,14},{14,12},{1,3},{3,1},... | collective-permute-start | bytes 1179656 | tf_op jit(solution)/shard_map/ppermute | solution.py:184
  116.7 0.2 maximum_add_fusion.1
  116.9 1.9 %collective-permute-start.11 = (bf16[2,96,1024]{2,1,0:T(8,128)(2,1)S(1)}, bf16[2,96,1024]{2,1,0:T(8,128)(2,1)S(1)}, u32[]{:S(2)}, u32[]{:S(2)}) collective-permute-start(bf16[2,96,1024]{2,1,0:T(8,128)(2,1)S(1)} %slice.129), channel_id=1, source_target_pairs={{0,14},{2,4},{4,2},{6,8},{8,6},{10,12},{12,10},{14,0},{1,15},{3,5}... | collective-permute-start | bytes 1179656 | tf_op jit(solution)/shard_map/ppermute | solution.py:184
  118.9 7.3 %collective-permute-done.7 = bf16[2,96,1024]{2,1,0:T(8,128)(2,1)S(1)} collective-permute-done((bf16[2,96,1024]{2,1,0:T(8,128)(2,1)S(1)}, bf16[2,96,1024]{2,1,0:T(8,128)(2,1)S(1)}, u32[]{:S(2)}, u32[]{:S(2)}) %collective-permute-start.7) | collective-permute-done | bytes 393248 | tf_op jit(solution)/shard_map/ppermute | solution.py:184
  126.2 0.1 fusion.29
  126.3 2.4 %collective-permute-done.11 = bf16[2,96,1024]{2,1,0:T(8,128)(2,1)S(1)} collective-permute-done((bf16[2,96,1024]{2,1,0:T(8,128)(2,1)S(1)}, bf16[2,96,1024]{2,1,0:T(8,128)(2,1)S(1)}, u32[]{:S(2)}, u32[]{:S(2)}) %collective-permute-start.11) | collective-permute-done | bytes 393248 | tf_op jit(solution)/shard_map/ppermute | solution.py:184
  128.7 0.1 fusion.28
  128.8 0.9 pad_maximum_fusion.2
  129.8 5.7 %all-to-all-start.2 = ((bf16[16,24,1024]{2,1,0:T(8,128)(2,1)}), bf16[16,24,1024]{2,1,0:T(8,128)(2,1)S(1)}, u32[]{:S(2)}, u32[]{:S(2)}) async-start(bf16[16,24,1024]{2,1,0:T(8,128)(2,1)} %bitcast.8), calls=%async_computation.2 | async-start | bytes 1572864 | tf_op jit(solution)/shard_map/all_to_all | solution.py:187
  135.4 18.2 %all-to-all-done.2 = bf16[16,24,1024]{2,1,0:T(8,128)(2,1)S(1)} async-done(((bf16[16,24,1024]{2,1,0:T(8,128)(2,1)}), bf16[16,24,1024]{2,1,0:T(8,128)(2,1)S(1)}, u32[]{:S(2)}, u32[]{:S(2)}) %all-to-all-start.2) | async-done | bytes 786464 | tf_op jit(solution)/shard_map/all_to_all | solution.py:187
  153.7 0.1 reduce_sum.12
  153.8 7.9 %collective-permute-start.13 = (bf16[24,1024]{1,0:T(8,128)(2,1)S(1)}, bf16[24,1024]{1,0:T(8,128)(2,1)S(1)}, u32[]{:S(2)}, u32[]{:S(2)}) collective-permute-start(bf16[24,1024]{1,0:T(8,128)(2,1)S(1)} %reduce_sum.12), channel_id=1, source_target_pairs={{0,0},{1,1},{2,2},{3,3},{4,4},{5,21},{6,22},{7,23},{8,24},{9,25},{... | collective-permute-start | bytes 147464 | tf_op jit(solution)/shard_map/ppermute | solution.py:193
  161.7 2.5 %collective-permute-start.12 = (bf16[8,1024]{1,0:T(8,128)(2,1)S(1)}, bf16[8,1024]{1,0:T(8,128)(2,1)S(1)}, u32[]{:S(2)}, u32[]{:S(2)}) collective-permute-start(bf16[8,1024]{1,0:T(8,128)(2,1)S(1)} %slice_select_fusion.2), channel_id=1, source_target_pairs={{5,5},{10,42},{21,69},{26,106},{37,197},{42,234},{53,133},{58,170}... | collective-permute-start | bytes 49160 | tf_op jit(solution)/shard_map/ppermute | solution.py:194
  164.2 6.2 %collective-permute-done.12 = bf16[8,1024]{1,0:T(8,128)(2,1)S(1)} collective-permute-done((bf16[8,1024]{1,0:T(8,128)(2,1)S(1)}, bf16[8,1024]{1,0:T(8,128)(2,1)S(1)}, u32[]{:S(2)}, u32[]{:S(2)}) %collective-permute-start.12) | collective-permute-done | bytes 16416 | tf_op jit(solution)/shard_map/ppermute | solution.py:194
  170.4 0.6 pad_maximum_fusion.3
  (39 shorter events, 0.7 us)
Async XLA Ops:
  0.7 9.4 %copy-start.4 = (s32[128,13]{0,1:T(8,128)S(1)}, s32[128,13]{0,1:T(8,128)}, u32[]{:S(2)}) copy-start(s32[128,13]{0,1:T(8,128)} %param.10) | copy-start | bytes 19972
  0.7 9.4 %copy-start.5 = (s32[13]{0:T(128)S(1)}, s32[13]{0:T(128)}, u32[]{:S(2)}) copy-start(s32[13]{0:T(128)} %param.11) | copy-start | bytes 160
  0.7 9.5 %copy-start.3 = (bf16[128,832]{0,1:T(8,128)(2,1)S(1)}, bf16[128,832]{0,1:T(8,128)(2,1)}, u32[]{:S(2)}) copy-start(bf16[128,832]{0,1:T(8,128)(2,1)} %param.8) | copy-start | bytes 638980
  4.6 36.5 %copy-start = (bf16[3,128,896]{2,1,0:T(8,128)(2,1)S(1)}, bf16[3,128,896]{2,1,0:T(8,128)(2,1)}, u32[]{:S(2)}) copy-start(bf16[3,128,896]{2,1,0:T(8,128)(2,1)} %constant.122.clone.spread_ref) | copy-start | bytes 2064388
  4.6 36.5 %copy-start.1 = (bf16[128,128]{1,0:T(8,128)(2,1)S(1)}, bf16[128,128]{1,0:T(8,128)(2,1)}, u32[]{:S(2)}) copy-start(bf16[128,128]{1,0:T(8,128)(2,1)} %constant.121.clone.lanes_ref) | copy-start | bytes 98308
  4.6 36.5 %copy-start.2 = (bf16[128,128]{1,0:T(8,128)(2,1)S(1)}, bf16[128,128]{1,0:T(8,128)(2,1)}, u32[]{:S(2)}) copy-start(bf16[128,128]{1,0:T(8,128)(2,1)} %constant.120.clone.rows_ref) | copy-start | bytes 98308
  4.6 31.0 %collective-permute-start.1 = (bf16[416,1024]{1,0:T(8,128)(2,1)S(1)}, bf16[416,1024]{1,0:T(8,128)(2,1)}, u32[]{:S(2)}, u32[]{:S(2)}) collective-permute-start(bf16[416,1024]{1,0:T(8,128)(2,1)S(1)} %get-tuple-element.22), channel_id=1, source_target_pairs={{0,64},{64,128},{128,192},{192,0},{1,65},{65,129},{129,193},{193,1... | collective-permute-start | bytes 2555912 | tf_op jit(solution)/shard_map/ppermute | solution.py:150
  7.6 28.1 %collective-permute-start = (bf16[416,1024]{1,0:T(8,128)(2,1)S(1)}, bf16[416,1024]{1,0:T(8,128)(2,1)}, u32[]{:S(2)}, u32[]{:S(2)}) collective-permute-start(bf16[416,1024]{1,0:T(8,128)(2,1)S(1)} %get-tuple-element.22), channel_id=1, source_target_pairs={{0,192},{64,0},{128,64},{192,128},{1,193},{65,1},{129,65},{193,129... | collective-permute-start | bytes 2555912 | tf_op jit(solution)/shard_map/ppermute | solution.py:149
  35.7 26.4 %collective-permute-start.3 = (bf16[416,1024]{1,0:T(8,128)(2,1)S(1)}, bf16[416,1024]{1,0:T(8,128)(2,1)}, u32[]{:S(2)}, u32[]{:S(2)}) collective-permute-start(bf16[416,1024]{1,0:T(8,128)(2,1)S(1)} %get-tuple-element.13), channel_id=1, source_target_pairs={{0,64},{64,128},{128,192},{192,0},{1,65},{65,129},{129,193},{193,1... | collective-permute-start | bytes 2555912 | tf_op jit(solution)/shard_map/ppermute | solution.py:160
  38.5 23.6 %collective-permute-start.2 = (bf16[416,1024]{1,0:T(8,128)(2,1)S(1)}, bf16[416,1024]{1,0:T(8,128)(2,1)}, u32[]{:S(2)}, u32[]{:S(2)}) collective-permute-start(bf16[416,1024]{1,0:T(8,128)(2,1)S(1)} %get-tuple-element.13), channel_id=1, source_target_pairs={{0,192},{64,0},{128,64},{192,128},{1,193},{65,1},{129,65},{193,129... | collective-permute-start | bytes 2555912 | tf_op jit(solution)/shard_map/ppermute | solution.py:159
  42.6 19.5 %all-to-all-start.1 = ((bf16[64,2,832]{2,1,0:T(2,128)(2,1)}), bf16[64,2,832]{2,1,0:T(2,128)(2,1)S(1)}, u32[]{:S(2)}, u32[]{:S(2)}) async-start(bf16[64,2,832]{2,1,0:T(2,128)(2,1)} %reshape.19), calls=%async_computation.1 | async-start | bytes 458752 | tf_op jit(solution)/shard_map/all_to_all | solution.py:162
  62.3 21.6 %collective-permute-start.5 = (bf16[128,832]{1,0:T(8,128)(2,1)S(1)}, bf16[128,832]{1,0:T(8,128)(2,1)S(1)}, u32[]{:S(2)}, u32[]{:S(2)}) collective-permute-start(bf16[128,832]{1,0:T(8,128)(2,1)S(1)} %reshape.20), channel_id=1, source_target_pairs={{0,256},{256,512},{512,0},{1,257},{257,513},{513,1},{2,258},{258,5... | collective-permute-start | bytes 638984 | tf_op jit(solution)/shard_map/ppermute | solution.py:172
  72.6 28.0 %collective-permute-start.4 = (bf16[128,832]{1,0:T(8,128)(2,1)S(1)}, bf16[128,832]{1,0:T(8,128)(2,1)S(1)}, u32[]{:S(2)}, u32[]{:S(2)}) collective-permute-start(bf16[128,832]{1,0:T(8,128)(2,1)S(1)} %reshape.20), channel_id=1, source_target_pairs={{0,512},{256,0},{512,256},{1,513},{257,1},{513,257},{2,514},{258,2... | collective-permute-start | bytes 638984 | tf_op jit(solution)/shard_map/ppermute | solution.py:171
  75.8 34.7 %collective-permute-start.8 = (bf16[416,1024]{1,0:T(8,128)(2,1)}, bf16[416,1024]{1,0:T(8,128)(2,1)S(1)}, u32[]{:S(2)}, u32[]{:S(2)}) collective-permute-start(bf16[416,1024]{1,0:T(8,128)(2,1)} %collective-permute-done.1), channel_id=1, source_target_pairs={{0,64},{64,128},{128,192},{192,0},{1,65},{65,129},{129,193},{193,1... | collective-permute-start | bytes 2555912 | tf_op jit(solution)/shard_map/ppermute | solution.py:164
  79.1 31.4 %collective-permute-start.9 = (bf16[416,1024]{1,0:T(8,128)(2,1)}, bf16[416,1024]{1,0:T(8,128)(2,1)S(1)}, u32[]{:S(2)}, u32[]{:S(2)}) collective-permute-start(bf16[416,1024]{1,0:T(8,128)(2,1)} %collective-permute-done.2), channel_id=1, source_target_pairs={{0,192},{64,0},{128,64},{192,128},{1,193},{65,1},{129,65},{193,129... | collective-permute-start | bytes 2555912 | tf_op jit(solution)/shard_map/ppermute | solution.py:165
  107.8 6.0 %collective-permute-start.6 = (bf16[2,192,1024]{2,1,0:T(8,128)(2,1)S(1)}, bf16[2,192,1024]{2,1,0:T(8,128)(2,1)S(1)}, u32[]{:S(2)}, u32[]{:S(2)}) collective-permute-start(bf16[2,192,1024]{2,1,0:T(8,128)(2,1)S(1)} %pad_maximum_fusion), channel_id=1, source_target_pairs={{0,1},{1,0},{2,3},{3,2},{4,5},{5,4},{6,7},{7,6},{8,9},{9,8},{10,11... | collective-permute-start | bytes 2359304 | tf_op jit(solution)/shard_map/ppermute | solution.py:182
  111.7 4.9 %collective-permute-start.10 = (bf16[2,192,1024]{2,1,0:T(8,128)(2,1)S(1)}, bf16[2,192,1024]{2,1,0:T(8,128)(2,1)S(1)}, u32[]{:S(2)}, u32[]{:S(2)}) collective-permute-start(bf16[2,192,1024]{2,1,0:T(8,128)(2,1)S(1)} %pad_maximum_fusion.1), channel_id=1, source_target_pairs={{0,1},{1,0},{2,3},{3,2},{4,5},{5,4},{6,7},{7,6},{8,9},{9,8},{10,11... | collective-permute-start | bytes 2359304 | tf_op jit(solution)/shard_map/ppermute | solution.py:182
  114.1 12.1 %collective-permute-start.7 = (bf16[2,96,1024]{2,1,0:T(8,128)(2,1)S(1)}, bf16[2,96,1024]{2,1,0:T(8,128)(2,1)S(1)}, u32[]{:S(2)}, u32[]{:S(2)}) collective-permute-start(bf16[2,96,1024]{2,1,0:T(8,128)(2,1)S(1)} %slice.130), channel_id=1, source_target_pairs={{0,2},{2,0},{4,6},{6,4},{8,10},{10,8},{12,14},{14,12},{1,3},{3,1},... | collective-permute-start | bytes 1179656 | tf_op jit(solution)/shard_map/ppermute | solution.py:184
  116.9 11.8 %collective-permute-start.11 = (bf16[2,96,1024]{2,1,0:T(8,128)(2,1)S(1)}, bf16[2,96,1024]{2,1,0:T(8,128)(2,1)S(1)}, u32[]{:S(2)}, u32[]{:S(2)}) collective-permute-start(bf16[2,96,1024]{2,1,0:T(8,128)(2,1)S(1)} %slice.129), channel_id=1, source_target_pairs={{0,14},{2,4},{4,2},{6,8},{8,6},{10,12},{12,10},{14,0},{1,15},{3,5}... | collective-permute-start | bytes 1179656 | tf_op jit(solution)/shard_map/ppermute | solution.py:184
  129.8 23.9 %all-to-all-start.2 = ((bf16[16,24,1024]{2,1,0:T(8,128)(2,1)}), bf16[16,24,1024]{2,1,0:T(8,128)(2,1)S(1)}, u32[]{:S(2)}, u32[]{:S(2)}) async-start(bf16[16,24,1024]{2,1,0:T(8,128)(2,1)} %bitcast.8), calls=%async_computation.2 | async-start | bytes 1572864 | tf_op jit(solution)/shard_map/all_to_all | solution.py:187
  153.8 16.6 %collective-permute-start.13 = (bf16[24,1024]{1,0:T(8,128)(2,1)S(1)}, bf16[24,1024]{1,0:T(8,128)(2,1)S(1)}, u32[]{:S(2)}, u32[]{:S(2)}) collective-permute-start(bf16[24,1024]{1,0:T(8,128)(2,1)S(1)} %reduce_sum.12), channel_id=1, source_target_pairs={{0,0},{1,1},{2,2},{3,3},{4,4},{5,21},{6,22},{7,23},{8,24},{9,25},{... | collective-permute-start | bytes 147464 | tf_op jit(solution)/shard_map/ppermute | solution.py:193
  161.7 8.7 %collective-permute-start.12 = (bf16[8,1024]{1,0:T(8,128)(2,1)S(1)}, bf16[8,1024]{1,0:T(8,128)(2,1)S(1)}, u32[]{:S(2)}, u32[]{:S(2)}) collective-permute-start(bf16[8,1024]{1,0:T(8,128)(2,1)S(1)} %slice_select_fusion.2), channel_id=1, source_target_pairs={{5,5},{10,42},{21,69},{26,106},{37,197},{42,234},{53,133},{58,170}... | collective-permute-start | bytes 49160 | tf_op jit(solution)/shard_map/ppermute | solution.py:194

commit v3 on v1

--- a/solution.py
+++ b/solution.py
@@ -95,6 +95,91 @@
     )
 
 
+def pack_kernel(hidden_ref, exponent_ref, index_ref, place_ref, out_ref):
+    out_ref[:, :768] = hidden_ref[:, :768]
+    scaling = jnp.exp2(exponent_ref[...].astype(jnp.float32)).astype(jnp.bfloat16)
+    inverse = (1.0 / scaling.astype(jnp.float32)).astype(jnp.bfloat16)
+    level = jnp.broadcast_to(7.5 - index_ref[...].astype(jnp.float32), (128, 13)).astype(jnp.bfloat16)
+    tail = jnp.dot(hidden_ref[:, 768:], place_ref[:64], preferred_element_type=jnp.float32)
+    for kind, extra in enumerate((scaling, inverse, level)):
+        tail += jnp.dot(extra, place_ref[64 + 16 * kind : 77 + 16 * kind], preferred_element_type=jnp.float32)
+    out_ref[:, 768:] = tail.astype(jnp.bfloat16)
+
+
+def pack(hidden, act_exponent, clip_index):
+    place = np.zeros((112, 128), np.float32)
+    place[np.arange(64), np.arange(64)] = 1.0
+    for kind in range(3):
+        place[64 + 16 * kind + np.arange(13), 64 + 13 * kind + np.arange(13)] = 1.0
+    return pl.pallas_call(
+        pack_kernel,
+        out_shape=jax.ShapeDtypeStruct((128, WIDTH), jnp.bfloat16),
+        in_specs=[pl.BlockSpec(memory_space=pltpu.VMEM)] * 4,
+        out_specs=pl.BlockSpec(memory_space=pltpu.VMEM),
+        compiler_params=pltpu.CompilerParams(vmem_limit_bytes=16 * 1024 * 1024),
+        cost_estimate=pl.CostEstimate(flops=4_000_000, bytes_accessed=500_000, transcendentals=0),
+    )(hidden, act_exponent, clip_index.reshape(1, 13), jnp.asarray(place, jnp.bfloat16))
+
+
+def accumulate(acts, pieces):
+    total, start = None, 0
+    for piece in pieces:
+        stop = start + piece.shape[0]
+        term = jnp.dot(acts[:, start:stop], piece[...], preferred_element_type=jnp.float32)
+        total = term if total is None else total + term
+        start = stop
+    return total
+
+
+def product_kernel(counts, acts_ref, *refs):
+    *pieces, other_ref, mine_ref = refs
+    start = 0
+    acts = acts_ref[...]
+    for at, count in enumerate(counts):
+        product = accumulate(acts, pieces[start : start + count])
+        other_ref[at] = product[:192].astype(jnp.bfloat16)
+        mine_ref[at] = product[192:]
+        start += count
+
+
+def products(acts, weights):
+    flat = [piece for weight in weights for piece in weight]
+    counts = tuple(len(weight) for weight in weights)
+    return pl.pallas_call(
+        lambda *refs: product_kernel(counts, *refs),
+        out_shape=(
+            jax.ShapeDtypeStruct((2, 192, 1024), jnp.bfloat16),
+            jax.ShapeDtypeStruct((2, 192, 1024), jnp.float32),
+        ),
+        in_specs=[pl.BlockSpec(memory_space=pltpu.VMEM)] * (1 + len(flat)),
+        out_specs=(pl.BlockSpec(memory_space=pltpu.VMEM),) * 2,
+        compiler_params=pltpu.CompilerParams(vmem_limit_bytes=32 * 1024 * 1024),
+        cost_estimate=pl.CostEstimate(flops=1_300_000_000, bytes_accessed=6_000_000, transcendentals=0),
+    )(acts, *flat)
+
+
+def arrange_kernel(source_ref, own_ref, next_1_ref, next_2_ref, out_ref):
+    column = lax.broadcasted_iota(jnp.int32, (384, 128), 1)
+    source = source_ref[...]
+    total = None
+    for at, rows_ref in enumerate((own_ref, next_1_ref, next_2_ref)):
+        chosen = jnp.where(source == column + 128 * at, 1.0, 0.0).astype(jnp.bfloat16)
+        term = jnp.dot(chosen, rows_ref[...], preferred_element_type=jnp.float32)
+        total = term if total is None else total + term
+    out_ref[...] = total.astype(jnp.bfloat16)
+
+
+def arrange(source, own, next_1, next_2):
+    return pl.pallas_call(
+        arrange_kernel,
+        out_shape=jax.ShapeDtypeStruct((384, 832), jnp.bfloat16),
+        in_specs=[pl.BlockSpec(memory_space=pltpu.VMEM)] * 4,
+        out_specs=pl.BlockSpec(memory_space=pltpu.VMEM),
+        compiler_params=pltpu.CompilerParams(vmem_limit_bytes=16 * 1024 * 1024),
+        cost_estimate=pl.CostEstimate(flops=20_000_000_000, bytes_accessed=1_500_000, transcendentals=0),
+    )(source, own, next_1, next_2)
+
+
 def quantize_weight(weight_matrix, weight_exponent):
     scaling = jnp.exp2(weight_exponent.astype(jnp.float32)).astype(jnp.bfloat16).astype(jnp.float32)[None, :]
     clipped = jnp.clip(weight_matrix.astype(jnp.float32) / scaling, -7.5, 7.5)
@@ -128,54 +213,61 @@
 
 
 def row_order(h, x, y_low, c):
-    at = lax.broadcasted_iota(jnp.int32, (384, 384), 0)
-    source = lax.broadcasted_iota(jnp.int32, (384, 384), 1)
+    at = lax.broadcasted_iota(jnp.int32, (384, 1), 0)
     core = jnp.where(at < 192, 1 - c, c)
     rest = at % 192
     parity = jnp.where(rest < 96, 1 - y_low, y_low)
     rest = rest % 96
     y = 2 * (rest // 24) + parity
     row = (2 * y + core) * 24 + rest % 24
-    shifted = (row - 128 * ((h + x) % 3) + 384) % 384
-    return (source == shifted).astype(jnp.bfloat16)
+    return (row - 128 * ((h + x) % 3) + 384) % 384
 
 
 def shards(hidden, down_weight, act_exponent, clip_index, weight_exponent):
     h, x, y_low, c = (lax.axis_index(name) for name in ("h", "x", "yl", "c"))
     y_high = lax.axis_index("yh")
 
-    weight_0 = quantize_weight(down_weight, weight_exponent)
-    weight_1 = lax.ppermute(weight_0, "x", ring(4, -1))
-    weight_3 = lax.ppermute(weight_0, "x", ring(4, 1))
-    weight_2 = jnp.concatenate(
-        [
-            lax.ppermute(weight_3[:416], "x", ring(4, 1)),
-            lax.ppermute(weight_1[416:], "x", ring(4, -1)),
-        ],
-        axis=0,
-    )
-
-    scaling = jnp.exp2(act_exponent.astype(jnp.float32)).astype(jnp.bfloat16)
-    inverse = (1.0 / scaling.astype(jnp.float32)).astype(jnp.bfloat16)
-    level = jnp.broadcast_to((7.5 - clip_index.astype(jnp.float32)).astype(jnp.bfloat16)[None, :], (128, 13))
-    packed = jnp.concatenate([hidden, scaling, inverse, level, jnp.zeros((128, 25), jnp.bfloat16)], axis=1)
+    def quantized_rows(source, start, stop):
+        return quantize_weight(source[start:stop], weight_exponent)
+
+    def to_right(rows):
+        return lax.ppermute(rows, "x", ring(4, 1))
+
+    def to_left(rows):
+        return lax.ppermute(rows, "x", ring(4, -1))
+
+    packed = pack(hidden, act_exponent, clip_index)
     arrived = lax.all_to_all(packed.reshape(64, 2, WIDTH), TENSOR, split_axis=0, concat_axis=0, tiled=True)
+    first_0 = quantized_rows(down_weight, 0, 256)
+    third_0 = quantized_rows(down_weight, 512, 832)
+    first_3, third_1 = to_right(first_0), to_left(third_0)
+
     quantized = rotate_and_quantize(arrived.reshape(128, WIDTH))
     returned = lax.all_to_all(quantized.reshape(64, 2, 832), TENSOR, split_axis=0, concat_axis=0, tiled=True)
+    second_3 = to_right(quantized_rows(down_weight, 256, 640))
+    second_1 = to_left(quantized_rows(down_weight, 128, 512))
+    second_0 = quantized_rows(down_weight, 256, 512)
+
     own = returned.reshape(128, 832)
     next_1 = lax.ppermute(own, "h", ring(3, -1))
     next_2 = lax.ppermute(own, "h", ring(3, 1))
-    gathered = jnp.concatenate([own, next_1, next_2], axis=0)
-    acts = jnp.dot(row_order(h, x, y_low, c), gathered, preferred_element_type=jnp.float32).astype(jnp.bfloat16)
+    last_3 = to_right(third_0[128:])
+    last_1 = to_left(first_0[:128])
+    early_2 = to_right(jnp.concatenate([first_3, second_3[:128]], axis=0))
+    late_2 = to_left(jnp.concatenate([second_1[256:], third_1], axis=0))
+    weight_0 = (first_0, second_0, third_0)
+    weight_1 = (last_1, second_1, third_1)
+    weight_2 = (early_2, late_2)
+    weight_3 = (first_3, second_3, last_3)
+    acts = arrange(row_order(h, x, y_low, c), own, next_1, next_2)
 
     y_pairs_near = [(y, y ^ 1) for y in range(8)]
     y_pairs_far = [(y, (y - 1) % 8 if y % 2 == 0 else (y + 1) % 8) for y in range(8)]
     parts = []
     for weights, y_pairs in (((weight_0, weight_1), y_pairs_near), ((weight_3, weight_2), y_pairs_far)):
-        products = [jnp.dot(acts, weight, preferred_element_type=jnp.float32) for weight in weights]
-        other = jnp.stack([product[:192] for product in products]).astype(jnp.bfloat16)
+        other, own_rows = products(acts, weights)
         from_core = lax.ppermute(other, "c", [(0, 1), (1, 0)])
-        mine = jnp.stack([product[192:] for product in products]) + from_core.astype(jnp.float32)
+        mine = own_rows + from_core.astype(jnp.float32)
         from_y = lax.ppermute(mine[:, :96].astype(jnp.bfloat16), ("yh", "yl"), y_pairs)
         parts.append((mine[:, 96:] + from_y.astype(jnp.float32)).astype(jnp.bfloat16))
     sums = jnp.concatenate(parts, axis=0).reshape(16, 24, 1024)

time: 183 us -> 187 us (1.022)
  waiting for transfers between devices: 88 us -> 60.4 us
  starting transfers between devices: 71.4 us -> 94 us
  matrix products: 7.56 us -> 0 us
  Pallas kernels: 0.73 us -> 7.86 us
  other arithmetic: 6.6 us -> 12.4 us
  local copies, waits for them, and re-layouts: 6.88 us -> 11.2 us
    ppermute x4 -> x8, starting transfers between devices: 10.6 us -> 23.9 us  [the longest x4 15.5 us: to_right(): return lax.ppermute(rows, 'x', ring(4, 1))]
    all_to_all x1, waiting for transfers between devices: 10.6 us -> 0.01 us  [shards(): lax.all_to_all(packed.reshape(64, 2, WIDTH), TENSOR, split_axis=0, concat...]
    ppermute x1, starting transfers between devices: 3.16 us -> 11.7 us  [shards(): next_1 = lax.ppermute(own, 'h', ring(3, -1))]
    ppermute x1, starting transfers between devices: 10.3 us -> 1.92 us  [shards(): next_2 = lax.ppermute(own, 'h', ring(3, 1))]
    ppermute x1, waiting for transfers between devices: 8.26 us -> 0.01 us  [shards(): next_2 = lax.ppermute(own, 'h', ring(3, 1))]
    dot_general x5 -> x0, matrix products: 7.56 us -> none  [the longest x4 5.48 us: shards(): jnp.dot(acts, weight, preferred_element_type=jnp.float32)]
    ppermute x1, waiting for transfers between devices: 16.7 us -> 9.33 us  [shards(): next_1 = lax.ppermute(own, 'h', ring(3, -1))]
    pallas_call x0 -> x4, Pallas kernels: none -> 7.14 us  [the longest x2 6.22 us: products(): pl.pallas_call(lambda *refs: product_kernel(counts, *refs), out_shape=(ja...]
  transfers between devices with their start and end apart: 15 -> 19, of which waited for: 10 -> 7; matrix products, arithmetic and copies ran while one was open for 8% -> 9% of each run, Pallas kernels for 0% -> 4%
where the time goes in v3:
time: 187 us; the launch traced here: 186 us
  starting transfers between devices  94 us (50%)
  waiting for transfers between devices  60.4 us (32%)
  other arithmetic  12.4 us (7%)
  local copies, waits for them, and re-layouts  11.2 us (6%)
  Pallas kernels  7.86 us (4%)
    all_to_all x1, waiting for transfers between devices, shards(): lax.all_to_all(sums, ('l', 'yh'), split_axis=0, concat_axis=0, tiled=True)  18.6 us
    ppermute x4, starting transfers between devices, to_right(): return lax.ppermute(rows, 'x', ring(4, 1))  15.5 us
    all_to_all x1, starting transfers between devices, shards(): lax.all_to_all(packed.reshape(64, 2, WIDTH), TENSOR, split_axis=0, concat...  13.7 us
    ppermute x4, waiting for transfers between devices, to_left(): return lax.ppermute(rows, 'x', ring(4, -1))  13.2 us
    ppermute x1, starting transfers between devices, shards(): next_1 = lax.ppermute(own, 'h', ring(3, -1))  11.7 us
    all_to_all x1, starting transfers between devices, shards(): lax.all_to_all(quantized.reshape(64, 2, 832), TENSOR, split_axis=0, conca...  11.6 us
    ppermute x2, waiting for transfers between devices, shards(): lax.ppermute(mine[:, :96].astype(jnp.bfloat16), ('yh', 'yl'), y_pairs)  10.3 us
    ppermute x1, waiting for transfers between devices, shards(): next_1 = lax.ppermute(own, 'h', ring(3, -1))  9.33 us
  transfers between devices with their start and end apart: 19, of which 7 were waited for; matrix products, arithmetic and copies ran while one was open for 9% of the time, Pallas kernels for 4%

profile of v3, /device:TPU:21, one launch (start us, length us, event | category | flops | bytes accessed | tf_op | source)
XLA Modules:
  0.0 186.2 jit_solution(6258664363571890608)
XLA Ops:
  0.0 1.1 copy.16.hidden_ref
  1.1 0.8 copy.17.exponent_ref
  1.9 0.7 copy-done
  2.7 0.7 copy-done.1
  3.5 0.8 reshape.198
  4.3 13.7 %all-to-all-start = ((bf16[64,2,896]{2,1,0:T(2,128)(2,1)}), bf16[64,2,896]{2,1,0:T(2,128)(2,1)S(1)}, u32[]{:S(2)}, u32[]{:S(2)}) async-start(bf16[64,2,896]{2,1,0:T(2,128)(2,1)} %reshape.198), calls=%async_computation | async-start | bytes 458752 | tf_op jit(solution)/shard_map/all_to_all | solution.py:240
  18.0 4.6 %multiply_convert_fusion.1 = (bf16[384,1024]{1,0:T(8,128)(2,1)}, bf16[384,1024]{1,0:T(8,128)(2,1)}) fusion(f32[1024]{0:T(1024)S(1)} %fusion.45, bf16[832,1024]{1,0:T(8,128)(2,1)} %param.10), kind=kLoop, calls=%fused_computation.16 | loop fusion | flops 18874368 | bytes 3149824 | tf_op jit(solution)/shard_map/convert_element_type | solution.py:186
  22.7 2.3 %collective-permute-start.3 = (bf16[384,1024]{1,0:T(8,128)(2,1)}, bf16[384,1024]{1,0:T(8,128)(2,1)}, u32[]{:S(2)}, u32[]{:S(2)}) collective-permute-start(bf16[384,1024]{1,0:T(8,128)(2,1)} %get-tuple-element.15), channel_id=1, source_target_pairs={{0,192},{64,0},{128,64},{192,128},{1,193},{65,1},{129,65},{193,129... | collective-permute-start | bytes 2359304 | tf_op jit(solution)/shard_map/ppermute | solution.py:237
  25.0 1.6 multiply_convert_fusion.3
  26.6 3.1 %collective-permute-start.7 = (bf16[256,1024]{1,0:T(8,128)(2,1)S(1)}, bf16[256,1024]{1,0:T(8,128)(2,1)S(1)}, u32[]{:S(2)}, u32[]{:S(2)}) collective-permute-start(bf16[256,1024]{1,0:T(8,128)(2,1)S(1)} %get-tuple-element.14.refs_1_), channel_id=1, source_target_pairs={{0,64},{64,128},{128,192},{192,0},{1,65},{65,129},{129,193},{193,1... | collective-permute-start | bytes 1572872 | tf_op jit(solution)/shard_map/ppermute | solution.py:234
  29.7 4.0 %collective-permute-start.8 = (bf16[384,1024]{1,0:T(8,128)(2,1)}, bf16[384,1024]{1,0:T(8,128)(2,1)}, u32[]{:S(2)}, u32[]{:S(2)}) collective-permute-start(bf16[384,1024]{1,0:T(8,128)(2,1)} %get-tuple-element.16), channel_id=1, source_target_pairs={{0,64},{64,128},{128,192},{192,0},{1,65},{65,129},{129,193},{193,1... | collective-permute-start | bytes 2359304 | tf_op jit(solution)/shard_map/ppermute | solution.py:234
  33.9 1.1 copy-done.2
  35.0 0.7 shard_map.92
  35.7 0.8 reshape.200
  36.5 11.6 %all-to-all-start.1 = ((bf16[64,2,832]{2,1,0:T(2,128)(2,1)}), bf16[64,2,832]{2,1,0:T(2,128)(2,1)S(1)}, u32[]{:S(2)}, u32[]{:S(2)}) async-start(bf16[64,2,832]{2,1,0:T(2,128)(2,1)} %reshape.200), calls=%async_computation.1 | async-start | bytes 458752 | tf_op jit(solution)/shard_map/all_to_all | solution.py:246
  48.1 2.1 %multiply_convert_fusion.2.refs_3_ = bf16[320,1024]{1,0:T(8,128)(2,1)S(1)} fusion(f32[1024]{0:T(1024)S(1)} %fusion.45, bf16[832,1024]{1,0:T(8,128)(2,1)} %param.10), kind=kLoop, calls=%fused_computation.29 | loop fusion | flops 7864320 | bytes 1314816 | tf_op jit(solution)/shard_map/convert_element_type | solution.py:186
  50.2 1.9 %collective-permute-start.4 = (bf16[320,1024]{1,0:T(8,128)(2,1)S(1)}, bf16[320,1024]{1,0:T(8,128)(2,1)S(1)}, u32[]{:S(2)}, u32[]{:S(2)}) collective-permute-start(bf16[320,1024]{1,0:T(8,128)(2,1)S(1)} %multiply_convert_fusion.2.refs_3_), channel_id=1, source_target_pairs={{0,192},{64,0},{128,64},{192,128},{1,193},{65,1},{129,65},{193,129... | collective-permute-start | bytes 1966088 | tf_op jit(solution)/shard_map/ppermute | solution.py:237
  52.1 0.7 slice.74
  52.8 1.9 %collective-permute-start.2 = (bf16[128,1024]{1,0:T(8,128)(2,1)}, bf16[128,1024]{1,0:T(8,128)(2,1)}, u32[]{:S(2)}, u32[]{:S(2)}) collective-permute-start(bf16[128,1024]{1,0:T(8,128)(2,1)} %slice.74), channel_id=1, source_target_pairs={{0,192},{64,0},{128,64},{192,128},{1,193},{65,1},{129,65},{193,129... | collective-permute-start | bytes 786440 | tf_op jit(solution)/shard_map/ppermute | solution.py:237
  54.8 0.8 slice.77
  55.6 0.5 add_select_fusion.source_ref
  56.1 2.2 %collective-permute-done.8.refs_2_ = bf16[384,1024]{1,0:T(8,128)(2,1)} collective-permute-done((bf16[384,1024]{1,0:T(8,128)(2,1)}, bf16[384,1024]{1,0:T(8,128)(2,1)}, u32[]{:S(2)}, u32[]{:S(2)}) %collective-permute-start.8) | collective-permute-done | bytes 786464 | tf_op jit(solution)/shard_map/ppermute | solution.py:234
  58.3 3.1 %collective-permute-start.9 = (bf16[192,1024]{1,0:T(8,128)(2,1)}, bf16[192,1024]{1,0:T(8,128)(2,1)}, u32[]{:S(2)}, u32[]{:S(2)}) collective-permute-start(bf16[192,1024]{1,0:T(8,128)(2,1)} %slice.77), channel_id=1, source_target_pairs={{0,64},{64,128},{128,192},{192,0},{1,65},{65,129},{129,193},{193,1... | collective-permute-start | bytes 1179656 | tf_op jit(solution)/shard_map/ppermute | solution.py:234
  61.4 1.7 slice.78
  63.1 1.7 slice.79
  65.0 11.7 %collective-permute-start = (bf16[128,832]{1,0:T(8,128)(2,1)S(1)}, bf16[128,832]{1,0:T(8,128)(2,1)S(1)}, u32[]{:S(2)}, u32[]{:S(2)}) collective-permute-start(bf16[128,832]{1,0:T(8,128)(2,1)S(1)} %reshape.201.own_ref), channel_id=1, source_target_pairs={{0,512},{256,0},{512,256},{1,513},{257,1},{513,257},{2,514},{258,2... | collective-permute-start | bytes 638984 | tf_op jit(solution)/shard_map/ppermute | solution.py:252
  76.7 1.9 %collective-permute-start.1 = (bf16[128,832]{1,0:T(8,128)(2,1)S(1)}, bf16[128,832]{1,0:T(8,128)(2,1)S(1)}, u32[]{:S(2)}, u32[]{:S(2)}) collective-permute-start(bf16[128,832]{1,0:T(8,128)(2,1)S(1)} %reshape.201.own_ref), channel_id=1, source_target_pairs={{0,256},{256,512},{512,0},{1,257},{257,513},{513,1},{2,258},{258,5... | collective-permute-start | bytes 638984 | tf_op jit(solution)/shard_map/ppermute | solution.py:253
  78.6 1.0 pad_maximum_fusion.1
  79.7 5.2 %collective-permute-start.10 = (bf16[384,1024]{1,0:T(8,128)(2,1)S(1)}, bf16[384,1024]{1,0:T(8,128)(2,1)S(1)}, u32[]{:S(2)}, u32[]{:S(2)}) collective-permute-start(bf16[384,1024]{1,0:T(8,128)(2,1)S(1)} %pad_maximum_fusion.1), channel_id=1, source_target_pairs={{0,64},{64,128},{128,192},{192,0},{1,65},{65,129},{129,193},{193,1... | collective-permute-start | bytes 2359304 | tf_op jit(solution)/shard_map/ppermute | solution.py:234
  85.0 9.3 %collective-permute-done.next_1_ref = bf16[128,832]{1,0:T(8,128)(2,1)S(1)} collective-permute-done((bf16[128,832]{1,0:T(8,128)(2,1)S(1)}, bf16[128,832]{1,0:T(8,128)(2,1)S(1)}, u32[]{:S(2)}, u32[]{:S(2)}) %collective-permute-start) | collective-permute-done | bytes 213024 | tf_op jit(solution)/shard_map/ppermute | solution.py:252
  94.3 2.3 %collective-permute-start.11 = (bf16[448,1024]{1,0:T(8,128)(2,1)S(1)}, bf16[448,1024]{1,0:T(8,128)(2,1)S(1)}, u32[]{:S(2)}, u32[]{:S(2)}) collective-permute-start(bf16[448,1024]{1,0:T(8,128)(2,1)S(1)} %pad_maximum_fusion), channel_id=1, source_target_pairs={{0,192},{64,0},{128,64},{192,128},{1,193},{65,1},{129,65},{193,129... | collective-permute-start | bytes 2752520 | tf_op jit(solution)/shard_map/ppermute | solution.py:237
  96.6 0.7 shard_map.93.refs_0_
  97.4 3.2 %shard_map.94 = (bf16[2,192,1024]{2,1,0:T(8,128)(2,1)S(1)}, f32[2,192,1024]{2,1,0:T(8,128)S(1)}) custom-call(bf16[384,832]{1,0:T(8,128)(2,1)S(1)} %shard_map.93.refs_0_, bf16[256,1024]{1,0:T(8,128)(2,1)S(1)} %get-tuple-element.14.refs_1_, bf16[256,1024]{1,0:T(8,128)(2,1)S(1)} %get-tuple-element.13.refs_2_, ...), custom_call_target="tpu_custom_call" | custom-call | flops 1300000000 | bytes 6000000 | tf_op jit(solution)/shard_map/pallas_call | solution.py:148
  100.6 4.4 %collective-permute-start.5 = (bf16[2,192,1024]{2,1,0:T(8,128)(2,1)S(1)}, bf16[2,192,1024]{2,1,0:T(8,128)(2,1)S(1)}, u32[]{:S(2)}, u32[]{:S(2)}) collective-permute-start(bf16[2,192,1024]{2,1,0:T(8,128)(2,1)S(1)} %get-tuple-element.10), channel_id=1, source_target_pairs={{0,1},{1,0},{2,3},{3,2},{4,5},{5,4},{6,7},{7,6},{8,9},{9,8},{10,11... | collective-permute-start | bytes 2359304 | tf_op jit(solution)/shard_map/ppermute | solution.py:269
  105.0 13.2 %collective-permute-done.11.refs_5_ = bf16[448,1024]{1,0:T(8,128)(2,1)S(1)} collective-permute-done((bf16[448,1024]{1,0:T(8,128)(2,1)S(1)}, bf16[448,1024]{1,0:T(8,128)(2,1)S(1)}, u32[]{:S(2)}, u32[]{:S(2)}) %collective-permute-start.11) | collective-permute-done | bytes 917536 | tf_op jit(solution)/shard_map/ppermute | solution.py:237
  118.2 3.0 %shard_map.95 = (bf16[2,192,1024]{2,1,0:T(8,128)(2,1)S(1)}, f32[2,192,1024]{2,1,0:T(8,128)S(1)}) custom-call(bf16[384,832]{1,0:T(8,128)(2,1)S(1)} %shard_map.93.refs_0_, bf16[256,1024]{1,0:T(8,128)(2,1)S(1)} %collective-permute-done.7.refs_1_, bf16[384,1024]{1,0:T(8,128)(2,1)} %collective-permute-done.8.refs_2_, ...), custom_call_target="tpu_custom_call" | custom-call | flops 1300000000 | bytes 6000000 | tf_op jit(solution)/shard_map/pallas_call | solution.py:148
  121.2 4.6 %collective-permute-start.12 = (bf16[2,192,1024]{2,1,0:T(8,128)(2,1)S(1)}, bf16[2,192,1024]{2,1,0:T(8,128)(2,1)S(1)}, u32[]{:S(2)}, u32[]{:S(2)}) collective-permute-start(bf16[2,192,1024]{2,1,0:T(8,128)(2,1)S(1)} %get-tuple-element.12), channel_id=1, source_target_pairs={{0,1},{1,0},{2,3},{3,2},{4,5},{5,4},{6,7},{7,6},{8,9},{9,8},{10,11... | collective-permute-start | bytes 2359304 | tf_op jit(solution)/shard_map/ppermute | solution.py:269
  126.1 3.1 %collective-permute-start.6 = (bf16[2,96,1024]{2,1,0:T(8,128)(2,1)S(1)}, bf16[2,96,1024]{2,1,0:T(8,128)(2,1)S(1)}, u32[]{:S(2)}, u32[]{:S(2)}) collective-permute-start(bf16[2,96,1024]{2,1,0:T(8,128)(2,1)S(1)} %slice.105), channel_id=1, source_target_pairs={{0,2},{2,0},{4,6},{6,4},{8,10},{10,8},{12,14},{14,12},{1,3},{3,1},... | collective-permute-start | bytes 1179656 | tf_op jit(solution)/shard_map/ppermute | solution.py:271
  129.5 1.9 %collective-permute-start.13 = (bf16[2,96,1024]{2,1,0:T(8,128)(2,1)S(1)}, bf16[2,96,1024]{2,1,0:T(8,128)(2,1)S(1)}, u32[]{:S(2)}, u32[]{:S(2)}) collective-permute-start(bf16[2,96,1024]{2,1,0:T(8,128)(2,1)S(1)} %slice.104), channel_id=1, source_target_pairs={{0,14},{2,4},{4,2},{6,8},{8,6},{10,12},{12,10},{14,0},{1,15},{3,5}... | collective-permute-start | bytes 1179656 | tf_op jit(solution)/shard_map/ppermute | solution.py:271
  131.5 7.2 %collective-permute-done.6 = bf16[2,96,1024]{2,1,0:T(8,128)(2,1)S(1)} collective-permute-done((bf16[2,96,1024]{2,1,0:T(8,128)(2,1)S(1)}, bf16[2,96,1024]{2,1,0:T(8,128)(2,1)S(1)}, u32[]{:S(2)}, u32[]{:S(2)}) %collective-permute-start.6) | collective-permute-done | bytes 393248 | tf_op jit(solution)/shard_map/ppermute | solution.py:271
  138.8 3.0 %collective-permute-done.13 = bf16[2,96,1024]{2,1,0:T(8,128)(2,1)S(1)} collective-permute-done((bf16[2,96,1024]{2,1,0:T(8,128)(2,1)S(1)}, bf16[2,96,1024]{2,1,0:T(8,128)(2,1)S(1)}, u32[]{:S(2)}, u32[]{:S(2)}) %collective-permute-start.13) | collective-permute-done | bytes 393248 | tf_op jit(solution)/shard_map/ppermute | solution.py:271
  141.9 1.0 pad_maximum_fusion.2
  142.9 7.8 %all-to-all-start.2 = ((bf16[16,24,1024]{2,1,0:T(8,128)(2,1)}), bf16[16,24,1024]{2,1,0:T(8,128)(2,1)S(1)}, u32[]{:S(2)}, u32[]{:S(2)}) async-start(bf16[16,24,1024]{2,1,0:T(8,128)(2,1)} %bitcast.1), calls=%async_computation.2 | async-start | bytes 1572864 | tf_op jit(solution)/shard_map/all_to_all | solution.py:274
  150.7 18.6 %all-to-all-done.2 = bf16[16,24,1024]{2,1,0:T(8,128)(2,1)S(1)} async-done(((bf16[16,24,1024]{2,1,0:T(8,128)(2,1)}), bf16[16,24,1024]{2,1,0:T(8,128)(2,1)S(1)}, u32[]{:S(2)}, u32[]{:S(2)}) %all-to-all-start.2) | async-done | bytes 786464 | tf_op jit(solution)/shard_map/all_to_all | solution.py:274
  169.5 7.4 %collective-permute-start.15 = (bf16[24,1024]{1,0:T(8,128)(2,1)S(1)}, bf16[24,1024]{1,0:T(8,128)(2,1)S(1)}, u32[]{:S(2)}, u32[]{:S(2)}) collective-permute-start(bf16[24,1024]{1,0:T(8,128)(2,1)S(1)} %reduce_sum.12), channel_id=1, source_target_pairs={{0,0},{1,1},{2,2},{3,3},{4,4},{5,21},{6,22},{7,23},{8,24},{9,25},{... | collective-permute-start | bytes 147464 | tf_op jit(solution)/shard_map/ppermute | solution.py:280
  176.9 1.9 %collective-permute-start.14 = (bf16[8,1024]{1,0:T(8,128)(2,1)S(1)}, bf16[8,1024]{1,0:T(8,128)(2,1)S(1)}, u32[]{:S(2)}, u32[]{:S(2)}) collective-permute-start(bf16[8,1024]{1,0:T(8,128)(2,1)S(1)} %slice_select_fusion.2), channel_id=1, source_target_pairs={{5,5},{10,42},{21,69},{26,106},{37,197},{42,234},{53,133},{58,170}... | collective-permute-start | bytes 49160 | tf_op jit(solution)/shard_map/ppermute | solution.py:281
  178.8 6.7 %collective-permute-done.14 = bf16[8,1024]{1,0:T(8,128)(2,1)S(1)} collective-permute-done((bf16[8,1024]{1,0:T(8,128)(2,1)S(1)}, bf16[8,1024]{1,0:T(8,128)(2,1)S(1)}, u32[]{:S(2)}, u32[]{:S(2)}) %collective-permute-start.14) | collective-permute-done | bytes 16416 | tf_op jit(solution)/shard_map/ppermute | solution.py:281
  185.6 0.6 pad_maximum_fusion.3
  (39 shorter events, 1.5 us)
Async XLA Ops:
  0.0 18.0 %copy-start.7 = (s32[1024]{0:T(1024)S(1)}, s32[1024]{0:T(1024)}, u32[]{:S(2)}) copy-start(s32[1024]{0:T(1024)} %param.13) | copy-start | bytes 12292
  1.9 0.7 copy-start
  2.7 0.7 copy-start.1
  4.3 29.5 %all-to-all-start = ((bf16[64,2,896]{2,1,0:T(2,128)(2,1)}), bf16[64,2,896]{2,1,0:T(2,128)(2,1)S(1)}, u32[]{:S(2)}, u32[]{:S(2)}) async-start(bf16[64,2,896]{2,1,0:T(2,128)(2,1)} %reshape.198), calls=%async_computation | async-start | bytes 458752 | tf_op jit(solution)/shard_map/all_to_all | solution.py:240
  18.0 7.0 %copy-start.5 = (bf16[832,1024]{1,0:T(8,128)(2,1)S(1)}, bf16[832,1024]{1,0:T(8,128)(2,1)}, u32[]{:S(2)}) copy-start(bf16[832,1024]{1,0:T(8,128)(2,1)} %param.10) | copy-start | bytes 5111812
  22.7 11.2 %copy-start.3 = (bf16[128,128]{1,0:T(8,128)(2,1)S(1)}, bf16[128,128]{1,0:T(8,128)(2,1)}, u32[]{:S(2)}) copy-start(bf16[128,128]{1,0:T(8,128)(2,1)} %constant.135.clone.rows_ref) | copy-start | bytes 98308
  22.7 11.2 %copy-start.4 = (bf16[128,128]{1,0:T(8,128)(2,1)S(1)}, bf16[128,128]{1,0:T(8,128)(2,1)}, u32[]{:S(2)}) copy-start(bf16[128,128]{1,0:T(8,128)(2,1)} %constant.136.clone.lanes_ref) | copy-start | bytes 98308
  22.7 40.4 %collective-permute-start.3 = (bf16[384,1024]{1,0:T(8,128)(2,1)}, bf16[384,1024]{1,0:T(8,128)(2,1)}, u32[]{:S(2)}, u32[]{:S(2)}) collective-permute-start(bf16[384,1024]{1,0:T(8,128)(2,1)} %get-tuple-element.15), channel_id=1, source_target_pairs={{0,192},{64,0},{128,64},{192,128},{1,193},{65,1},{129,65},{193,129... | collective-permute-start | bytes 2359304 | tf_op jit(solution)/shard_map/ppermute | solution.py:237
  26.6 50.1 %collective-permute-start.7 = (bf16[256,1024]{1,0:T(8,128)(2,1)S(1)}, bf16[256,1024]{1,0:T(8,128)(2,1)S(1)}, u32[]{:S(2)}, u32[]{:S(2)}) collective-permute-start(bf16[256,1024]{1,0:T(8,128)(2,1)S(1)} %get-tuple-element.14.refs_1_), channel_id=1, source_target_pairs={{0,64},{64,128},{128,192},{192,0},{1,65},{65,129},{129,193},{193,1... | collective-permute-start | bytes 1572872 | tf_op jit(solution)/shard_map/ppermute | solution.py:234
  29.7 28.6 %collective-permute-start.8 = (bf16[384,1024]{1,0:T(8,128)(2,1)}, bf16[384,1024]{1,0:T(8,128)(2,1)}, u32[]{:S(2)}, u32[]{:S(2)}) collective-permute-start(bf16[384,1024]{1,0:T(8,128)(2,1)} %get-tuple-element.16), channel_id=1, source_target_pairs={{0,64},{64,128},{128,192},{192,0},{1,65},{65,129},{129,193},{193,1... | collective-permute-start | bytes 2359304 | tf_op jit(solution)/shard_map/ppermute | solution.py:234
  33.9 1.1 copy-start.2
  36.5 28.3 %all-to-all-start.1 = ((bf16[64,2,832]{2,1,0:T(2,128)(2,1)}), bf16[64,2,832]{2,1,0:T(2,128)(2,1)S(1)}, u32[]{:S(2)}, u32[]{:S(2)}) async-start(bf16[64,2,832]{2,1,0:T(2,128)(2,1)} %reshape.200), calls=%async_computation.1 | async-start | bytes 458752 | tf_op jit(solution)/shard_map/all_to_all | solution.py:246
  50.2 29.4 %collective-permute-start.4 = (bf16[320,1024]{1,0:T(8,128)(2,1)S(1)}, bf16[320,1024]{1,0:T(8,128)(2,1)S(1)}, u32[]{:S(2)}, u32[]{:S(2)}) collective-permute-start(bf16[320,1024]{1,0:T(8,128)(2,1)S(1)} %multiply_convert_fusion.2.refs_3_), channel_id=1, source_target_pairs={{0,192},{64,0},{128,64},{192,128},{1,193},{65,1},{129,65},{193,129... | collective-permute-start | bytes 1966088 | tf_op jit(solution)/shard_map/ppermute | solution.py:237
  52.8 44.5 %collective-permute-start.2 = (bf16[128,1024]{1,0:T(8,128)(2,1)}, bf16[128,1024]{1,0:T(8,128)(2,1)}, u32[]{:S(2)}, u32[]{:S(2)}) collective-permute-start(bf16[128,1024]{1,0:T(8,128)(2,1)} %slice.74), channel_id=1, source_target_pairs={{0,192},{64,0},{128,64},{192,128},{1,193},{65,1},{129,65},{193,129... | collective-permute-start | bytes 786440 | tf_op jit(solution)/shard_map/ppermute | solution.py:237
  58.3 46.7 %collective-permute-start.9 = (bf16[192,1024]{1,0:T(8,128)(2,1)}, bf16[192,1024]{1,0:T(8,128)(2,1)}, u32[]{:S(2)}, u32[]{:S(2)}) collective-permute-start(bf16[192,1024]{1,0:T(8,128)(2,1)} %slice.77), channel_id=1, source_target_pairs={{0,64},{64,128},{128,192},{192,0},{1,65},{65,129},{129,193},{193,1... | collective-permute-start | bytes 1179656 | tf_op jit(solution)/shard_map/ppermute | solution.py:234
  65.0 19.9 %copy-start.6 = (bf16[128,1024]{1,0:T(8,128)(2,1)S(1)}, bf16[128,1024]{1,0:T(8,128)(2,1)}, u32[]{:S(2)}) copy-start(bf16[128,1024]{1,0:T(8,128)(2,1)} %slice.79) | copy-start | bytes 786436
  65.0 29.3 %collective-permute-start = (bf16[128,832]{1,0:T(8,128)(2,1)S(1)}, bf16[128,832]{1,0:T(8,128)(2,1)S(1)}, u32[]{:S(2)}, u32[]{:S(2)}) collective-permute-start(bf16[128,832]{1,0:T(8,128)(2,1)S(1)} %reshape.201.own_ref), channel_id=1, source_target_pairs={{0,512},{256,0},{512,256},{1,513},{257,1},{513,257},{2,514},{258,2... | collective-permute-start | bytes 638984 | tf_op jit(solution)/shard_map/ppermute | solution.py:252
  76.7 19.9 %collective-permute-start.1 = (bf16[128,832]{1,0:T(8,128)(2,1)S(1)}, bf16[128,832]{1,0:T(8,128)(2,1)S(1)}, u32[]{:S(2)}, u32[]{:S(2)}) collective-permute-start(bf16[128,832]{1,0:T(8,128)(2,1)S(1)} %reshape.201.own_ref), channel_id=1, source_target_pairs={{0,256},{256,512},{512,0},{1,257},{257,513},{513,1},{2,258},{258,5... | collective-permute-start | bytes 638984 | tf_op jit(solution)/shard_map/ppermute | solution.py:253
  79.7 25.4 %collective-permute-start.10 = (bf16[384,1024]{1,0:T(8,128)(2,1)S(1)}, bf16[384,1024]{1,0:T(8,128)(2,1)S(1)}, u32[]{:S(2)}, u32[]{:S(2)}) collective-permute-start(bf16[384,1024]{1,0:T(8,128)(2,1)S(1)} %pad_maximum_fusion.1), channel_id=1, source_target_pairs={{0,64},{64,128},{128,192},{192,0},{1,65},{65,129},{129,193},{193,1... | collective-permute-start | bytes 2359304 | tf_op jit(solution)/shard_map/ppermute | solution.py:234
  94.3 23.9 %collective-permute-start.11 = (bf16[448,1024]{1,0:T(8,128)(2,1)S(1)}, bf16[448,1024]{1,0:T(8,128)(2,1)S(1)}, u32[]{:S(2)}, u32[]{:S(2)}) collective-permute-start(bf16[448,1024]{1,0:T(8,128)(2,1)S(1)} %pad_maximum_fusion), channel_id=1, source_target_pairs={{0,192},{64,0},{128,64},{192,128},{1,193},{65,1},{129,65},{193,129... | collective-permute-start | bytes 2752520 | tf_op jit(solution)/shard_map/ppermute | solution.py:237
  100.6 25.2 %collective-permute-start.5 = (bf16[2,192,1024]{2,1,0:T(8,128)(2,1)S(1)}, bf16[2,192,1024]{2,1,0:T(8,128)(2,1)S(1)}, u32[]{:S(2)}, u32[]{:S(2)}) collective-permute-start(bf16[2,192,1024]{2,1,0:T(8,128)(2,1)S(1)} %get-tuple-element.10), channel_id=1, source_target_pairs={{0,1},{1,0},{2,3},{3,2},{4,5},{5,4},{6,7},{7,6},{8,9},{9,8},{10,11... | collective-permute-start | bytes 2359304 | tf_op jit(solution)/shard_map/ppermute | solution.py:269
  121.2 8.0 %collective-permute-start.12 = (bf16[2,192,1024]{2,1,0:T(8,128)(2,1)S(1)}, bf16[2,192,1024]{2,1,0:T(8,128)(2,1)S(1)}, u32[]{:S(2)}, u32[]{:S(2)}) collective-permute-start(bf16[2,192,1024]{2,1,0:T(8,128)(2,1)S(1)} %get-tuple-element.12), channel_id=1, source_target_pairs={{0,1},{1,0},{2,3},{3,2},{4,5},{5,4},{6,7},{7,6},{8,9},{9,8},{10,11... | collective-permute-start | bytes 2359304 | tf_op jit(solution)/shard_map/ppermute | solution.py:269
  126.1 12.6 %collective-permute-start.6 = (bf16[2,96,1024]{2,1,0:T(8,128)(2,1)S(1)}, bf16[2,96,1024]{2,1,0:T(8,128)(2,1)S(1)}, u32[]{:S(2)}, u32[]{:S(2)}) collective-permute-start(bf16[2,96,1024]{2,1,0:T(8,128)(2,1)S(1)} %slice.105), channel_id=1, source_target_pairs={{0,2},{2,0},{4,6},{6,4},{8,10},{10,8},{12,14},{14,12},{1,3},{3,1},... | collective-permute-start | bytes 1179656 | tf_op jit(solution)/shard_map/ppermute | solution.py:271
  129.5 12.3 %collective-permute-start.13 = (bf16[2,96,1024]{2,1,0:T(8,128)(2,1)S(1)}, bf16[2,96,1024]{2,1,0:T(8,128)(2,1)S(1)}, u32[]{:S(2)}, u32[]{:S(2)}) collective-permute-start(bf16[2,96,1024]{2,1,0:T(8,128)(2,1)S(1)} %slice.104), channel_id=1, source_target_pairs={{0,14},{2,4},{4,2},{6,8},{8,6},{10,12},{12,10},{14,0},{1,15},{3,5}... | collective-permute-start | bytes 1179656 | tf_op jit(solution)/shard_map/ppermute | solution.py:271
  142.9 26.4 %all-to-all-start.2 = ((bf16[16,24,1024]{2,1,0:T(8,128)(2,1)}), bf16[16,24,1024]{2,1,0:T(8,128)(2,1)S(1)}, u32[]{:S(2)}, u32[]{:S(2)}) async-start(bf16[16,24,1024]{2,1,0:T(8,128)(2,1)} %bitcast.1), calls=%async_computation.2 | async-start | bytes 1572864 | tf_op jit(solution)/shard_map/all_to_all | solution.py:274
  169.5 16.1 %collective-permute-start.15 = (bf16[24,1024]{1,0:T(8,128)(2,1)S(1)}, bf16[24,1024]{1,0:T(8,128)(2,1)S(1)}, u32[]{:S(2)}, u32[]{:S(2)}) collective-permute-start(bf16[24,1024]{1,0:T(8,128)(2,1)S(1)} %reduce_sum.12), channel_id=1, source_target_pairs={{0,0},{1,1},{2,2},{3,3},{4,4},{5,21},{6,22},{7,23},{8,24},{9,25},{... | collective-permute-start | bytes 147464 | tf_op jit(solution)/shard_map/ppermute | solution.py:280
  176.9 8.7 %collective-permute-start.14 = (bf16[8,1024]{1,0:T(8,128)(2,1)S(1)}, bf16[8,1024]{1,0:T(8,128)(2,1)S(1)}, u32[]{:S(2)}, u32[]{:S(2)}) collective-permute-start(bf16[8,1024]{1,0:T(8,128)(2,1)S(1)} %slice_select_fusion.2), channel_id=1, source_target_pairs={{5,5},{10,42},{21,69},{26,106},{37,197},{42,234},{53,133},{58,170}... | collective-permute-start | bytes 49160 | tf_op jit(solution)/shard_map/ppermute | solution.py:281

commit v4 on v3

--- a/solution.py
+++ b/solution.py
@@ -13,6 +13,7 @@
 TENSOR = ("l", "yh", "yl", "c")
 SLOTS = (0, 1, 3, 2)
 WIDTH = 896
+SPLIT = 384
 
 
 def sine_coefficients():
@@ -95,32 +96,6 @@
     )
 
 
-def pack_kernel(hidden_ref, exponent_ref, index_ref, place_ref, out_ref):
-    out_ref[:, :768] = hidden_ref[:, :768]
-    scaling = jnp.exp2(exponent_ref[...].astype(jnp.float32)).astype(jnp.bfloat16)
-    inverse = (1.0 / scaling.astype(jnp.float32)).astype(jnp.bfloat16)
-    level = jnp.broadcast_to(7.5 - index_ref[...].astype(jnp.float32), (128, 13)).astype(jnp.bfloat16)
-    tail = jnp.dot(hidden_ref[:, 768:], place_ref[:64], preferred_element_type=jnp.float32)
-    for kind, extra in enumerate((scaling, inverse, level)):
-        tail += jnp.dot(extra, place_ref[64 + 16 * kind : 77 + 16 * kind], preferred_element_type=jnp.float32)
-    out_ref[:, 768:] = tail.astype(jnp.bfloat16)
-
-
-def pack(hidden, act_exponent, clip_index):
-    place = np.zeros((112, 128), np.float32)
-    place[np.arange(64), np.arange(64)] = 1.0
-    for kind in range(3):
-        place[64 + 16 * kind + np.arange(13), 64 + 13 * kind + np.arange(13)] = 1.0
-    return pl.pallas_call(
-        pack_kernel,
-        out_shape=jax.ShapeDtypeStruct((128, WIDTH), jnp.bfloat16),
-        in_specs=[pl.BlockSpec(memory_space=pltpu.VMEM)] * 4,
-        out_specs=pl.BlockSpec(memory_space=pltpu.VMEM),
-        compiler_params=pltpu.CompilerParams(vmem_limit_bytes=16 * 1024 * 1024),
-        cost_estimate=pl.CostEstimate(flops=4_000_000, bytes_accessed=500_000, transcendentals=0),
-    )(hidden, act_exponent, clip_index.reshape(1, 13), jnp.asarray(place, jnp.bfloat16))
-
-
 def accumulate(acts, pieces):
     total, start = None, 0
     for piece in pieces:
@@ -227,38 +202,31 @@
     h, x, y_low, c = (lax.axis_index(name) for name in ("h", "x", "yl", "c"))
     y_high = lax.axis_index("yh")
 
-    def quantized_rows(source, start, stop):
-        return quantize_weight(source[start:stop], weight_exponent)
-
     def to_right(rows):
         return lax.ppermute(rows, "x", ring(4, 1))
 
     def to_left(rows):
         return lax.ppermute(rows, "x", ring(4, -1))
 
-    packed = pack(hidden, act_exponent, clip_index)
+    top_0 = quantize_weight(down_weight[:SPLIT], weight_exponent)
+    top_1, top_3 = to_left(top_0), to_right(top_0)
+    scaling = jnp.exp2(act_exponent.astype(jnp.float32)).astype(jnp.bfloat16)
+    inverse = (1.0 / scaling.astype(jnp.float32)).astype(jnp.bfloat16)
+    level = jnp.broadcast_to((7.5 - clip_index.astype(jnp.float32)).astype(jnp.bfloat16)[None, :], (128, 13))
+    packed = jnp.concatenate([hidden, scaling, inverse, level, jnp.zeros((128, 25), jnp.bfloat16)], axis=1)
+    packed, down_weight = lax.optimization_barrier((packed, down_weight))
+    low_0 = quantize_weight(down_weight[SPLIT:], weight_exponent)
     arrived = lax.all_to_all(packed.reshape(64, 2, WIDTH), TENSOR, split_axis=0, concat_axis=0, tiled=True)
-    first_0 = quantized_rows(down_weight, 0, 256)
-    third_0 = quantized_rows(down_weight, 512, 832)
-    first_3, third_1 = to_right(first_0), to_left(third_0)
-
+    arrived, top_1, top_3 = lax.optimization_barrier((arrived, top_1, top_3))
     quantized = rotate_and_quantize(arrived.reshape(128, WIDTH))
     returned = lax.all_to_all(quantized.reshape(64, 2, 832), TENSOR, split_axis=0, concat_axis=0, tiled=True)
-    second_3 = to_right(quantized_rows(down_weight, 256, 640))
-    second_1 = to_left(quantized_rows(down_weight, 128, 512))
-    second_0 = quantized_rows(down_weight, 256, 512)
-
+    low_1, low_3 = to_left(low_0), to_right(low_0)
+    returned, low_1, low_3 = lax.optimization_barrier((returned, low_1, low_3))
     own = returned.reshape(128, 832)
     next_1 = lax.ppermute(own, "h", ring(3, -1))
     next_2 = lax.ppermute(own, "h", ring(3, 1))
-    last_3 = to_right(third_0[128:])
-    last_1 = to_left(first_0[:128])
-    early_2 = to_right(jnp.concatenate([first_3, second_3[:128]], axis=0))
-    late_2 = to_left(jnp.concatenate([second_1[256:], third_1], axis=0))
-    weight_0 = (first_0, second_0, third_0)
-    weight_1 = (last_1, second_1, third_1)
-    weight_2 = (early_2, late_2)
-    weight_3 = (first_3, second_3, last_3)
+    top_2, low_2 = to_right(top_3), to_left(low_1)
+    weight_0, weight_1, weight_2, weight_3 = (top_0, low_0), (top_1, low_1), (top_2, low_2), (top_3, low_3)
     acts = arrange(row_order(h, x, y_low, c), own, next_1, next_2)
 
     y_pairs_near = [(y, y ^ 1) for y in range(8)]

time: 187 us -> 168 us (0.90)
  the two profiles are of different devices: /device:TPU:21 before, /device:TPU:40 now
where the time goes in v4:
time: 168 us; the launch traced here: 167 us
  starting transfers between devices  91.4 us (54%)
  waiting for transfers between devices  55.3 us (33%)
  other arithmetic  8.56 us (5%)
  Pallas kernels  7.57 us (5%)
  local copies, waits for them, and re-layouts  3.82 us (2%)
    all_to_all x1, waiting for transfers between devices, shards(): lax.all_to_all(sums, ('l', 'yh'), split_axis=0, concat_axis=0, tiled=True)  18 us
    ppermute x3, starting transfers between devices, to_left(): return lax.ppermute(rows, 'x', ring(4, -1))  14.9 us
    all_to_all x1, starting transfers between devices, shards(): lax.all_to_all(sums, ('l', 'yh'), split_axis=0, concat_axis=0, tiled=True)  14.5 us
    all_to_all x1, starting transfers between devices, shards(): lax.all_to_all(packed.reshape(64, 2, WIDTH), TENSOR, split_axis=0, concat...  13.1 us
    ppermute x1, starting transfers between devices, shards(): next_1 = lax.ppermute(own, 'h', ring(3, -1))  11.9 us
    all_to_all x1, starting transfers between devices, shards(): lax.all_to_all(quantized.reshape(64, 2, 832), TENSOR, split_axis=0, conca...  10.7 us
    ppermute x2, waiting for transfers between devices, shards(): lax.ppermute(mine[:, :96].astype(jnp.bfloat16), ('yh', 'yl'), y_pairs)  9.81 us
    ppermute x1, waiting for transfers between devices, shards(): next_1 = lax.ppermute(own, 'h', ring(3, -1))  9.71 us
  transfers between devices with their start and end apart: 17, of which 8 were waited for; matrix products, arithmetic and copies ran while one was open for 4% of the time, Pallas kernels for 5%

profile of v4, /device:TPU:40, one launch (start us, length us, event | category | flops | bytes accessed | tf_op | source)
XLA Modules:
  0.0 167.1 jit_solution(13013006722687072616)
XLA Ops:
  0.0 0.7 fusion.30
  0.7 2.3 %multiply_convert_fusion.1.refs_1_ = bf16[384,1024]{1,0:T(8,128)(2,1)S(1)} fusion(f32[1024]{0:T(1024)S(1)} %fusion.30, bf16[832,1024]{1,0:T(8,128)(2,1)} %param.9), kind=kLoop, calls=%fused_computation.15 | loop fusion | flops 9437184 | bytes 1576960 | tf_op jit(solution)/shard_map/convert_element_type | solution.py:161
  3.1 4.7 %collective-permute-start = (bf16[384,1024]{1,0:T(8,128)(2,1)S(1)}, bf16[384,1024]{1,0:T(8,128)(2,1)}, u32[]{:S(2)}, u32[]{:S(2)}) collective-permute-start(bf16[384,1024]{1,0:T(8,128)(2,1)S(1)} %multiply_convert_fusion.1.refs_1_), channel_id=1, source_target_pairs={{0,192},{64,0},{128,64},{192,128},{1,193},{65,1},{129,65},{193,129... | collective-permute-start | bytes 2359304 | tf_op jit(solution)/shard_map/ppermute | solution.py:209
  7.8 1.9 %collective-permute-start.1 = (bf16[384,1024]{1,0:T(8,128)(2,1)S(1)}, bf16[384,1024]{1,0:T(8,128)(2,1)}, u32[]{:S(2)}, u32[]{:S(2)}) collective-permute-start(bf16[384,1024]{1,0:T(8,128)(2,1)S(1)} %multiply_convert_fusion.1.refs_1_), channel_id=1, source_target_pairs={{0,64},{64,128},{128,192},{192,0},{1,65},{65,129},{129,193},{193,1... | collective-permute-start | bytes 2359304 | tf_op jit(solution)/shard_map/ppermute | solution.py:206
  9.7 0.1 broadcast_in_dim.35
  9.8 0.5 concatenate.9
  10.3 0.2 copy.13
  10.5 0.8 reshape.195
  11.3 13.1 %all-to-all-start = ((bf16[64,2,896]{2,1,0:T(2,128)(2,1)}), bf16[64,2,896]{2,1,0:T(2,128)(2,1)S(1)}, u32[]{:S(2)}, u32[]{:S(2)}) async-start(bf16[64,2,896]{2,1,0:T(2,128)(2,1)} %reshape.195), calls=%async_computation | async-start | bytes 458752 | tf_op jit(solution)/shard_map/all_to_all | solution.py:219
  24.4 2.6 %multiply_convert_fusion.refs_2_ = bf16[448,1024]{1,0:T(8,128)(2,1)S(1)} fusion(f32[1024]{0:T(1024)S(1)} %fusion.30, bf16[832,1024]{1,0:T(8,128)(2,1)} %param.9), kind=kLoop, calls=%fused_computation.2 | loop fusion | flops 11010048 | bytes 1839104 | tf_op jit(solution)/shard_map/convert_element_type | solution.py:161
  27.0 5.1 %collective-permute-start.2 = (bf16[448,1024]{1,0:T(8,128)(2,1)S(1)}, bf16[448,1024]{1,0:T(8,128)(2,1)}, u32[]{:S(2)}, u32[]{:S(2)}) collective-permute-start(bf16[448,1024]{1,0:T(8,128)(2,1)S(1)} %multiply_convert_fusion.refs_2_), channel_id=1, source_target_pairs={{0,192},{64,0},{128,64},{192,128},{1,193},{65,1},{129,65},{193,129... | collective-permute-start | bytes 2752520 | tf_op jit(solution)/shard_map/ppermute | solution.py:209
  32.1 1.9 %collective-permute-start.3 = (bf16[448,1024]{1,0:T(8,128)(2,1)S(1)}, bf16[448,1024]{1,0:T(8,128)(2,1)S(1)}, u32[]{:S(2)}, u32[]{:S(2)}) collective-permute-start(bf16[448,1024]{1,0:T(8,128)(2,1)S(1)} %multiply_convert_fusion.refs_2_), channel_id=1, source_target_pairs={{0,64},{64,128},{128,192},{192,0},{1,65},{65,129},{129,193},{193,1... | collective-permute-start | bytes 2752520 | tf_op jit(solution)/shard_map/ppermute | solution.py:206
  34.1 0.1 reshape.196.x_ref
  34.2 1.1 copy-done
  35.3 0.7 shard_map.82
  36.1 0.8 reshape.197
  36.9 10.7 %all-to-all-start.1 = ((bf16[64,2,832]{2,1,0:T(2,128)(2,1)}), bf16[64,2,832]{2,1,0:T(2,128)(2,1)S(1)}, u32[]{:S(2)}, u32[]{:S(2)}) async-start(bf16[64,2,832]{2,1,0:T(2,128)(2,1)} %reshape.197), calls=%async_computation.1 | async-start | bytes 458752 | tf_op jit(solution)/shard_map/all_to_all | solution.py:222
  47.6 4.5 %collective-permute-done.2.refs_4_ = bf16[448,1024]{1,0:T(8,128)(2,1)} collective-permute-done((bf16[448,1024]{1,0:T(8,128)(2,1)S(1)}, bf16[448,1024]{1,0:T(8,128)(2,1)}, u32[]{:S(2)}, u32[]{:S(2)}) %collective-permute-start.2) | collective-permute-done | bytes 917536 | tf_op jit(solution)/shard_map/ppermute | solution.py:209
  52.0 5.3 %collective-permute-done.3.refs_2_ = bf16[448,1024]{1,0:T(8,128)(2,1)S(1)} collective-permute-done((bf16[448,1024]{1,0:T(8,128)(2,1)S(1)}, bf16[448,1024]{1,0:T(8,128)(2,1)S(1)}, u32[]{:S(2)}, u32[]{:S(2)}) %collective-permute-start.3) | collective-permute-done | bytes 917536 | tf_op jit(solution)/shard_map/ppermute | solution.py:206
  57.4 0.2 reshape.198.own_ref
  57.6 11.9 %collective-permute-start.4 = (bf16[128,832]{1,0:T(8,128)(2,1)S(1)}, bf16[128,832]{1,0:T(8,128)(2,1)S(1)}, u32[]{:S(2)}, u32[]{:S(2)}) collective-permute-start(bf16[128,832]{1,0:T(8,128)(2,1)S(1)} %reshape.198.own_ref), channel_id=1, source_target_pairs={{0,512},{256,0},{512,256},{1,513},{257,1},{513,257},{2,514},{258,2... | collective-permute-start | bytes 638984 | tf_op jit(solution)/shard_map/ppermute | solution.py:226
  69.4 1.9 %collective-permute-start.5 = (bf16[128,832]{1,0:T(8,128)(2,1)S(1)}, bf16[128,832]{1,0:T(8,128)(2,1)S(1)}, u32[]{:S(2)}, u32[]{:S(2)}) collective-permute-start(bf16[128,832]{1,0:T(8,128)(2,1)S(1)} %reshape.198.own_ref), channel_id=1, source_target_pairs={{0,256},{256,512},{512,0},{1,257},{257,513},{513,1},{2,258},{258,5... | collective-permute-start | bytes 638984 | tf_op jit(solution)/shard_map/ppermute | solution.py:227
  71.4 0.5 add_select_fusion.source_ref
  71.9 1.9 %collective-permute-start.8 = (bf16[384,1024]{1,0:T(8,128)(2,1)}, bf16[384,1024]{1,0:T(8,128)(2,1)S(1)}, u32[]{:S(2)}, u32[]{:S(2)}) collective-permute-start(bf16[384,1024]{1,0:T(8,128)(2,1)} %collective-permute-done.1.refs_1_), channel_id=1, source_target_pairs={{0,64},{64,128},{128,192},{192,0},{1,65},{65,129},{129,193},{193,1... | collective-permute-start | bytes 2359304 | tf_op jit(solution)/shard_map/ppermute | solution.py:206
  73.8 5.1 %collective-permute-start.9 = (bf16[448,1024]{1,0:T(8,128)(2,1)}, bf16[448,1024]{1,0:T(8,128)(2,1)S(1)}, u32[]{:S(2)}, u32[]{:S(2)}) collective-permute-start(bf16[448,1024]{1,0:T(8,128)(2,1)} %collective-permute-done.2.refs_4_), channel_id=1, source_target_pairs={{0,192},{64,0},{128,64},{192,128},{1,193},{65,1},{129,65},{193,129... | collective-permute-start | bytes 2752520 | tf_op jit(solution)/shard_map/ppermute | solution.py:209
  79.0 9.7 %collective-permute-done.4.next_1_ref = bf16[128,832]{1,0:T(8,128)(2,1)S(1)} collective-permute-done((bf16[128,832]{1,0:T(8,128)(2,1)S(1)}, bf16[128,832]{1,0:T(8,128)(2,1)S(1)}, u32[]{:S(2)}, u32[]{:S(2)}) %collective-permute-start.4) | collective-permute-done | bytes 213024 | tf_op jit(solution)/shard_map/ppermute | solution.py:226
  88.7 0.7 shard_map.83.refs_0_
  89.4 3.2 %shard_map.84 = (bf16[2,192,1024]{2,1,0:T(8,128)(2,1)S(1)}, f32[2,192,1024]{2,1,0:T(8,128)S(1)}) custom-call(bf16[384,832]{1,0:T(8,128)(2,1)S(1)} %shard_map.83.refs_0_, bf16[384,1024]{1,0:T(8,128)(2,1)S(1)} %multiply_convert_fusion.1.refs_1_, bf16[448,1024]{1,0:T(8,128)(2,1)S(1)} %multiply_convert_fusion.refs_2_, ...), custom_call_target="tpu_custom_call" | custom-call | flops 1300000000 | bytes 6000000 | tf_op jit(solution)/shard_map/pallas_call | solution.py:123
  92.6 1.9 %collective-permute-start.6 = (bf16[2,192,1024]{2,1,0:T(8,128)(2,1)S(1)}, bf16[2,192,1024]{2,1,0:T(8,128)(2,1)S(1)}, u32[]{:S(2)}, u32[]{:S(2)}) collective-permute-start(bf16[2,192,1024]{2,1,0:T(8,128)(2,1)S(1)} %get-tuple-element.24), channel_id=1, source_target_pairs={{0,1},{1,0},{2,3},{3,2},{4,5},{5,4},{6,7},{7,6},{8,9},{9,8},{10,11... | collective-permute-start | bytes 2359304 | tf_op jit(solution)/shard_map/ppermute | solution.py:237
  94.6 3.3 %collective-permute-done.9.refs_4_ = bf16[448,1024]{1,0:T(8,128)(2,1)S(1)} collective-permute-done((bf16[448,1024]{1,0:T(8,128)(2,1)}, bf16[448,1024]{1,0:T(8,128)(2,1)S(1)}, u32[]{:S(2)}, u32[]{:S(2)}) %collective-permute-start.9) | collective-permute-done | bytes 917536 | tf_op jit(solution)/shard_map/ppermute | solution.py:209
  97.9 2.9 %shard_map.85 = (bf16[2,192,1024]{2,1,0:T(8,128)(2,1)S(1)}, f32[2,192,1024]{2,1,0:T(8,128)S(1)}) custom-call(bf16[384,832]{1,0:T(8,128)(2,1)S(1)} %shard_map.83.refs_0_, bf16[384,1024]{1,0:T(8,128)(2,1)} %collective-permute-done.1.refs_1_, bf16[448,1024]{1,0:T(8,128)(2,1)S(1)} %collective-permute-done.3.refs_2_, ...), custom_call_target="tpu_custom_call" | custom-call | flops 1300000000 | bytes 6000000 | tf_op jit(solution)/shard_map/pallas_call | solution.py:123
  100.8 1.9 %collective-permute-start.10 = (bf16[2,192,1024]{2,1,0:T(8,128)(2,1)S(1)}, bf16[2,192,1024]{2,1,0:T(8,128)(2,1)S(1)}, u32[]{:S(2)}, u32[]{:S(2)}) collective-permute-start(bf16[2,192,1024]{2,1,0:T(8,128)(2,1)S(1)} %get-tuple-element.28), channel_id=1, source_target_pairs={{0,1},{1,0},{2,3},{3,2},{4,5},{5,4},{6,7},{7,6},{8,9},{9,8},{10,11... | collective-permute-start | bytes 2359304 | tf_op jit(solution)/shard_map/ppermute | solution.py:237
  102.7 0.2 convert_add_fusion.1
  103.0 3.0 %collective-permute-start.7 = (bf16[2,96,1024]{2,1,0:T(8,128)(2,1)S(1)}, bf16[2,96,1024]{2,1,0:T(8,128)(2,1)S(1)}, u32[]{:S(2)}, u32[]{:S(2)}) collective-permute-start(bf16[2,96,1024]{2,1,0:T(8,128)(2,1)S(1)} %slice.70), channel_id=1, source_target_pairs={{0,2},{2,0},{4,6},{6,4},{8,10},{10,8},{12,14},{14,12},{1,3},{3,1},... | collective-permute-start | bytes 1179656 | tf_op jit(solution)/shard_map/ppermute | solution.py:239
  106.0 0.2 convert_add_fusion
  106.3 3.2 %collective-permute-start.11 = (bf16[2,96,1024]{2,1,0:T(8,128)(2,1)S(1)}, bf16[2,96,1024]{2,1,0:T(8,128)(2,1)S(1)}, u32[]{:S(2)}, u32[]{:S(2)}) collective-permute-start(bf16[2,96,1024]{2,1,0:T(8,128)(2,1)S(1)} %slice.69), channel_id=1, source_target_pairs={{0,14},{2,4},{4,2},{6,8},{8,6},{10,12},{12,10},{14,0},{1,15},{3,5}... | collective-permute-start | bytes 1179656 | tf_op jit(solution)/shard_map/ppermute | solution.py:239
  109.5 6.9 %collective-permute-done.7 = bf16[2,96,1024]{2,1,0:T(8,128)(2,1)S(1)} collective-permute-done((bf16[2,96,1024]{2,1,0:T(8,128)(2,1)S(1)}, bf16[2,96,1024]{2,1,0:T(8,128)(2,1)S(1)}, u32[]{:S(2)}, u32[]{:S(2)}) %collective-permute-start.7) | collective-permute-done | bytes 393248 | tf_op jit(solution)/shard_map/ppermute | solution.py:239
  116.4 0.1 fusion.11
  116.5 2.9 %collective-permute-done.11 = bf16[2,96,1024]{2,1,0:T(8,128)(2,1)S(1)} collective-permute-done((bf16[2,96,1024]{2,1,0:T(8,128)(2,1)S(1)}, bf16[2,96,1024]{2,1,0:T(8,128)(2,1)S(1)}, u32[]{:S(2)}, u32[]{:S(2)}) %collective-permute-start.11) | collective-permute-done | bytes 393248 | tf_op jit(solution)/shard_map/ppermute | solution.py:239
  119.4 0.1 fusion.10
  119.5 1.0 pad_maximum_fusion
  120.5 14.5 %all-to-all-start.2 = ((bf16[16,24,1024]{2,1,0:T(8,128)(2,1)}), bf16[16,24,1024]{2,1,0:T(8,128)(2,1)S(1)}, u32[]{:S(2)}, u32[]{:S(2)}) async-start(bf16[16,24,1024]{2,1,0:T(8,128)(2,1)} %bitcast), calls=%async_computation.2 | async-start | bytes 1572864 | tf_op jit(solution)/shard_map/all_to_all | solution.py:242
  135.0 18.0 %all-to-all-done.2 = bf16[16,24,1024]{2,1,0:T(8,128)(2,1)S(1)} async-done(((bf16[16,24,1024]{2,1,0:T(8,128)(2,1)}), bf16[16,24,1024]{2,1,0:T(8,128)(2,1)S(1)}, u32[]{:S(2)}, u32[]{:S(2)}) %all-to-all-start.2) | async-done | bytes 786464 | tf_op jit(solution)/shard_map/all_to_all | solution.py:242
  153.0 0.1 reduce_sum.12
  153.1 3.5 %collective-permute-start.13 = (bf16[24,1024]{1,0:T(8,128)(2,1)S(1)}, bf16[24,1024]{1,0:T(8,128)(2,1)S(1)}, u32[]{:S(2)}, u32[]{:S(2)}) collective-permute-start(bf16[24,1024]{1,0:T(8,128)(2,1)S(1)} %reduce_sum.12), channel_id=1, source_target_pairs={{0,0},{1,1},{2,2},{3,3},{4,4},{5,21},{6,22},{7,23},{8,24},{9,25},{... | collective-permute-start | bytes 147464 | tf_op jit(solution)/shard_map/ppermute | solution.py:248
  156.6 5.1 %collective-permute-start.12 = (bf16[8,1024]{1,0:T(8,128)(2,1)S(1)}, bf16[8,1024]{1,0:T(8,128)(2,1)S(1)}, u32[]{:S(2)}, u32[]{:S(2)}) collective-permute-start(bf16[8,1024]{1,0:T(8,128)(2,1)S(1)} %slice_select_fusion.2), channel_id=1, source_target_pairs={{5,5},{10,42},{21,69},{26,106},{37,197},{42,234},{53,133},{58,170}... | collective-permute-start | bytes 49160 | tf_op jit(solution)/shard_map/ppermute | solution.py:249
  161.8 4.7 %collective-permute-done.12 = bf16[8,1024]{1,0:T(8,128)(2,1)S(1)} collective-permute-done((bf16[8,1024]{1,0:T(8,128)(2,1)S(1)}, bf16[8,1024]{1,0:T(8,128)(2,1)S(1)}, u32[]{:S(2)}, u32[]{:S(2)}) %collective-permute-start.12) | collective-permute-done | bytes 16416 | tf_op jit(solution)/shard_map/ppermute | solution.py:249
  166.5 0.6 pad_maximum_fusion.1
  (27 shorter events, 0.2 us)
Async XLA Ops:
  0.0 9.7 %copy-start.4 = (s32[128,13]{0,1:T(8,128)S(1)}, s32[128,13]{0,1:T(8,128)}, u32[]{:S(2)}) copy-start(s32[128,13]{0,1:T(8,128)} %param.10) | copy-start | bytes 19972
  0.0 9.7 %copy-start.5 = (s32[13]{0:T(128)S(1)}, s32[13]{0:T(128)}, u32[]{:S(2)}) copy-start(s32[13]{0:T(128)} %param.11) | copy-start | bytes 160
  0.0 9.8 %copy-start.3 = (bf16[128,832]{0,1:T(8,128)(2,1)S(1)}, bf16[128,832]{0,1:T(8,128)(2,1)}, u32[]{:S(2)}) copy-start(bf16[128,832]{0,1:T(8,128)(2,1)} %param.8) | copy-start | bytes 638980
  3.1 31.0 %collective-permute-start = (bf16[384,1024]{1,0:T(8,128)(2,1)S(1)}, bf16[384,1024]{1,0:T(8,128)(2,1)}, u32[]{:S(2)}, u32[]{:S(2)}) collective-permute-start(bf16[384,1024]{1,0:T(8,128)(2,1)S(1)} %multiply_convert_fusion.1.refs_1_), channel_id=1, source_target_pairs={{0,192},{64,0},{128,64},{192,128},{1,193},{65,1},{129,65},{193,129... | collective-permute-start | bytes 2359304 | tf_op jit(solution)/shard_map/ppermute | solution.py:209
  7.8 26.3 %collective-permute-start.1 = (bf16[384,1024]{1,0:T(8,128)(2,1)S(1)}, bf16[384,1024]{1,0:T(8,128)(2,1)}, u32[]{:S(2)}, u32[]{:S(2)}) collective-permute-start(bf16[384,1024]{1,0:T(8,128)(2,1)S(1)} %multiply_convert_fusion.1.refs_1_), channel_id=1, source_target_pairs={{0,64},{64,128},{128,192},{192,0},{1,65},{65,129},{129,193},{193,1... | collective-permute-start | bytes 2359304 | tf_op jit(solution)/shard_map/ppermute | solution.py:206
  10.5 23.7 %copy-start.1 = (bf16[128,128]{1,0:T(8,128)(2,1)S(1)}, bf16[128,128]{1,0:T(8,128)(2,1)}, u32[]{:S(2)}) copy-start(bf16[128,128]{1,0:T(8,128)(2,1)} %constant.128.clone.rows_ref) | copy-start | bytes 98308
  10.5 23.7 %copy-start.2 = (bf16[128,128]{1,0:T(8,128)(2,1)S(1)}, bf16[128,128]{1,0:T(8,128)(2,1)}, u32[]{:S(2)}) copy-start(bf16[128,128]{1,0:T(8,128)(2,1)} %constant.129.clone.lanes_ref) | copy-start | bytes 98308
  11.3 22.7 %all-to-all-start = ((bf16[64,2,896]{2,1,0:T(2,128)(2,1)}), bf16[64,2,896]{2,1,0:T(2,128)(2,1)S(1)}, u32[]{:S(2)}, u32[]{:S(2)}) async-start(bf16[64,2,896]{2,1,0:T(2,128)(2,1)} %reshape.195), calls=%async_computation | async-start | bytes 458752 | tf_op jit(solution)/shard_map/all_to_all | solution.py:219
  27.0 25.0 %collective-permute-start.2 = (bf16[448,1024]{1,0:T(8,128)(2,1)S(1)}, bf16[448,1024]{1,0:T(8,128)(2,1)}, u32[]{:S(2)}, u32[]{:S(2)}) collective-permute-start(bf16[448,1024]{1,0:T(8,128)(2,1)S(1)} %multiply_convert_fusion.refs_2_), channel_id=1, source_target_pairs={{0,192},{64,0},{128,64},{192,128},{1,193},{65,1},{129,65},{193,129... | collective-permute-start | bytes 2752520 | tf_op jit(solution)/shard_map/ppermute | solution.py:209
  32.1 25.2 %collective-permute-start.3 = (bf16[448,1024]{1,0:T(8,128)(2,1)S(1)}, bf16[448,1024]{1,0:T(8,128)(2,1)S(1)}, u32[]{:S(2)}, u32[]{:S(2)}) collective-permute-start(bf16[448,1024]{1,0:T(8,128)(2,1)S(1)} %multiply_convert_fusion.refs_2_), channel_id=1, source_target_pairs={{0,64},{64,128},{128,192},{192,0},{1,65},{65,129},{129,193},{193,1... | collective-permute-start | bytes 2752520 | tf_op jit(solution)/shard_map/ppermute | solution.py:206
  34.2 1.1 copy-start
  36.9 20.5 %all-to-all-start.1 = ((bf16[64,2,832]{2,1,0:T(2,128)(2,1)}), bf16[64,2,832]{2,1,0:T(2,128)(2,1)S(1)}, u32[]{:S(2)}, u32[]{:S(2)}) async-start(bf16[64,2,832]{2,1,0:T(2,128)(2,1)} %reshape.197), calls=%async_computation.1 | async-start | bytes 458752 | tf_op jit(solution)/shard_map/all_to_all | solution.py:222
  57.6 31.1 %collective-permute-start.4 = (bf16[128,832]{1,0:T(8,128)(2,1)S(1)}, bf16[128,832]{1,0:T(8,128)(2,1)S(1)}, u32[]{:S(2)}, u32[]{:S(2)}) collective-permute-start(bf16[128,832]{1,0:T(8,128)(2,1)S(1)} %reshape.198.own_ref), channel_id=1, source_target_pairs={{0,512},{256,0},{512,256},{1,513},{257,1},{513,257},{2,514},{258,2... | collective-permute-start | bytes 638984 | tf_op jit(solution)/shard_map/ppermute | solution.py:226
  69.4 19.3 %collective-permute-start.5 = (bf16[128,832]{1,0:T(8,128)(2,1)S(1)}, bf16[128,832]{1,0:T(8,128)(2,1)S(1)}, u32[]{:S(2)}, u32[]{:S(2)}) collective-permute-start(bf16[128,832]{1,0:T(8,128)(2,1)S(1)} %reshape.198.own_ref), channel_id=1, source_target_pairs={{0,256},{256,512},{512,0},{1,257},{257,513},{513,1},{2,258},{258,5... | collective-permute-start | bytes 638984 | tf_op jit(solution)/shard_map/ppermute | solution.py:227
  71.9 22.7 %collective-permute-start.8 = (bf16[384,1024]{1,0:T(8,128)(2,1)}, bf16[384,1024]{1,0:T(8,128)(2,1)S(1)}, u32[]{:S(2)}, u32[]{:S(2)}) collective-permute-start(bf16[384,1024]{1,0:T(8,128)(2,1)} %collective-permute-done.1.refs_1_), channel_id=1, source_target_pairs={{0,64},{64,128},{128,192},{192,0},{1,65},{65,129},{129,193},{193,1... | collective-permute-start | bytes 2359304 | tf_op jit(solution)/shard_map/ppermute | solution.py:206
  73.8 24.0 %collective-permute-start.9 = (bf16[448,1024]{1,0:T(8,128)(2,1)}, bf16[448,1024]{1,0:T(8,128)(2,1)S(1)}, u32[]{:S(2)}, u32[]{:S(2)}) collective-permute-start(bf16[448,1024]{1,0:T(8,128)(2,1)} %collective-permute-done.2.refs_4_), channel_id=1, source_target_pairs={{0,192},{64,0},{128,64},{192,128},{1,193},{65,1},{129,65},{193,129... | collective-permute-start | bytes 2752520 | tf_op jit(solution)/shard_map/ppermute | solution.py:209
  92.6 10.1 %collective-permute-start.6 = (bf16[2,192,1024]{2,1,0:T(8,128)(2,1)S(1)}, bf16[2,192,1024]{2,1,0:T(8,128)(2,1)S(1)}, u32[]{:S(2)}, u32[]{:S(2)}) collective-permute-start(bf16[2,192,1024]{2,1,0:T(8,128)(2,1)S(1)} %get-tuple-element.24), channel_id=1, source_target_pairs={{0,1},{1,0},{2,3},{3,2},{4,5},{5,4},{6,7},{7,6},{8,9},{9,8},{10,11... | collective-permute-start | bytes 2359304 | tf_op jit(solution)/shard_map/ppermute | solution.py:237
  100.8 5.2 %collective-permute-start.10 = (bf16[2,192,1024]{2,1,0:T(8,128)(2,1)S(1)}, bf16[2,192,1024]{2,1,0:T(8,128)(2,1)S(1)}, u32[]{:S(2)}, u32[]{:S(2)}) collective-permute-start(bf16[2,192,1024]{2,1,0:T(8,128)(2,1)S(1)} %get-tuple-element.28), channel_id=1, source_target_pairs={{0,1},{1,0},{2,3},{3,2},{4,5},{5,4},{6,7},{7,6},{8,9},{9,8},{10,11... | collective-permute-start | bytes 2359304 | tf_op jit(solution)/shard_map/ppermute | solution.py:237
  103.0 13.4 %collective-permute-start.7 = (bf16[2,96,1024]{2,1,0:T(8,128)(2,1)S(1)}, bf16[2,96,1024]{2,1,0:T(8,128)(2,1)S(1)}, u32[]{:S(2)}, u32[]{:S(2)}) collective-permute-start(bf16[2,96,1024]{2,1,0:T(8,128)(2,1)S(1)} %slice.70), channel_id=1, source_target_pairs={{0,2},{2,0},{4,6},{6,4},{8,10},{10,8},{12,14},{14,12},{1,3},{3,1},... | collective-permute-start | bytes 1179656 | tf_op jit(solution)/shard_map/ppermute | solution.py:239
  106.3 13.1 %collective-permute-start.11 = (bf16[2,96,1024]{2,1,0:T(8,128)(2,1)S(1)}, bf16[2,96,1024]{2,1,0:T(8,128)(2,1)S(1)}, u32[]{:S(2)}, u32[]{:S(2)}) collective-permute-start(bf16[2,96,1024]{2,1,0:T(8,128)(2,1)S(1)} %slice.69), channel_id=1, source_target_pairs={{0,14},{2,4},{4,2},{6,8},{8,6},{10,12},{12,10},{14,0},{1,15},{3,5}... | collective-permute-start | bytes 1179656 | tf_op jit(solution)/shard_map/ppermute | solution.py:239
  120.5 32.5 %all-to-all-start.2 = ((bf16[16,24,1024]{2,1,0:T(8,128)(2,1)}), bf16[16,24,1024]{2,1,0:T(8,128)(2,1)S(1)}, u32[]{:S(2)}, u32[]{:S(2)}) async-start(bf16[16,24,1024]{2,1,0:T(8,128)(2,1)} %bitcast), calls=%async_computation.2 | async-start | bytes 1572864 | tf_op jit(solution)/shard_map/all_to_all | solution.py:242
  153.1 13.3 %collective-permute-start.13 = (bf16[24,1024]{1,0:T(8,128)(2,1)S(1)}, bf16[24,1024]{1,0:T(8,128)(2,1)S(1)}, u32[]{:S(2)}, u32[]{:S(2)}) collective-permute-start(bf16[24,1024]{1,0:T(8,128)(2,1)S(1)} %reduce_sum.12), channel_id=1, source_target_pairs={{0,0},{1,1},{2,2},{3,3},{4,4},{5,21},{6,22},{7,23},{8,24},{9,25},{... | collective-permute-start | bytes 147464 | tf_op jit(solution)/shard_map/ppermute | solution.py:248
  156.6 9.8 %collective-permute-start.12 = (bf16[8,1024]{1,0:T(8,128)(2,1)S(1)}, bf16[8,1024]{1,0:T(8,128)(2,1)S(1)}, u32[]{:S(2)}, u32[]{:S(2)}) collective-permute-start(bf16[8,1024]{1,0:T(8,128)(2,1)S(1)} %slice_select_fusion.2), channel_id=1, source_target_pairs={{5,5},{10,42},{21,69},{26,106},{37,197},{42,234},{53,133},{58,170}... | collective-permute-start | bytes 49160 | tf_op jit(solution)/shard_map/ppermute | solution.py:249

commit v5 on v4

--- a/solution.py
+++ b/solution.py
@@ -87,7 +87,7 @@
         in_specs=[pl.BlockSpec(memory_space=pltpu.VMEM)] * 4,
         out_specs=pl.BlockSpec(memory_space=pltpu.VMEM),
         compiler_params=pltpu.CompilerParams(vmem_limit_bytes=24 * 1024 * 1024),
-        cost_estimate=pl.CostEstimate(flops=400_000_000, bytes_accessed=1_500_000, transcendentals=0),
+        cost_estimate=pl.CostEstimate(flops=40000000000, bytes_accessed=1_500_000, transcendentals=0),
     )(
         arrived,
         jnp.asarray(rows, jnp.bfloat16),
@@ -151,7 +151,7 @@
         in_specs=[pl.BlockSpec(memory_space=pltpu.VMEM)] * 4,
         out_specs=pl.BlockSpec(memory_space=pltpu.VMEM),
         compiler_params=pltpu.CompilerParams(vmem_limit_bytes=16 * 1024 * 1024),
-        cost_estimate=pl.CostEstimate(flops=20_000_000_000, bytes_accessed=1_500_000, transcendentals=0),
+        cost_estimate=pl.CostEstimate(flops=20000000000, bytes_accessed=1_500_000, transcendentals=0),
     )(source, own, next_1, next_2)
 
 
@@ -208,31 +208,26 @@
     def to_left(rows):
         return lax.ppermute(rows, "x", ring(4, -1))
 
-    top_0 = quantize_weight(down_weight[:SPLIT], weight_exponent)
-    top_1, top_3 = to_left(top_0), to_right(top_0)
     scaling = jnp.exp2(act_exponent.astype(jnp.float32)).astype(jnp.bfloat16)
     inverse = (1.0 / scaling.astype(jnp.float32)).astype(jnp.bfloat16)
     level = jnp.broadcast_to((7.5 - clip_index.astype(jnp.float32)).astype(jnp.bfloat16)[None, :], (128, 13))
     packed = jnp.concatenate([hidden, scaling, inverse, level, jnp.zeros((128, 25), jnp.bfloat16)], axis=1)
     packed, down_weight = lax.optimization_barrier((packed, down_weight))
-    low_0 = quantize_weight(down_weight[SPLIT:], weight_exponent)
+    weight_0 = quantize_weight(down_weight, weight_exponent)
+    weight_1, weight_3 = to_left(weight_0), to_right(weight_0)
     arrived = lax.all_to_all(packed.reshape(64, 2, WIDTH), TENSOR, split_axis=0, concat_axis=0, tiled=True)
-    arrived, top_1, top_3 = lax.optimization_barrier((arrived, top_1, top_3))
     quantized = rotate_and_quantize(arrived.reshape(128, WIDTH))
     returned = lax.all_to_all(quantized.reshape(64, 2, 832), TENSOR, split_axis=0, concat_axis=0, tiled=True)
-    low_1, low_3 = to_left(low_0), to_right(low_0)
-    returned, low_1, low_3 = lax.optimization_barrier((returned, low_1, low_3))
     own = returned.reshape(128, 832)
     next_1 = lax.ppermute(own, "h", ring(3, -1))
     next_2 = lax.ppermute(own, "h", ring(3, 1))
-    top_2, low_2 = to_right(top_3), to_left(low_1)
-    weight_0, weight_1, weight_2, weight_3 = (top_0, low_0), (top_1, low_1), (top_2, low_2), (top_3, low_3)
+    weight_2 = (to_right(weight_3[:SPLIT]), to_left(weight_1[SPLIT:]))
     acts = arrange(row_order(h, x, y_low, c), own, next_1, next_2)
 
     y_pairs_near = [(y, y ^ 1) for y in range(8)]
     y_pairs_far = [(y, (y - 1) % 8 if y % 2 == 0 else (y + 1) % 8) for y in range(8)]
     parts = []
-    for weights, y_pairs in (((weight_0, weight_1), y_pairs_near), ((weight_3, weight_2), y_pairs_far)):
+    for weights, y_pairs in ((((weight_0,), (weight_1,)), y_pairs_near), (((weight_3,), weight_2), y_pairs_far)):
         other, own_rows = products(acts, weights)
         from_core = lax.ppermute(other, "c", [(0, 1), (1, 0)])
         mine = own_rows + from_core.astype(jnp.float32)

time: 168 us -> 167 us (level)
  the two profiles are of different devices: /device:TPU:40 before, /device:TPU:21 now
where the time goes in v5:
time: 167 us; the launch traced here: 166 us
  starting transfers between devices  71.6 us (43%)
  waiting for transfers between devices  48.4 us (29%)
  blocking collectives  19.5 us (12%)
  local copies, waits for them, and re-layouts  11.8 us (7%)
  Pallas kernels  7.53 us (5%)
  other arithmetic  7.06 us (4%)
    all_to_all x1, blocking collectives, shards(): lax.all_to_all(quantized.reshape(64, 2, 832), TENSOR, split_axis=0, conca...  19.5 us
    all_to_all x1, waiting for transfers between devices, shards(): lax.all_to_all(sums, ('l', 'yh'), split_axis=0, concat_axis=0, tiled=True)  18.1 us
    all_to_all x1, starting transfers between devices, shards(): lax.all_to_all(packed.reshape(64, 2, WIDTH), TENSOR, split_axis=0, concat...  13.9 us
    all_to_all x1, starting transfers between devices, shards(): lax.all_to_all(sums, ('l', 'yh'), split_axis=0, concat_axis=0, tiled=True)  12.5 us
    ppermute x1, starting transfers between devices, shards(): next_1 = lax.ppermute(own, 'h', ring(3, -1))  11.6 us
    ppermute x2, waiting for transfers between devices, shards(): lax.ppermute(mine[:, :96].astype(jnp.bfloat16), ('yh', 'yl'), y_pairs)  10.2 us
    ppermute x1, waiting for transfers between devices, shards(): next_1 = lax.ppermute(own, 'h', ring(3, -1))  9.98 us
    ppermute x1, starting transfers between devices, shards(): lax.ppermute(total, ('x', 'l', 'yh', 'yl', 'c'), final_pairs('main'))  8.13 us
  transfers between devices with their start and end apart: 14, of which 8 were waited for; matrix products, arithmetic and copies ran while one was open for 6% of the time, Pallas kernels for 5%

profile of v5, /device:TPU:21, one launch (start us, length us, event | category | flops | bytes accessed | tf_op | source)
XLA Modules:
  0.0 166.2 jit_solution(11535878924340649511)
XLA Ops:
  0.0 0.8 divide_convert_fusion
  0.9 0.7 subtract_convert_fusion
  1.6 1.4 concatenate.9
  3.0 0.2 copy.13
  3.2 0.8 reshape.195
  3.9 13.9 %all-to-all-start = ((bf16[64,2,896]{2,1,0:T(2,128)(2,1)}), bf16[64,2,896]{2,1,0:T(2,128)(2,1)}, u32[]{:S(2)}, u32[]{:S(2)}) async-start(bf16[64,2,896]{2,1,0:T(2,128)(2,1)} %reshape.195), calls=%async_computation | async-start | bytes 458752 | tf_op jit(solution)/shard_map/all_to_all | solution.py:218
  17.9 2.7 %multiply_convert_fusion.refs_1_ = bf16[832,1024]{1,0:T(8,128)(2,1)S(1)} fusion(bf16[832,1024]{1,0:T(8,128)(2,1)S(1)} %copy-done.6, f32[1024]{0:T(1024)S(1)} %fusion.25), kind=kLoop, calls=%fused_computation.1 | loop fusion | flops 20447232 | bytes 3411968 | tf_op jit(solution)/shard_map/convert_element_type | solution.py:161
  20.6 2.2 %collective-permute-start.2 = (bf16[832,1024]{1,0:T(8,128)(2,1)S(1)}, bf16[832,1024]{1,0:T(8,128)(2,1)S(1)}, u32[]{:S(2)}, u32[]{:S(2)}) collective-permute-start(bf16[832,1024]{1,0:T(8,128)(2,1)S(1)} %multiply_convert_fusion.refs_1_), channel_id=1, source_target_pairs={{0,192},{64,0},{128,64},{192,128},{1,193},{65,1},{129,65},{193,129... | collective-permute-start | bytes 5111816 | tf_op jit(solution)/shard_map/ppermute | solution.py:209
  22.7 3.1 %collective-permute-start.5 = (bf16[832,1024]{1,0:T(8,128)(2,1)S(1)}, bf16[832,1024]{1,0:T(8,128)(2,1)}, u32[]{:S(2)}, u32[]{:S(2)}) collective-permute-start(bf16[832,1024]{1,0:T(8,128)(2,1)S(1)} %multiply_convert_fusion.refs_1_), channel_id=1, source_target_pairs={{0,64},{64,128},{128,192},{192,0},{1,65},{65,129},{129,193},{193,1... | collective-permute-start | bytes 5111816 | tf_op jit(solution)/shard_map/ppermute | solution.py:206
  25.9 2.5 %all-to-all-done = bf16[64,2,896]{2,1,0:T(2,128)(2,1)} async-done(((bf16[64,2,896]{2,1,0:T(2,128)(2,1)}), bf16[64,2,896]{2,1,0:T(2,128)(2,1)}, u32[]{:S(2)}, u32[]{:S(2)}) %all-to-all-start) | async-done | bytes 229408 | tf_op jit(solution)/shard_map/all_to_all | solution.py:218
  28.4 1.7 %reshape.196.x_ref = bf16[128,896]{1,0:T(8,128)(2,1)} reshape(bf16[64,2,896]{2,1,0:T(2,128)(2,1)} %all-to-all-done) | data formatting | bytes 458752 | tf_op jit(solution)/shard_map/reshape | solution.py:219
  30.1 0.9 copy-done.1
  31.0 1.1 copy-done.3
  32.1 0.7 shard_map.82
  32.9 0.7 copy-done.2
  33.5 1.7 %reshape.197 = bf16[64,2,832]{2,1,0:T(2,128)(2,1)} reshape(bf16[128,832]{1,0:T(8,128)(2,1)} %copy-done.2) | data formatting | bytes 425984 | tf_op jit(solution)/shard_map/reshape | solution.py:220
  35.3 19.5 %all_to_all.15 = bf16[64,2,832]{2,1,0:T(2,128)(2,1)} all-to-all(bf16[64,2,832]{2,1,0:T(2,128)(2,1)} %reshape.197), channel_id=1, replica_groups=mesh['h'=3,'x'=4,'l'=4,'yh'=4,'yl'=2,'c'=2] {'l','yh','yl','c'}, dimensions={0} | all-to-all | bytes 425984 | tf_op jit(solution)/shard_map/all_to_all | solution.py:220
  54.8 1.8 %reshape.198.own_ref = bf16[128,832]{1,0:T(8,128)(2,1)} reshape(bf16[64,2,832]{2,1,0:T(2,128)(2,1)} %all_to_all.15) | data formatting | bytes 425984 | tf_op jit(solution)/shard_map/reshape | solution.py:221
  56.6 11.6 %collective-permute-start = (bf16[128,832]{1,0:T(8,128)(2,1)}, bf16[128,832]{1,0:T(8,128)(2,1)}, u32[]{:S(2)}, u32[]{:S(2)}) collective-permute-start(bf16[128,832]{1,0:T(8,128)(2,1)} %reshape.198.own_ref), channel_id=1, source_target_pairs={{0,512},{256,0},{512,256},{1,513},{257,1},{513,257},{2,514},{258,2... | collective-permute-start | bytes 638984 | tf_op jit(solution)/shard_map/ppermute | solution.py:222
  68.2 1.9 %collective-permute-start.1 = (bf16[128,832]{1,0:T(8,128)(2,1)}, bf16[128,832]{1,0:T(8,128)(2,1)}, u32[]{:S(2)}, u32[]{:S(2)}) collective-permute-start(bf16[128,832]{1,0:T(8,128)(2,1)} %reshape.198.own_ref), channel_id=1, source_target_pairs={{0,256},{256,512},{512,0},{1,257},{257,513},{513,1},{2,258},{258,5... | collective-permute-start | bytes 638984 | tf_op jit(solution)/shard_map/ppermute | solution.py:223
  70.1 0.5 add_select_fusion.source_ref
  70.8 2.3 %collective-permute-start.7 = (bf16[448,1024]{1,0:T(8,128)(2,1)S(1)}, bf16[448,1024]{1,0:T(8,128)(2,1)S(1)}, u32[]{:S(2)}, u32[]{:S(2)}) collective-permute-start(bf16[448,1024]{1,0:T(8,128)(2,1)S(1)} %slice.49), channel_id=1, source_target_pairs={{0,192},{64,0},{128,64},{192,128},{1,193},{65,1},{129,65},{193,129... | collective-permute-start | bytes 2752520 | tf_op jit(solution)/shard_map/ppermute | solution.py:209
  73.1 1.2 slice.48
  74.3 3.8 %collective-permute-start.6 = (bf16[384,1024]{1,0:T(8,128)(2,1)S(1)}, bf16[384,1024]{1,0:T(8,128)(2,1)S(1)}, u32[]{:S(2)}, u32[]{:S(2)}) collective-permute-start(bf16[384,1024]{1,0:T(8,128)(2,1)S(1)} %slice.48), channel_id=1, source_target_pairs={{0,64},{64,128},{128,192},{192,0},{1,65},{65,129},{129,193},{193,1... | collective-permute-start | bytes 2359304 | tf_op jit(solution)/shard_map/ppermute | solution.py:206
  78.1 10.0 %collective-permute-done.next_1_ref = bf16[128,832]{1,0:T(8,128)(2,1)} collective-permute-done((bf16[128,832]{1,0:T(8,128)(2,1)}, bf16[128,832]{1,0:T(8,128)(2,1)}, u32[]{:S(2)}, u32[]{:S(2)}) %collective-permute-start) | collective-permute-done | bytes 213024 | tf_op jit(solution)/shard_map/ppermute | solution.py:222
  88.0 0.3 collective-permute-done.1.next_2_ref
  88.3 1.8 %shard_map.83.refs_0_ = bf16[384,832]{1,0:T(8,128)(2,1)S(1)} custom-call(s32[384,1]{1,0:T(8,128)S(1)} %add_select_fusion.source_ref, bf16[128,832]{1,0:T(8,128)(2,1)S(1)} %copy-done, bf16[128,832]{1,0:T(8,128)(2,1)} %collective-permute-done.next_1_ref, bf16[128,832]{1,0:T(8,128)(2,1)} %collective-permute-done.1.next_2_ref), custom_call_target="tpu_custom_call" | custom-call | flops 20000000000 | bytes 1500000 | tf_op jit(solution)/shard_map/pallas_call | solution.py:148
  90.1 1.8 %shard_map.84 = (bf16[2,192,1024]{2,1,0:T(8,128)(2,1)S(1)}, f32[2,192,1024]{2,1,0:T(8,128)S(1)}) custom-call(bf16[384,832]{1,0:T(8,128)(2,1)S(1)} %shard_map.83.refs_0_, bf16[832,1024]{1,0:T(8,128)(2,1)S(1)} %multiply_convert_fusion.refs_1_, bf16[832,1024]{1,0:T(8,128)(2,1)S(1)} %collective-permute-done.2.refs_2_), custom_call_target="tpu_custom_call" | custom-call | flops 1300000000 | bytes 6000000 | tf_op jit(solution)/shard_map/pallas_call | solution.py:123
  91.9 2.4 %collective-permute-start.3 = (bf16[2,192,1024]{2,1,0:T(8,128)(2,1)S(1)}, bf16[2,192,1024]{2,1,0:T(8,128)(2,1)S(1)}, u32[]{:S(2)}, u32[]{:S(2)}) collective-permute-start(bf16[2,192,1024]{2,1,0:T(8,128)(2,1)S(1)} %get-tuple-element.14), channel_id=1, source_target_pairs={{0,1},{1,0},{2,3},{3,2},{4,5},{5,4},{6,7},{7,6},{8,9},{9,8},{10,11... | collective-permute-start | bytes 2359304 | tf_op jit(solution)/shard_map/ppermute | solution.py:232
  94.4 0.6 collective-permute-done.7.refs_3_
  95.0 3.2 %shard_map.85 = (bf16[2,192,1024]{2,1,0:T(8,128)(2,1)S(1)}, f32[2,192,1024]{2,1,0:T(8,128)S(1)}) custom-call(bf16[384,832]{1,0:T(8,128)(2,1)S(1)} %shard_map.83.refs_0_, bf16[832,1024]{1,0:T(8,128)(2,1)} %collective-permute-done.5.refs_1_, bf16[384,1024]{1,0:T(8,128)(2,1)S(1)} %collective-permute-done.6.refs_2_, ...), custom_call_target="tpu_custom_call" | custom-call | flops 1300000000 | bytes 6000000 | tf_op jit(solution)/shard_map/pallas_call | solution.py:123
  98.2 3.1 %collective-permute-start.8 = (bf16[2,192,1024]{2,1,0:T(8,128)(2,1)S(1)}, bf16[2,192,1024]{2,1,0:T(8,128)(2,1)S(1)}, u32[]{:S(2)}, u32[]{:S(2)}) collective-permute-start(bf16[2,192,1024]{2,1,0:T(8,128)(2,1)S(1)} %get-tuple-element.16), channel_id=1, source_target_pairs={{0,1},{1,0},{2,3},{3,2},{4,5},{5,4},{6,7},{7,6},{8,9},{9,8},{10,11... | collective-permute-start | bytes 2359304 | tf_op jit(solution)/shard_map/ppermute | solution.py:232
  101.4 0.2 convert_add_fusion.1
  101.7 2.7 %collective-permute-start.4 = (bf16[2,96,1024]{2,1,0:T(8,128)(2,1)S(1)}, bf16[2,96,1024]{2,1,0:T(8,128)(2,1)S(1)}, u32[]{:S(2)}, u32[]{:S(2)}) collective-permute-start(bf16[2,96,1024]{2,1,0:T(8,128)(2,1)S(1)} %slice.70), channel_id=1, source_target_pairs={{0,2},{2,0},{4,6},{6,4},{8,10},{10,8},{12,14},{14,12},{1,3},{3,1},... | collective-permute-start | bytes 1179656 | tf_op jit(solution)/shard_map/ppermute | solution.py:234
  104.4 0.2 convert_add_fusion
  104.7 2.0 %collective-permute-start.9 = (bf16[2,96,1024]{2,1,0:T(8,128)(2,1)S(1)}, bf16[2,96,1024]{2,1,0:T(8,128)(2,1)S(1)}, u32[]{:S(2)}, u32[]{:S(2)}) collective-permute-start(bf16[2,96,1024]{2,1,0:T(8,128)(2,1)S(1)} %slice.69), channel_id=1, source_target_pairs={{0,14},{2,4},{4,2},{6,8},{8,6},{10,12},{12,10},{14,0},{1,15},{3,5}... | collective-permute-start | bytes 1179656 | tf_op jit(solution)/shard_map/ppermute | solution.py:234
  106.7 7.6 %collective-permute-done.4 = bf16[2,96,1024]{2,1,0:T(8,128)(2,1)S(1)} collective-permute-done((bf16[2,96,1024]{2,1,0:T(8,128)(2,1)S(1)}, bf16[2,96,1024]{2,1,0:T(8,128)(2,1)S(1)}, u32[]{:S(2)}, u32[]{:S(2)}) %collective-permute-start.4) | collective-permute-done | bytes 393248 | tf_op jit(solution)/shard_map/ppermute | solution.py:234
  114.3 0.1 fusion.6
  114.4 2.6 %collective-permute-done.9 = bf16[2,96,1024]{2,1,0:T(8,128)(2,1)S(1)} collective-permute-done((bf16[2,96,1024]{2,1,0:T(8,128)(2,1)S(1)}, bf16[2,96,1024]{2,1,0:T(8,128)(2,1)S(1)}, u32[]{:S(2)}, u32[]{:S(2)}) %collective-permute-start.9) | collective-permute-done | bytes 393248 | tf_op jit(solution)/shard_map/ppermute | solution.py:234
  117.0 0.1 fusion.5
  117.1 0.9 pad_maximum_fusion
  118.0 12.5 %all-to-all-start.2 = ((bf16[16,24,1024]{2,1,0:T(8,128)(2,1)}), bf16[16,24,1024]{2,1,0:T(8,128)(2,1)S(1)}, u32[]{:S(2)}, u32[]{:S(2)}) async-start(bf16[16,24,1024]{2,1,0:T(8,128)(2,1)} %bitcast), calls=%async_computation.2 | async-start | bytes 1572864 | tf_op jit(solution)/shard_map/all_to_all | solution.py:237
  130.5 18.1 %all-to-all-done.2 = bf16[16,24,1024]{2,1,0:T(8,128)(2,1)S(1)} async-done(((bf16[16,24,1024]{2,1,0:T(8,128)(2,1)}), bf16[16,24,1024]{2,1,0:T(8,128)(2,1)S(1)}, u32[]{:S(2)}, u32[]{:S(2)}) %all-to-all-start.2) | async-done | bytes 786464 | tf_op jit(solution)/shard_map/all_to_all | solution.py:237
  148.6 0.1 reduce_sum.12
  148.7 8.1 %collective-permute-start.11 = (bf16[24,1024]{1,0:T(8,128)(2,1)S(1)}, bf16[24,1024]{1,0:T(8,128)(2,1)S(1)}, u32[]{:S(2)}, u32[]{:S(2)}) collective-permute-start(bf16[24,1024]{1,0:T(8,128)(2,1)S(1)} %reduce_sum.12), channel_id=1, source_target_pairs={{0,0},{1,1},{2,2},{3,3},{4,4},{5,21},{6,22},{7,23},{8,24},{9,25},{... | collective-permute-start | bytes 147464 | tf_op jit(solution)/shard_map/ppermute | solution.py:243
  156.9 1.9 %collective-permute-start.10 = (bf16[8,1024]{1,0:T(8,128)(2,1)S(1)}, bf16[8,1024]{1,0:T(8,128)(2,1)S(1)}, u32[]{:S(2)}, u32[]{:S(2)}) collective-permute-start(bf16[8,1024]{1,0:T(8,128)(2,1)S(1)} %slice_select_fusion.2), channel_id=1, source_target_pairs={{5,5},{10,42},{21,69},{26,106},{37,197},{42,234},{53,133},{58,170}... | collective-permute-start | bytes 49160 | tf_op jit(solution)/shard_map/ppermute | solution.py:244
  158.8 6.7 %collective-permute-done.10 = bf16[8,1024]{1,0:T(8,128)(2,1)S(1)} collective-permute-done((bf16[8,1024]{1,0:T(8,128)(2,1)S(1)}, bf16[8,1024]{1,0:T(8,128)(2,1)S(1)}, u32[]{:S(2)}, u32[]{:S(2)}) %collective-permute-start.10) | collective-permute-done | bytes 16416 | tf_op jit(solution)/shard_map/ppermute | solution.py:244
  165.6 0.6 pad_maximum_fusion.1
  (27 shorter events, 0.3 us)
Async XLA Ops:
  0.0 17.9 %copy-start.6 = (bf16[832,1024]{1,0:T(8,128)(2,1)S(1)}, bf16[832,1024]{1,0:T(8,128)(2,1)}, u32[]{:S(2)}) copy-start(bf16[832,1024]{1,0:T(8,128)(2,1)} %param.9) | copy-start | bytes 5111812
  0.0 17.8 %copy-start.7 = (s32[1024]{0:T(1024)S(1)}, s32[1024]{0:T(1024)}, u32[]{:S(2)}) copy-start(s32[1024]{0:T(1024)} %param.12) | copy-start | bytes 12292
  3.9 24.4 %all-to-all-start = ((bf16[64,2,896]{2,1,0:T(2,128)(2,1)}), bf16[64,2,896]{2,1,0:T(2,128)(2,1)}, u32[]{:S(2)}, u32[]{:S(2)}) async-start(bf16[64,2,896]{2,1,0:T(2,128)(2,1)} %reshape.195), calls=%async_computation | async-start | bytes 458752 | tf_op jit(solution)/shard_map/all_to_all | solution.py:218
  17.9 12.2 %copy-start.4 = (bf16[128,128]{1,0:T(8,128)(2,1)S(1)}, bf16[128,128]{1,0:T(8,128)(2,1)}, u32[]{:S(2)}) copy-start(bf16[128,128]{1,0:T(8,128)(2,1)} %constant.120.clone.rows_ref) | copy-start | bytes 98308
  17.9 12.2 %copy-start.5 = (bf16[128,128]{1,0:T(8,128)(2,1)S(1)}, bf16[128,128]{1,0:T(8,128)(2,1)}, u32[]{:S(2)}) copy-start(bf16[128,128]{1,0:T(8,128)(2,1)} %constant.121.clone.lanes_ref) | copy-start | bytes 98308
  20.6 50.1 %collective-permute-start.2 = (bf16[832,1024]{1,0:T(8,128)(2,1)S(1)}, bf16[832,1024]{1,0:T(8,128)(2,1)S(1)}, u32[]{:S(2)}, u32[]{:S(2)}) collective-permute-start(bf16[832,1024]{1,0:T(8,128)(2,1)S(1)} %multiply_convert_fusion.refs_1_), channel_id=1, source_target_pairs={{0,192},{64,0},{128,64},{192,128},{1,193},{65,1},{129,65},{193,129... | collective-permute-start | bytes 5111816 | tf_op jit(solution)/shard_map/ppermute | solution.py:209
  22.7 50.3 %collective-permute-start.5 = (bf16[832,1024]{1,0:T(8,128)(2,1)S(1)}, bf16[832,1024]{1,0:T(8,128)(2,1)}, u32[]{:S(2)}, u32[]{:S(2)}) collective-permute-start(bf16[832,1024]{1,0:T(8,128)(2,1)S(1)} %multiply_convert_fusion.refs_1_), channel_id=1, source_target_pairs={{0,64},{64,128},{128,192},{192,0},{1,65},{65,129},{129,193},{193,1... | collective-permute-start | bytes 5111816 | tf_op jit(solution)/shard_map/ppermute | solution.py:206
  30.1 0.9 copy-start.1
  31.0 1.1 copy-start.3
  32.9 0.7 copy-start.2
  56.6 31.4 %collective-permute-start = (bf16[128,832]{1,0:T(8,128)(2,1)}, bf16[128,832]{1,0:T(8,128)(2,1)}, u32[]{:S(2)}, u32[]{:S(2)}) collective-permute-start(bf16[128,832]{1,0:T(8,128)(2,1)} %reshape.198.own_ref), channel_id=1, source_target_pairs={{0,512},{256,0},{512,256},{1,513},{257,1},{513,257},{2,514},{258,2... | collective-permute-start | bytes 638984 | tf_op jit(solution)/shard_map/ppermute | solution.py:222
  68.2 20.1 %collective-permute-start.1 = (bf16[128,832]{1,0:T(8,128)(2,1)}, bf16[128,832]{1,0:T(8,128)(2,1)}, u32[]{:S(2)}, u32[]{:S(2)}) collective-permute-start(bf16[128,832]{1,0:T(8,128)(2,1)} %reshape.198.own_ref), channel_id=1, source_target_pairs={{0,256},{256,512},{512,0},{1,257},{257,513},{513,1},{2,258},{258,5... | collective-permute-start | bytes 638984 | tf_op jit(solution)/shard_map/ppermute | solution.py:223
  70.7 17.7 %copy-start = (bf16[128,832]{1,0:T(8,128)(2,1)S(1)}, bf16[128,832]{1,0:T(8,128)(2,1)}, u32[]{:S(2)}) copy-start(bf16[128,832]{1,0:T(8,128)(2,1)} %reshape.198.own_ref) | copy-start | bytes 638980
  70.8 24.2 %collective-permute-start.7 = (bf16[448,1024]{1,0:T(8,128)(2,1)S(1)}, bf16[448,1024]{1,0:T(8,128)(2,1)S(1)}, u32[]{:S(2)}, u32[]{:S(2)}) collective-permute-start(bf16[448,1024]{1,0:T(8,128)(2,1)S(1)} %slice.49), channel_id=1, source_target_pairs={{0,192},{64,0},{128,64},{192,128},{1,193},{65,1},{129,65},{193,129... | collective-permute-start | bytes 2752520 | tf_op jit(solution)/shard_map/ppermute | solution.py:209
  74.3 20.1 %collective-permute-start.6 = (bf16[384,1024]{1,0:T(8,128)(2,1)S(1)}, bf16[384,1024]{1,0:T(8,128)(2,1)S(1)}, u32[]{:S(2)}, u32[]{:S(2)}) collective-permute-start(bf16[384,1024]{1,0:T(8,128)(2,1)S(1)} %slice.48), channel_id=1, source_target_pairs={{0,64},{64,128},{128,192},{192,0},{1,65},{65,129},{129,193},{193,1... | collective-permute-start | bytes 2359304 | tf_op jit(solution)/shard_map/ppermute | solution.py:206
  91.9 9.5 %collective-permute-start.3 = (bf16[2,192,1024]{2,1,0:T(8,128)(2,1)S(1)}, bf16[2,192,1024]{2,1,0:T(8,128)(2,1)S(1)}, u32[]{:S(2)}, u32[]{:S(2)}) collective-permute-start(bf16[2,192,1024]{2,1,0:T(8,128)(2,1)S(1)} %get-tuple-element.14), channel_id=1, source_target_pairs={{0,1},{1,0},{2,3},{3,2},{4,5},{5,4},{6,7},{7,6},{8,9},{9,8},{10,11... | collective-permute-start | bytes 2359304 | tf_op jit(solution)/shard_map/ppermute | solution.py:232
  98.2 6.1 %collective-permute-start.8 = (bf16[2,192,1024]{2,1,0:T(8,128)(2,1)S(1)}, bf16[2,192,1024]{2,1,0:T(8,128)(2,1)S(1)}, u32[]{:S(2)}, u32[]{:S(2)}) collective-permute-start(bf16[2,192,1024]{2,1,0:T(8,128)(2,1)S(1)} %get-tuple-element.16), channel_id=1, source_target_pairs={{0,1},{1,0},{2,3},{3,2},{4,5},{5,4},{6,7},{7,6},{8,9},{9,8},{10,11... | collective-permute-start | bytes 2359304 | tf_op jit(solution)/shard_map/ppermute | solution.py:232
  101.7 12.6 %collective-permute-start.4 = (bf16[2,96,1024]{2,1,0:T(8,128)(2,1)S(1)}, bf16[2,96,1024]{2,1,0:T(8,128)(2,1)S(1)}, u32[]{:S(2)}, u32[]{:S(2)}) collective-permute-start(bf16[2,96,1024]{2,1,0:T(8,128)(2,1)S(1)} %slice.70), channel_id=1, source_target_pairs={{0,2},{2,0},{4,6},{6,4},{8,10},{10,8},{12,14},{14,12},{1,3},{3,1},... | collective-permute-start | bytes 1179656 | tf_op jit(solution)/shard_map/ppermute | solution.py:234
  104.7 12.3 %collective-permute-start.9 = (bf16[2,96,1024]{2,1,0:T(8,128)(2,1)S(1)}, bf16[2,96,1024]{2,1,0:T(8,128)(2,1)S(1)}, u32[]{:S(2)}, u32[]{:S(2)}) collective-permute-start(bf16[2,96,1024]{2,1,0:T(8,128)(2,1)S(1)} %slice.69), channel_id=1, source_target_pairs={{0,14},{2,4},{4,2},{6,8},{8,6},{10,12},{12,10},{14,0},{1,15},{3,5}... | collective-permute-start | bytes 1179656 | tf_op jit(solution)/shard_map/ppermute | solution.py:234
  118.0 30.6 %all-to-all-start.2 = ((bf16[16,24,1024]{2,1,0:T(8,128)(2,1)}), bf16[16,24,1024]{2,1,0:T(8,128)(2,1)S(1)}, u32[]{:S(2)}, u32[]{:S(2)}) async-start(bf16[16,24,1024]{2,1,0:T(8,128)(2,1)} %bitcast), calls=%async_computation.2 | async-start | bytes 1572864 | tf_op jit(solution)/shard_map/all_to_all | solution.py:237
  148.7 16.8 %collective-permute-start.11 = (bf16[24,1024]{1,0:T(8,128)(2,1)S(1)}, bf16[24,1024]{1,0:T(8,128)(2,1)S(1)}, u32[]{:S(2)}, u32[]{:S(2)}) collective-permute-start(bf16[24,1024]{1,0:T(8,128)(2,1)S(1)} %reduce_sum.12), channel_id=1, source_target_pairs={{0,0},{1,1},{2,2},{3,3},{4,4},{5,21},{6,22},{7,23},{8,24},{9,25},{... | collective-permute-start | bytes 147464 | tf_op jit(solution)/shard_map/ppermute | solution.py:243
  156.9 8.7 %collective-permute-start.10 = (bf16[8,1024]{1,0:T(8,128)(2,1)S(1)}, bf16[8,1024]{1,0:T(8,128)(2,1)S(1)}, u32[]{:S(2)}, u32[]{:S(2)}) collective-permute-start(bf16[8,1024]{1,0:T(8,128)(2,1)S(1)} %slice_select_fusion.2), channel_id=1, source_target_pairs={{5,5},{10,42},{21,69},{26,106},{37,197},{42,234},{53,133},{58,170}... | collective-permute-start | bytes 49160 | tf_op jit(solution)/shard_map/ppermute | solution.py:244

commit v6 on v5

--- a/solution.py
+++ b/solution.py
@@ -46,54 +46,86 @@
     return (1 - 2 * parity).astype(np.float32)
 
 
-def rotate_kernel(x_ref, rows_ref, lanes_ref, spread_ref, out_ref):
-    arrived = x_ref[...]
-    mixed = jnp.dot(rows_ref[...], arrived, preferred_element_type=jnp.float32)
-    extra = arrived[:, 768:896]
-    lanes = lanes_ref[...]
-    for piece in range(7):
-        width = 128 if piece < 6 else 64
-        rest = mixed[:, piece * 128 : piece * 128 + 128]
-        rotated = None
-        for _ in range(3):
-            part = rest.astype(jnp.bfloat16)
-            rest = rest - part.astype(jnp.float32)
-            term = jnp.dot(part, lanes, preferred_element_type=jnp.float32)
-            rotated = term if rotated is None else rotated + term
-        scale, inverse, level = (
-            jnp.dot(
-                extra,
-                spread_ref[kind, :, piece * 128 : piece * 128 + 128],
-                preferred_element_type=jnp.float32,
+def dot(left, right):
+    return jnp.dot(left, right, preferred_element_type=jnp.float32)
+
+
+def dot_transposed(left, right):
+    return lax.dot_general(left, right, (((1,), (1,)), ((), ())), preferred_element_type=jnp.float32)
+
+
+def ones_where(condition):
+    return jnp.where(condition, 1.0, 0.0).astype(jnp.bfloat16)
+
+
+def pack_kernel(hidden_ref, exponent_ref, index_ref, out_ref):
+    scaling = jnp.exp2(exponent_ref[...].astype(jnp.float32)).astype(jnp.bfloat16)
+    inverse = (1.0 / scaling.astype(jnp.float32)).astype(jnp.bfloat16)
+    level = 7.5 - index_ref[...].astype(jnp.float32)
+    lane = lax.broadcasted_iota(jnp.int32, (128, 64), 0)
+    tail = dot(ones_where(lane == lax.broadcasted_iota(jnp.int32, (128, 64), 1)), hidden_ref[768:])
+    lane = lax.broadcasted_iota(jnp.int32, (128, 13), 0)
+    group = lax.broadcasted_iota(jnp.int32, (128, 13), 1)
+    for kind, extra in enumerate((scaling, inverse)):
+        tail += dot(ones_where(lane == group + (64 + 13 * kind)), extra)
+    tail += jnp.sum(jnp.where(lane == group + 90, level, 0.0), axis=1, keepdims=True)
+    tail = tail.astype(jnp.bfloat16)
+    target = lax.broadcasted_iota(jnp.int32, (64, 128), 0)
+    token = lax.broadcasted_iota(jnp.int32, (64, 128), 1)
+    for which in range(2):
+        chosen = ones_where(token == 2 * target + which)
+        out_ref[:, which, :768] = dot_transposed(chosen, hidden_ref[:768]).astype(jnp.bfloat16)
+        out_ref[:, which, 768:] = dot_transposed(chosen, tail).astype(jnp.bfloat16)
+
+
+def pack(hidden, act_exponent, clip_index):
+    return pl.pallas_call(
+        pack_kernel,
+        out_shape=jax.ShapeDtypeStruct((64, 2, WIDTH), jnp.bfloat16),
+        in_specs=[pl.BlockSpec(memory_space=pltpu.VMEM)] * 3,
+        out_specs=pl.BlockSpec(memory_space=pltpu.VMEM),
+        compiler_params=pltpu.CompilerParams(vmem_limit_bytes=16 * 1024 * 1024),
+        cost_estimate=pl.CostEstimate(flops=40_000_000, bytes_accessed=500_000, transcendentals=0),
+    )(hidden.T, act_exponent.T, clip_index.reshape(1, 13))
+
+
+def rotate_kernel(x_ref, rows_ref, lanes_ref, out_ref):
+    lanes, rows = lanes_ref[...], rows_ref[...]
+    row = lax.broadcasted_iota(jnp.int32, (128, 128), 0)
+    upper = jnp.where(lax.broadcasted_iota(jnp.int32, (128, 128), 1) >= 64, 1, 0)
+    place = row - upper
+    for which in range(2):
+        arrived = x_ref[:, which, :]
+        mixed = dot(rows, arrived)
+        extra = arrived[:, 768:896]
+        for piece in range(7):
+            width = 128 if piece < 6 else 64
+            rest = mixed[:, piece * 128 : piece * 128 + 128]
+            rotated = None
+            for _ in range(3):
+                part = rest.astype(jnp.bfloat16)
+                rest = rest - part.astype(jnp.float32)
+                term = dot(part, lanes)
+                rotated = term if rotated is None else rotated + term
+            scale, inverse, level = (
+                dot(extra, ones_where(place == 64 + 13 * kind + 2 * piece)) for kind in range(3)
             )
-            for kind in range(3)
-        )
-        scaled = rotated * (1.0 / 64.0) * inverse
-        clipped = jnp.maximum(jnp.minimum(scaled, level), -level)
-        quantized = (soft_round(clipped) * scale).astype(jnp.bfloat16)
-        out_ref[:, piece * 128 : piece * 128 + width] = quantized[:, :width]
+            scaled = rotated * (1.0 / 64.0) * inverse
+            clipped = jnp.maximum(jnp.minimum(scaled, level), -level)
+            quantized = (soft_round(clipped) * scale).astype(jnp.bfloat16)
+            out_ref[:, which, piece * 128 : piece * 128 + width] = quantized[:, :width]
 
 
 def rotate_and_quantize(arrived):
-    rows = np.kron(walsh(64), np.eye(2, dtype=np.float32))
     lanes = np.kron(np.eye(2, dtype=np.float32), walsh(64))
-    spread = np.zeros((3, 128, WIDTH), np.float32)
-    for kind in range(3):
-        for group in range(13):
-            spread[kind, 64 + 13 * kind + group, 64 * group : 64 * group + 64] = 1.0
     return pl.pallas_call(
         rotate_kernel,
-        out_shape=jax.ShapeDtypeStruct((128, 832), jnp.bfloat16),
-        in_specs=[pl.BlockSpec(memory_space=pltpu.VMEM)] * 4,
+        out_shape=jax.ShapeDtypeStruct((64, 2, 832), jnp.bfloat16),
+        in_specs=[pl.BlockSpec(memory_space=pltpu.VMEM)] * 3,
         out_specs=pl.BlockSpec(memory_space=pltpu.VMEM),
         compiler_params=pltpu.CompilerParams(vmem_limit_bytes=24 * 1024 * 1024),
-        cost_estimate=pl.CostEstimate(flops=40000000000, bytes_accessed=1_500_000, transcendentals=0),
-    )(
-        arrived,
-        jnp.asarray(rows, jnp.bfloat16),
-        jnp.asarray(lanes, jnp.bfloat16),
-        jnp.asarray(spread, jnp.bfloat16),
-    )
+        cost_estimate=pl.CostEstimate(flops=40_000_000_000, bytes_accessed=1_500_000, transcendentals=0),
+    )(arrived, jnp.asarray(walsh(64), jnp.bfloat16), jnp.asarray(lanes, jnp.bfloat16))
 
 
 def accumulate(acts, pieces):
@@ -134,13 +166,13 @@
 
 
 def arrange_kernel(source_ref, own_ref, next_1_ref, next_2_ref, out_ref):
-    column = lax.broadcasted_iota(jnp.int32, (384, 128), 1)
+    column = lax.broadcasted_iota(jnp.int32, (384, 64), 1)
     source = source_ref[...]
     total = None
     for at, rows_ref in enumerate((own_ref, next_1_ref, next_2_ref)):
-        chosen = jnp.where(source == column + 128 * at, 1.0, 0.0).astype(jnp.bfloat16)
-        term = jnp.dot(chosen, rows_ref[...], preferred_element_type=jnp.float32)
-        total = term if total is None else total + term
+        for which in range(2):
+            term = dot(ones_where(source == 2 * column + (which + 128 * at)), rows_ref[:, which, :])
+            total = term if total is None else total + term
     out_ref[...] = total.astype(jnp.bfloat16)
 
 
@@ -208,17 +240,13 @@
     def to_left(rows):
         return lax.ppermute(rows, "x", ring(4, -1))
 
-    scaling = jnp.exp2(act_exponent.astype(jnp.float32)).astype(jnp.bfloat16)
-    inverse = (1.0 / scaling.astype(jnp.float32)).astype(jnp.bfloat16)
-    level = jnp.broadcast_to((7.5 - clip_index.astype(jnp.float32)).astype(jnp.bfloat16)[None, :], (128, 13))
-    packed = jnp.concatenate([hidden, scaling, inverse, level, jnp.zeros((128, 25), jnp.bfloat16)], axis=1)
+    packed = pack(hidden, act_exponent, clip_index)
     packed, down_weight = lax.optimization_barrier((packed, down_weight))
     weight_0 = quantize_weight(down_weight, weight_exponent)
     weight_1, weight_3 = to_left(weight_0), to_right(weight_0)
-    arrived = lax.all_to_all(packed.reshape(64, 2, WIDTH), TENSOR, split_axis=0, concat_axis=0, tiled=True)
-    quantized = rotate_and_quantize(arrived.reshape(128, WIDTH))
-    returned = lax.all_to_all(quantized.reshape(64, 2, 832), TENSOR, split_axis=0, concat_axis=0, tiled=True)
-    own = returned.reshape(128, 832)
+    arrived = lax.all_to_all(packed, TENSOR, split_axis=0, concat_axis=0, tiled=True)
+    quantized = rotate_and_quantize(arrived)
+    own = lax.all_to_all(quantized, TENSOR, split_axis=0, concat_axis=0, tiled=True)
     next_1 = lax.ppermute(own, "h", ring(3, -1))
     next_2 = lax.ppermute(own, "h", ring(3, 1))
     weight_2 = (to_right(weight_3[:SPLIT]), to_left(weight_1[SPLIT:]))

time: 167 us -> 162 us (0.970)
  the two profiles are of different devices: /device:TPU:21 before, /device:TPU:40 now
where the time goes in v6:
time: 162 us; the launch traced here: 161 us
  starting transfers between devices  74.1 us (46%)
  waiting for transfers between devices  44.4 us (27%)
  blocking collectives  19.4 us (12%)
  Pallas kernels  12.2 us (8%)
  other arithmetic  7.37 us (5%)
  local copies, waits for them, and re-layouts  3.63 us (2%)
    all_to_all x1, blocking collectives, shards(): lax.all_to_all(quantized, TENSOR, split_axis=0, concat_axis=0, tiled=True)  19.4 us
    all_to_all x1, waiting for transfers between devices, shards(): lax.all_to_all(sums, ('l', 'yh'), split_axis=0, concat_axis=0, tiled=True)  17.9 us
    all_to_all x1, starting transfers between devices, shards(): lax.all_to_all(packed, TENSOR, split_axis=0, concat_axis=0, tiled=True)  13.9 us
    all_to_all x1, starting transfers between devices, shards(): lax.all_to_all(sums, ('l', 'yh'), split_axis=0, concat_axis=0, tiled=True)  13.4 us
    ppermute x1, starting transfers between devices, shards(): next_1 = lax.ppermute(own, 'h', ring(3, -1))  11.8 us
    ppermute x2, waiting for transfers between devices, shards(): lax.ppermute(mine[:, :96].astype(jnp.bfloat16), ('yh', 'yl'), y_pairs)  9.56 us
    ppermute x2, starting transfers between devices, to_left(): return lax.ppermute(rows, 'x', ring(4, -1))  9.18 us
    ppermute x1, waiting for transfers between devices, shards(): next_1 = lax.ppermute(own, 'h', ring(3, -1))  9.12 us
  transfers between devices with their start and end apart: 14, of which 7 were waited for; matrix products, arithmetic and copies ran while one was open for 4% of the time, Pallas kernels for 7%

profile of v6, /device:TPU:40, one launch (start us, length us, event | category | flops | bytes accessed | tf_op | source)
XLA Modules:
  0.0 161.4 jit_solution(4478504971533924686)
XLA Ops:
  0.0 0.9 copy-done
  0.9 0.7 copy-done.1
  1.6 0.7 copy-done.2
  2.3 1.1 shard_map.73
  3.4 13.9 %all-to-all-start = ((bf16[64,2,896]{2,1,0:T(2,128)(2,1)}), bf16[64,2,896]{2,1,0:T(2,128)(2,1)}, u32[]{:S(2)}, u32[]{:S(2)}) async-start(bf16[64,2,896]{2,1,0:T(2,128)(2,1)} %shard_map.73), calls=%async_computation | async-start | bytes 458752 | tf_op jit(solution)/shard_map/all_to_all | solution.py:247
  17.3 0.7 fusion.25
  18.0 3.8 %multiply_convert_fusion.refs_1_ = bf16[832,1024]{1,0:T(8,128)(2,1)S(1)} fusion(bf16[832,1024]{1,0:T(8,128)(2,1)} %param.8, f32[1024]{0:T(1024)S(1)} %fusion.25), kind=kLoop, calls=%fused_computation.1 | loop fusion | flops 20447232 | bytes 3411968 | tf_op jit(solution)/shard_map/convert_element_type | solution.py:193
  21.8 4.0 %collective-permute-start.2 = (bf16[832,1024]{1,0:T(8,128)(2,1)S(1)}, bf16[832,1024]{1,0:T(8,128)(2,1)S(1)}, u32[]{:S(2)}, u32[]{:S(2)}) collective-permute-start(bf16[832,1024]{1,0:T(8,128)(2,1)S(1)} %multiply_convert_fusion.refs_1_), channel_id=1, source_target_pairs={{0,192},{64,0},{128,64},{192,128},{1,193},{65,1},{129,65},{193,129... | collective-permute-start | bytes 5111816 | tf_op jit(solution)/shard_map/ppermute | solution.py:241
  25.9 1.9 %collective-permute-start.5 = (bf16[832,1024]{1,0:T(8,128)(2,1)S(1)}, bf16[832,1024]{1,0:T(8,128)(2,1)}, u32[]{:S(2)}, u32[]{:S(2)}) collective-permute-start(bf16[832,1024]{1,0:T(8,128)(2,1)S(1)} %multiply_convert_fusion.refs_1_), channel_id=1, source_target_pairs={{0,64},{64,128},{128,192},{192,0},{1,65},{65,129},{129,193},{193,1... | collective-permute-start | bytes 5111816 | tf_op jit(solution)/shard_map/ppermute | solution.py:238
  27.8 0.0 all-to-all-done.x_ref
  27.8 2.7 %shard_map.74 = bf16[64,2,832]{2,1,0:T(2,128)(2,1)S(1)} custom-call(bf16[64,2,896]{2,1,0:T(2,128)(2,1)} %all-to-all-done.x_ref, bf16[64,64]{1,0:T(8,128)(2,1)S(1)} %copy-done.4, bf16[128,128]{1,0:T(8,128)(2,1)S(1)} %copy-done.3), custom_call_target="tpu_custom_call" | custom-call | flops 40000000000 | bytes 1500000 | tf_op jit(solution)/shard_map/pallas_call | solution.py:121
  30.5 19.4 %all_to_all.15.own_ref = bf16[64,2,832]{2,1,0:T(2,128)(2,1)} all-to-all(bf16[64,2,832]{2,1,0:T(2,128)(2,1)S(1)} %shard_map.74), channel_id=1, replica_groups=mesh['h'=3,'x'=4,'l'=4,'yh'=4,'yl'=2,'c'=2] {'l','yh','yl','c'}, dimensions={0} | all-to-all | bytes 425984 | tf_op jit(solution)/shard_map/all_to_all | solution.py:249
  50.0 11.8 %collective-permute-start = (bf16[64,2,832]{2,1,0:T(2,128)(2,1)}, bf16[64,2,832]{2,1,0:T(2,128)(2,1)}, u32[]{:S(2)}, u32[]{:S(2)}) collective-permute-start(bf16[64,2,832]{2,1,0:T(2,128)(2,1)} %all_to_all.15.own_ref), channel_id=1, source_target_pairs={{0,512},{256,0},{512,256},{1,513},{257,1},{513,257},{2,514},{258,2... | collective-permute-start | bytes 638984 | tf_op jit(solution)/shard_map/ppermute | solution.py:250
  61.8 1.9 %collective-permute-start.1 = (bf16[64,2,832]{2,1,0:T(2,128)(2,1)}, bf16[64,2,832]{2,1,0:T(2,128)(2,1)}, u32[]{:S(2)}, u32[]{:S(2)}) collective-permute-start(bf16[64,2,832]{2,1,0:T(2,128)(2,1)} %all_to_all.15.own_ref), channel_id=1, source_target_pairs={{0,256},{256,512},{512,0},{1,257},{257,513},{513,1},{2,258},{258,5... | collective-permute-start | bytes 638984 | tf_op jit(solution)/shard_map/ppermute | solution.py:251
  63.8 0.5 add_select_fusion.source_ref
  64.3 0.0 collective-permute-done.2.refs_2_
  64.3 0.1 slice.49
  64.4 5.1 %collective-permute-start.7 = (bf16[448,1024]{1,0:T(8,128)(2,1)S(1)}, bf16[448,1024]{1,0:T(8,128)(2,1)S(1)}, u32[]{:S(2)}, u32[]{:S(2)}) collective-permute-start(bf16[448,1024]{1,0:T(8,128)(2,1)S(1)} %slice.49), channel_id=1, source_target_pairs={{0,192},{64,0},{128,64},{192,128},{1,193},{65,1},{129,65},{193,129... | collective-permute-start | bytes 2752520 | tf_op jit(solution)/shard_map/ppermute | solution.py:241
  69.5 1.2 slice.48
  70.7 1.9 %collective-permute-start.6 = (bf16[384,1024]{1,0:T(8,128)(2,1)S(1)}, bf16[384,1024]{1,0:T(8,128)(2,1)S(1)}, u32[]{:S(2)}, u32[]{:S(2)}) collective-permute-start(bf16[384,1024]{1,0:T(8,128)(2,1)S(1)} %slice.48), channel_id=1, source_target_pairs={{0,64},{64,128},{128,192},{192,0},{1,65},{65,129},{129,193},{193,1... | collective-permute-start | bytes 2359304 | tf_op jit(solution)/shard_map/ppermute | solution.py:238
  72.7 9.1 %collective-permute-done.next_1_ref = bf16[64,2,832]{2,1,0:T(2,128)(2,1)} collective-permute-done((bf16[64,2,832]{2,1,0:T(2,128)(2,1)}, bf16[64,2,832]{2,1,0:T(2,128)(2,1)}, u32[]{:S(2)}, u32[]{:S(2)}) %collective-permute-start) | collective-permute-done | bytes 213024 | tf_op jit(solution)/shard_map/ppermute | solution.py:250
  81.8 0.5 collective-permute-done.1.next_2_ref
  82.3 3.3 %shard_map.75.refs_0_ = bf16[384,832]{1,0:T(8,128)(2,1)S(1)} custom-call(s32[384,1]{1,0:T(8,128)S(1)} %add_select_fusion.source_ref, bf16[64,2,832]{2,1,0:T(2,128)(2,1)} %all_to_all.15.own_ref, bf16[64,2,832]{2,1,0:T(2,128)(2,1)} %collective-permute-done.next_1_ref, bf16[64,2,832]{2,1,0:T(2,128)(2,1)} %collective-permute-done.1.next_2_ref), custom_call_target="tpu_custom_call" | custom-call | flops 20000000000 | bytes 1500000 | tf_op jit(solution)/shard_map/pallas_call | solution.py:180
  85.6 1.8 %shard_map.76 = (bf16[2,192,1024]{2,1,0:T(8,128)(2,1)S(1)}, f32[2,192,1024]{2,1,0:T(8,128)S(1)}) custom-call(bf16[384,832]{1,0:T(8,128)(2,1)S(1)} %shard_map.75.refs_0_, bf16[832,1024]{1,0:T(8,128)(2,1)S(1)} %multiply_convert_fusion.refs_1_, bf16[832,1024]{1,0:T(8,128)(2,1)S(1)} %collective-permute-done.2.refs_2_), custom_call_target="tpu_custom_call" | custom-call | flops 1300000000 | bytes 6000000 | tf_op jit(solution)/shard_map/pallas_call | solution.py:155
  87.4 1.9 %collective-permute-start.3 = (bf16[2,192,1024]{2,1,0:T(8,128)(2,1)S(1)}, bf16[2,192,1024]{2,1,0:T(8,128)(2,1)S(1)}, u32[]{:S(2)}, u32[]{:S(2)}) collective-permute-start(bf16[2,192,1024]{2,1,0:T(8,128)(2,1)S(1)} %get-tuple-element.14), channel_id=1, source_target_pairs={{0,1},{1,0},{2,3},{3,2},{4,5},{5,4},{6,7},{7,6},{8,9},{9,8},{10,11... | collective-permute-start | bytes 2359304 | tf_op jit(solution)/shard_map/ppermute | solution.py:260
  89.3 3.5 %collective-permute-done.6.refs_2_ = bf16[384,1024]{1,0:T(8,128)(2,1)S(1)} collective-permute-done((bf16[384,1024]{1,0:T(8,128)(2,1)S(1)}, bf16[384,1024]{1,0:T(8,128)(2,1)S(1)}, u32[]{:S(2)}, u32[]{:S(2)}) %collective-permute-start.6) | collective-permute-done | bytes 786464 | tf_op jit(solution)/shard_map/ppermute | solution.py:238
  92.8 3.2 %shard_map.77 = (bf16[2,192,1024]{2,1,0:T(8,128)(2,1)S(1)}, f32[2,192,1024]{2,1,0:T(8,128)S(1)}) custom-call(bf16[384,832]{1,0:T(8,128)(2,1)S(1)} %shard_map.75.refs_0_, bf16[832,1024]{1,0:T(8,128)(2,1)} %collective-permute-done.5.refs_1_, bf16[384,1024]{1,0:T(8,128)(2,1)S(1)} %collective-permute-done.6.refs_2_, ...), custom_call_target="tpu_custom_call" | custom-call | flops 1300000000 | bytes 6000000 | tf_op jit(solution)/shard_map/pallas_call | solution.py:155
  96.1 1.9 %collective-permute-start.8 = (bf16[2,192,1024]{2,1,0:T(8,128)(2,1)S(1)}, bf16[2,192,1024]{2,1,0:T(8,128)(2,1)S(1)}, u32[]{:S(2)}, u32[]{:S(2)}) collective-permute-start(bf16[2,192,1024]{2,1,0:T(8,128)(2,1)S(1)} %get-tuple-element.16), channel_id=1, source_target_pairs={{0,1},{1,0},{2,3},{3,2},{4,5},{5,4},{6,7},{7,6},{8,9},{9,8},{10,11... | collective-permute-start | bytes 2359304 | tf_op jit(solution)/shard_map/ppermute | solution.py:260
  98.0 0.0 collective-permute-done.3
  98.0 0.2 convert_add_fusion.1
  98.2 0.1 slice.70
  98.3 2.7 %collective-permute-start.4 = (bf16[2,96,1024]{2,1,0:T(8,128)(2,1)S(1)}, bf16[2,96,1024]{2,1,0:T(8,128)(2,1)S(1)}, u32[]{:S(2)}, u32[]{:S(2)}) collective-permute-start(bf16[2,96,1024]{2,1,0:T(8,128)(2,1)S(1)} %slice.70), channel_id=1, source_target_pairs={{0,2},{2,0},{4,6},{6,4},{8,10},{10,8},{12,14},{14,12},{1,3},{3,1},... | collective-permute-start | bytes 1179656 | tf_op jit(solution)/shard_map/ppermute | solution.py:262
  101.0 0.0 collective-permute-done.8
  101.0 0.2 convert_add_fusion
  101.3 3.5 %collective-permute-start.9 = (bf16[2,96,1024]{2,1,0:T(8,128)(2,1)S(1)}, bf16[2,96,1024]{2,1,0:T(8,128)(2,1)S(1)}, u32[]{:S(2)}, u32[]{:S(2)}) collective-permute-start(bf16[2,96,1024]{2,1,0:T(8,128)(2,1)S(1)} %slice.69), channel_id=1, source_target_pairs={{0,14},{2,4},{4,2},{6,8},{8,6},{10,12},{12,10},{14,0},{1,15},{3,5}... | collective-permute-start | bytes 1179656 | tf_op jit(solution)/shard_map/ppermute | solution.py:262
  104.8 6.9 %collective-permute-done.4 = bf16[2,96,1024]{2,1,0:T(8,128)(2,1)S(1)} collective-permute-done((bf16[2,96,1024]{2,1,0:T(8,128)(2,1)S(1)}, bf16[2,96,1024]{2,1,0:T(8,128)(2,1)S(1)}, u32[]{:S(2)}, u32[]{:S(2)}) %collective-permute-start.4) | collective-permute-done | bytes 393248 | tf_op jit(solution)/shard_map/ppermute | solution.py:262
  111.7 0.1 fusion.6
  111.8 2.6 %collective-permute-done.9 = bf16[2,96,1024]{2,1,0:T(8,128)(2,1)S(1)} collective-permute-done((bf16[2,96,1024]{2,1,0:T(8,128)(2,1)S(1)}, bf16[2,96,1024]{2,1,0:T(8,128)(2,1)S(1)}, u32[]{:S(2)}, u32[]{:S(2)}) %collective-permute-start.9) | collective-permute-done | bytes 393248 | tf_op jit(solution)/shard_map/ppermute | solution.py:262
  114.4 0.1 fusion.5
  114.5 0.9 pad_maximum_fusion
  115.5 13.4 %all-to-all-start.2 = ((bf16[16,24,1024]{2,1,0:T(8,128)(2,1)}), bf16[16,24,1024]{2,1,0:T(8,128)(2,1)S(1)}, u32[]{:S(2)}, u32[]{:S(2)}) async-start(bf16[16,24,1024]{2,1,0:T(8,128)(2,1)} %bitcast.3), calls=%async_computation.2 | async-start | bytes 1572864 | tf_op jit(solution)/shard_map/all_to_all | solution.py:265
  128.9 17.9 %all-to-all-done.2 = bf16[16,24,1024]{2,1,0:T(8,128)(2,1)S(1)} async-done(((bf16[16,24,1024]{2,1,0:T(8,128)(2,1)}), bf16[16,24,1024]{2,1,0:T(8,128)(2,1)S(1)}, u32[]{:S(2)}, u32[]{:S(2)}) %all-to-all-start.2) | async-done | bytes 786464 | tf_op jit(solution)/shard_map/all_to_all | solution.py:265
  146.8 0.1 reduce_sum.12
  146.9 4.0 %collective-permute-start.11 = (bf16[24,1024]{1,0:T(8,128)(2,1)S(1)}, bf16[24,1024]{1,0:T(8,128)(2,1)S(1)}, u32[]{:S(2)}, u32[]{:S(2)}) collective-permute-start(bf16[24,1024]{1,0:T(8,128)(2,1)S(1)} %reduce_sum.12), channel_id=1, source_target_pairs={{0,0},{1,1},{2,2},{3,3},{4,4},{5,21},{6,22},{7,23},{8,24},{9,25},{... | collective-permute-start | bytes 147464 | tf_op jit(solution)/shard_map/ppermute | solution.py:271
  150.9 6.0 %collective-permute-start.10 = (bf16[8,1024]{1,0:T(8,128)(2,1)S(1)}, bf16[8,1024]{1,0:T(8,128)(2,1)S(1)}, u32[]{:S(2)}, u32[]{:S(2)}) collective-permute-start(bf16[8,1024]{1,0:T(8,128)(2,1)S(1)} %slice_select_fusion.2), channel_id=1, source_target_pairs={{5,5},{10,42},{21,69},{26,106},{37,197},{42,234},{53,133},{58,170}... | collective-permute-start | bytes 49160 | tf_op jit(solution)/shard_map/ppermute | solution.py:272
  157.0 3.8 %collective-permute-done.10 = bf16[8,1024]{1,0:T(8,128)(2,1)S(1)} collective-permute-done((bf16[8,1024]{1,0:T(8,128)(2,1)S(1)}, bf16[8,1024]{1,0:T(8,128)(2,1)S(1)}, u32[]{:S(2)}, u32[]{:S(2)}) %collective-permute-start.10) | collective-permute-done | bytes 16416 | tf_op jit(solution)/shard_map/ppermute | solution.py:272
  160.7 0.0 collective-permute-done.11
  160.8 0.6 pad_maximum_fusion.1
  (12 shorter events, 0.1 us)
Async XLA Ops:
  0.0 0.9 copy-start
  0.9 0.7 copy-start.1
  1.6 0.7 copy-start.2
  3.4 24.4 %all-to-all-start = ((bf16[64,2,896]{2,1,0:T(2,128)(2,1)}), bf16[64,2,896]{2,1,0:T(2,128)(2,1)}, u32[]{:S(2)}, u32[]{:S(2)}) async-start(bf16[64,2,896]{2,1,0:T(2,128)(2,1)} %shard_map.73), calls=%async_computation | async-start | bytes 458752 | tf_op jit(solution)/shard_map/all_to_all | solution.py:247
  18.0 9.8 %copy-start.3 = (bf16[128,128]{1,0:T(8,128)(2,1)S(1)}, bf16[128,128]{1,0:T(8,128)(2,1)}, u32[]{:S(2)}) copy-start(bf16[128,128]{1,0:T(8,128)(2,1)} %constant.115.clone.lanes_ref) | copy-start | bytes 98308
  18.0 9.8 %copy-start.4 = (bf16[64,64]{1,0:T(8,128)(2,1)S(1)}, bf16[64,64]{1,0:T(8,128)(2,1)}, u32[]{:S(2)}) copy-start(bf16[64,64]{1,0:T(8,128)(2,1)} %constant.114.clone.rows_ref) | copy-start | bytes 24580
  21.8 42.5 %collective-permute-start.2 = (bf16[832,1024]{1,0:T(8,128)(2,1)S(1)}, bf16[832,1024]{1,0:T(8,128)(2,1)S(1)}, u32[]{:S(2)}, u32[]{:S(2)}) collective-permute-start(bf16[832,1024]{1,0:T(8,128)(2,1)S(1)} %multiply_convert_fusion.refs_1_), channel_id=1, source_target_pairs={{0,192},{64,0},{128,64},{192,128},{1,193},{65,1},{129,65},{193,129... | collective-permute-start | bytes 5111816 | tf_op jit(solution)/shard_map/ppermute | solution.py:241
  25.9 43.7 %collective-permute-start.5 = (bf16[832,1024]{1,0:T(8,128)(2,1)S(1)}, bf16[832,1024]{1,0:T(8,128)(2,1)}, u32[]{:S(2)}, u32[]{:S(2)}) collective-permute-start(bf16[832,1024]{1,0:T(8,128)(2,1)S(1)} %multiply_convert_fusion.refs_1_), channel_id=1, source_target_pairs={{0,64},{64,128},{128,192},{192,0},{1,65},{65,129},{129,193},{193,1... | collective-permute-start | bytes 5111816 | tf_op jit(solution)/shard_map/ppermute | solution.py:238
  50.0 31.8 %collective-permute-start = (bf16[64,2,832]{2,1,0:T(2,128)(2,1)}, bf16[64,2,832]{2,1,0:T(2,128)(2,1)}, u32[]{:S(2)}, u32[]{:S(2)}) collective-permute-start(bf16[64,2,832]{2,1,0:T(2,128)(2,1)} %all_to_all.15.own_ref), channel_id=1, source_target_pairs={{0,512},{256,0},{512,256},{1,513},{257,1},{513,257},{2,514},{258,2... | collective-permute-start | bytes 638984 | tf_op jit(solution)/shard_map/ppermute | solution.py:250
  61.8 20.5 %collective-permute-start.1 = (bf16[64,2,832]{2,1,0:T(2,128)(2,1)}, bf16[64,2,832]{2,1,0:T(2,128)(2,1)}, u32[]{:S(2)}, u32[]{:S(2)}) collective-permute-start(bf16[64,2,832]{2,1,0:T(2,128)(2,1)} %all_to_all.15.own_ref), channel_id=1, source_target_pairs={{0,256},{256,512},{512,0},{1,257},{257,513},{513,1},{2,258},{258,5... | collective-permute-start | bytes 638984 | tf_op jit(solution)/shard_map/ppermute | solution.py:251
  64.4 28.4 %collective-permute-start.7 = (bf16[448,1024]{1,0:T(8,128)(2,1)S(1)}, bf16[448,1024]{1,0:T(8,128)(2,1)S(1)}, u32[]{:S(2)}, u32[]{:S(2)}) collective-permute-start(bf16[448,1024]{1,0:T(8,128)(2,1)S(1)} %slice.49), channel_id=1, source_target_pairs={{0,192},{64,0},{128,64},{192,128},{1,193},{65,1},{129,65},{193,129... | collective-permute-start | bytes 2752520 | tf_op jit(solution)/shard_map/ppermute | solution.py:241
  70.7 22.1 %collective-permute-start.6 = (bf16[384,1024]{1,0:T(8,128)(2,1)S(1)}, bf16[384,1024]{1,0:T(8,128)(2,1)S(1)}, u32[]{:S(2)}, u32[]{:S(2)}) collective-permute-start(bf16[384,1024]{1,0:T(8,128)(2,1)S(1)} %slice.48), channel_id=1, source_target_pairs={{0,64},{64,128},{128,192},{192,0},{1,65},{65,129},{129,193},{193,1... | collective-permute-start | bytes 2359304 | tf_op jit(solution)/shard_map/ppermute | solution.py:238
  87.4 10.6 %collective-permute-start.3 = (bf16[2,192,1024]{2,1,0:T(8,128)(2,1)S(1)}, bf16[2,192,1024]{2,1,0:T(8,128)(2,1)S(1)}, u32[]{:S(2)}, u32[]{:S(2)}) collective-permute-start(bf16[2,192,1024]{2,1,0:T(8,128)(2,1)S(1)} %get-tuple-element.14), channel_id=1, source_target_pairs={{0,1},{1,0},{2,3},{3,2},{4,5},{5,4},{6,7},{7,6},{8,9},{9,8},{10,11... | collective-permute-start | bytes 2359304 | tf_op jit(solution)/shard_map/ppermute | solution.py:260
  96.1 4.9 %collective-permute-start.8 = (bf16[2,192,1024]{2,1,0:T(8,128)(2,1)S(1)}, bf16[2,192,1024]{2,1,0:T(8,128)(2,1)S(1)}, u32[]{:S(2)}, u32[]{:S(2)}) collective-permute-start(bf16[2,192,1024]{2,1,0:T(8,128)(2,1)S(1)} %get-tuple-element.16), channel_id=1, source_target_pairs={{0,1},{1,0},{2,3},{3,2},{4,5},{5,4},{6,7},{7,6},{8,9},{9,8},{10,11... | collective-permute-start | bytes 2359304 | tf_op jit(solution)/shard_map/ppermute | solution.py:260
  98.3 13.4 %collective-permute-start.4 = (bf16[2,96,1024]{2,1,0:T(8,128)(2,1)S(1)}, bf16[2,96,1024]{2,1,0:T(8,128)(2,1)S(1)}, u32[]{:S(2)}, u32[]{:S(2)}) collective-permute-start(bf16[2,96,1024]{2,1,0:T(8,128)(2,1)S(1)} %slice.70), channel_id=1, source_target_pairs={{0,2},{2,0},{4,6},{6,4},{8,10},{10,8},{12,14},{14,12},{1,3},{3,1},... | collective-permute-start | bytes 1179656 | tf_op jit(solution)/shard_map/ppermute | solution.py:262
  101.3 13.1 %collective-permute-start.9 = (bf16[2,96,1024]{2,1,0:T(8,128)(2,1)S(1)}, bf16[2,96,1024]{2,1,0:T(8,128)(2,1)S(1)}, u32[]{:S(2)}, u32[]{:S(2)}) collective-permute-start(bf16[2,96,1024]{2,1,0:T(8,128)(2,1)S(1)} %slice.69), channel_id=1, source_target_pairs={{0,14},{2,4},{4,2},{6,8},{8,6},{10,12},{12,10},{14,0},{1,15},{3,5}... | collective-permute-start | bytes 1179656 | tf_op jit(solution)/shard_map/ppermute | solution.py:262
  115.5 31.3 %all-to-all-start.2 = ((bf16[16,24,1024]{2,1,0:T(8,128)(2,1)}), bf16[16,24,1024]{2,1,0:T(8,128)(2,1)S(1)}, u32[]{:S(2)}, u32[]{:S(2)}) async-start(bf16[16,24,1024]{2,1,0:T(8,128)(2,1)} %bitcast.3), calls=%async_computation.2 | async-start | bytes 1572864 | tf_op jit(solution)/shard_map/all_to_all | solution.py:265
  146.9 13.9 %collective-permute-start.11 = (bf16[24,1024]{1,0:T(8,128)(2,1)S(1)}, bf16[24,1024]{1,0:T(8,128)(2,1)S(1)}, u32[]{:S(2)}, u32[]{:S(2)}) collective-permute-start(bf16[24,1024]{1,0:T(8,128)(2,1)S(1)} %reduce_sum.12), channel_id=1, source_target_pairs={{0,0},{1,1},{2,2},{3,3},{4,4},{5,21},{6,22},{7,23},{8,24},{9,25},{... | collective-permute-start | bytes 147464 | tf_op jit(solution)/shard_map/ppermute | solution.py:271
  150.9 9.8 %collective-permute-start.10 = (bf16[8,1024]{1,0:T(8,128)(2,1)S(1)}, bf16[8,1024]{1,0:T(8,128)(2,1)S(1)}, u32[]{:S(2)}, u32[]{:S(2)}) collective-permute-start(bf16[8,1024]{1,0:T(8,128)(2,1)S(1)} %slice_select_fusion.2), channel_id=1, source_target_pairs={{5,5},{10,42},{21,69},{26,106},{37,197},{42,234},{53,133},{58,170}... | collective-permute-start | bytes 49160 | tf_op jit(solution)/shard_map/ppermute | solution.py:272

commit v7 on v6

--- a/solution.py
+++ b/solution.py
@@ -90,30 +90,29 @@
 
 
 def rotate_kernel(x_ref, rows_ref, lanes_ref, out_ref):
-    lanes, rows = lanes_ref[...], rows_ref[...]
+    lanes = lanes_ref[...]
     row = lax.broadcasted_iota(jnp.int32, (128, 128), 0)
     upper = jnp.where(lax.broadcasted_iota(jnp.int32, (128, 128), 1) >= 64, 1, 0)
     place = row - upper
-    for which in range(2):
-        arrived = x_ref[:, which, :]
-        mixed = dot(rows, arrived)
-        extra = arrived[:, 768:896]
-        for piece in range(7):
-            width = 128 if piece < 6 else 64
-            rest = mixed[:, piece * 128 : piece * 128 + 128]
-            rotated = None
-            for _ in range(3):
-                part = rest.astype(jnp.bfloat16)
-                rest = rest - part.astype(jnp.float32)
-                term = dot(part, lanes)
-                rotated = term if rotated is None else rotated + term
-            scale, inverse, level = (
-                dot(extra, ones_where(place == 64 + 13 * kind + 2 * piece)) for kind in range(3)
-            )
-            scaled = rotated * (1.0 / 64.0) * inverse
-            clipped = jnp.maximum(jnp.minimum(scaled, level), -level)
-            quantized = (soft_round(clipped) * scale).astype(jnp.bfloat16)
-            out_ref[:, which, piece * 128 : piece * 128 + width] = quantized[:, :width]
+    arrived = x_ref[...].reshape(128, WIDTH)
+    mixed = dot(rows_ref[...], arrived)
+    extra = arrived[:, 768:896]
+    for piece in range(7):
+        width = 128 if piece < 6 else 64
+        rest = mixed[:, piece * 128 : piece * 128 + 128]
+        rotated = None
+        for _ in range(3):
+            part = rest.astype(jnp.bfloat16)
+            rest = rest - part.astype(jnp.float32)
+            term = dot(part, lanes)
+            rotated = term if rotated is None else rotated + term
+        scale, inverse, level = (
+            dot(extra, ones_where(place == 64 + 13 * kind + 2 * piece)) for kind in range(3)
+        )
+        scaled = rotated * (1.0 / 64.0) * inverse
+        clipped = jnp.maximum(jnp.minimum(scaled, level), -level)
+        quantized = (soft_round(clipped) * scale).astype(jnp.bfloat16)
+        out_ref[:, :, piece * 128 : piece * 128 + width] = quantized[:, :width].reshape(64, 2, width)
 
 
 def rotate_and_quantize(arrived):
@@ -124,8 +123,8 @@
         in_specs=[pl.BlockSpec(memory_space=pltpu.VMEM)] * 3,
         out_specs=pl.BlockSpec(memory_space=pltpu.VMEM),
         compiler_params=pltpu.CompilerParams(vmem_limit_bytes=24 * 1024 * 1024),
-        cost_estimate=pl.CostEstimate(flops=40_000_000_000, bytes_accessed=1_500_000, transcendentals=0),
-    )(arrived, jnp.asarray(walsh(64), jnp.bfloat16), jnp.asarray(lanes, jnp.bfloat16))
+        cost_estimate=pl.CostEstimate(flops=2_000_000_000, bytes_accessed=1_500_000, transcendentals=0),
+    )(arrived, jnp.asarray(np.kron(walsh(64), np.eye(2)), jnp.bfloat16), jnp.asarray(lanes, jnp.bfloat16))
 
 
 def accumulate(acts, pieces):
@@ -166,13 +165,12 @@
 
 
 def arrange_kernel(source_ref, own_ref, next_1_ref, next_2_ref, out_ref):
-    column = lax.broadcasted_iota(jnp.int32, (384, 64), 1)
+    column = lax.broadcasted_iota(jnp.int32, (384, 128), 1)
     source = source_ref[...]
     total = None
     for at, rows_ref in enumerate((own_ref, next_1_ref, next_2_ref)):
-        for which in range(2):
-            term = dot(ones_where(source == 2 * column + (which + 128 * at)), rows_ref[:, which, :])
-            total = term if total is None else total + term
+        term = dot(ones_where(source == column + 128 * at), rows_ref[...].reshape(128, 832))
+        total = term if total is None else total + term
     out_ref[...] = total.astype(jnp.bfloat16)
 
 

time: 162 us -> 161 us (level)
  the two profiles are of different devices: /device:TPU:40 before, /device:TPU:21 now
where the time goes in v7:
time: 161 us; the launch traced here: 160 us
  starting transfers between devices  71.9 us (45%)
  waiting for transfers between devices  46.3 us (29%)
  blocking collectives  21.1 us (13%)
  Pallas kernels  9.84 us (6%)
  other arithmetic  7.37 us (5%)
  local copies, waits for them, and re-layouts  3.63 us (2%)
    all_to_all x1, blocking collectives, shards(): lax.all_to_all(quantized, TENSOR, split_axis=0, concat_axis=0, tiled=True)  21.1 us
    all_to_all x1, waiting for transfers between devices, shards(): lax.all_to_all(sums, ('l', 'yh'), split_axis=0, concat_axis=0, tiled=True)  18.1 us
    all_to_all x1, starting transfers between devices, shards(): lax.all_to_all(packed, TENSOR, split_axis=0, concat_axis=0, tiled=True)  13.9 us
    all_to_all x1, starting transfers between devices, shards(): lax.all_to_all(sums, ('l', 'yh'), split_axis=0, concat_axis=0, tiled=True)  12.7 us
    ppermute x1, starting transfers between devices, shards(): next_1 = lax.ppermute(own, 'h', ring(3, -1))  11.6 us
    ppermute x2, waiting for transfers between devices, shards(): lax.ppermute(mine[:, :96].astype(jnp.bfloat16), ('yh', 'yl'), y_pairs)  10.2 us
    ppermute x1, waiting for transfers between devices, shards(): next_1 = lax.ppermute(own, 'h', ring(3, -1))  10.1 us
    ppermute x1, starting transfers between devices, shards(): lax.ppermute(total, ('x', 'l', 'yh', 'yl', 'c'), final_pairs('main'))  8.11 us
  transfers between devices with their start and end apart: 14, of which 8 were waited for; matrix products, arithmetic and copies ran while one was open for 4% of the time, Pallas kernels for 5%

profile of v7, /device:TPU:21, one launch (start us, length us, event | category | flops | bytes accessed | tf_op | source)
XLA Modules:
  0.0 160.5 jit_solution(7643706294496033545)
XLA Ops:
  0.0 0.9 copy-done
  0.9 0.7 copy-done.1
  1.6 0.7 copy-done.2
  2.3 1.1 shard_map.73
  3.4 13.9 %all-to-all-start = ((bf16[64,2,896]{2,1,0:T(2,128)(2,1)}), bf16[64,2,896]{2,1,0:T(2,128)(2,1)}, u32[]{:S(2)}, u32[]{:S(2)}) async-start(bf16[64,2,896]{2,1,0:T(2,128)(2,1)} %shard_map.73), calls=%async_computation | async-start | bytes 458752 | tf_op jit(solution)/shard_map/all_to_all | solution.py:245
  17.3 0.7 fusion.25
  18.0 3.8 %multiply_convert_fusion.refs_1_ = bf16[832,1024]{1,0:T(8,128)(2,1)S(1)} fusion(bf16[832,1024]{1,0:T(8,128)(2,1)} %param.8, f32[1024]{0:T(1024)S(1)} %fusion.25), kind=kLoop, calls=%fused_computation.1 | loop fusion | flops 20447232 | bytes 3411968 | tf_op jit(solution)/shard_map/convert_element_type | solution.py:191
  21.8 2.2 %collective-permute-start.2 = (bf16[832,1024]{1,0:T(8,128)(2,1)S(1)}, bf16[832,1024]{1,0:T(8,128)(2,1)S(1)}, u32[]{:S(2)}, u32[]{:S(2)}) collective-permute-start(bf16[832,1024]{1,0:T(8,128)(2,1)S(1)} %multiply_convert_fusion.refs_1_), channel_id=1, source_target_pairs={{0,192},{64,0},{128,64},{192,128},{1,193},{65,1},{129,65},{193,129... | collective-permute-start | bytes 5111816 | tf_op jit(solution)/shard_map/ppermute | solution.py:239
  24.0 3.1 %collective-permute-start.5 = (bf16[832,1024]{1,0:T(8,128)(2,1)S(1)}, bf16[832,1024]{1,0:T(8,128)(2,1)}, u32[]{:S(2)}, u32[]{:S(2)}) collective-permute-start(bf16[832,1024]{1,0:T(8,128)(2,1)S(1)} %multiply_convert_fusion.refs_1_), channel_id=1, source_target_pairs={{0,64},{64,128},{128,192},{192,0},{1,65},{65,129},{129,193},{193,1... | collective-permute-start | bytes 5111816 | tf_op jit(solution)/shard_map/ppermute | solution.py:236
  27.1 0.7 all-to-all-done.x_ref
  27.8 1.8 %shard_map.74 = bf16[64,2,832]{2,1,0:T(2,128)(2,1)S(1)} custom-call(bf16[64,2,896]{2,1,0:T(2,128)(2,1)} %all-to-all-done.x_ref, bf16[128,128]{1,0:T(8,128)(2,1)S(1)} %copy-done.3, bf16[128,128]{1,0:T(8,128)(2,1)S(1)} %copy-done.4), custom_call_target="tpu_custom_call" | custom-call | flops 2000000000 | bytes 1500000 | tf_op jit(solution)/shard_map/pallas_call | solution.py:120
  29.6 21.1 %all_to_all.15.own_ref = bf16[64,2,832]{2,1,0:T(2,128)(2,1)} all-to-all(bf16[64,2,832]{2,1,0:T(2,128)(2,1)S(1)} %shard_map.74), channel_id=1, replica_groups=mesh['h'=3,'x'=4,'l'=4,'yh'=4,'yl'=2,'c'=2] {'l','yh','yl','c'}, dimensions={0} | all-to-all | bytes 425984 | tf_op jit(solution)/shard_map/all_to_all | solution.py:247
  50.7 11.6 %collective-permute-start = (bf16[64,2,832]{2,1,0:T(2,128)(2,1)}, bf16[64,2,832]{2,1,0:T(2,128)(2,1)}, u32[]{:S(2)}, u32[]{:S(2)}) collective-permute-start(bf16[64,2,832]{2,1,0:T(2,128)(2,1)} %all_to_all.15.own_ref), channel_id=1, source_target_pairs={{0,512},{256,0},{512,256},{1,513},{257,1},{513,257},{2,514},{258,2... | collective-permute-start | bytes 638984 | tf_op jit(solution)/shard_map/ppermute | solution.py:248
  62.3 1.9 %collective-permute-start.1 = (bf16[64,2,832]{2,1,0:T(2,128)(2,1)}, bf16[64,2,832]{2,1,0:T(2,128)(2,1)}, u32[]{:S(2)}, u32[]{:S(2)}) collective-permute-start(bf16[64,2,832]{2,1,0:T(2,128)(2,1)} %all_to_all.15.own_ref), channel_id=1, source_target_pairs={{0,256},{256,512},{512,0},{1,257},{257,513},{513,1},{2,258},{258,5... | collective-permute-start | bytes 638984 | tf_op jit(solution)/shard_map/ppermute | solution.py:249
  64.3 0.5 add_select_fusion.source_ref
  64.8 0.0 collective-permute-done.2.refs_2_
  64.8 0.1 slice.49
  64.9 2.2 %collective-permute-start.7 = (bf16[448,1024]{1,0:T(8,128)(2,1)S(1)}, bf16[448,1024]{1,0:T(8,128)(2,1)S(1)}, u32[]{:S(2)}, u32[]{:S(2)}) collective-permute-start(bf16[448,1024]{1,0:T(8,128)(2,1)S(1)} %slice.49), channel_id=1, source_target_pairs={{0,192},{64,0},{128,64},{192,128},{1,193},{65,1},{129,65},{193,129... | collective-permute-start | bytes 2752520 | tf_op jit(solution)/shard_map/ppermute | solution.py:239
  67.1 0.0 collective-permute-done.5.refs_1_
  67.1 1.2 slice.48
  68.3 3.8 %collective-permute-start.6 = (bf16[384,1024]{1,0:T(8,128)(2,1)S(1)}, bf16[384,1024]{1,0:T(8,128)(2,1)S(1)}, u32[]{:S(2)}, u32[]{:S(2)}) collective-permute-start(bf16[384,1024]{1,0:T(8,128)(2,1)S(1)} %slice.48), channel_id=1, source_target_pairs={{0,64},{64,128},{128,192},{192,0},{1,65},{65,129},{129,193},{193,1... | collective-permute-start | bytes 2359304 | tf_op jit(solution)/shard_map/ppermute | solution.py:236
  72.1 10.1 %collective-permute-done.next_1_ref = bf16[64,2,832]{2,1,0:T(2,128)(2,1)} collective-permute-done((bf16[64,2,832]{2,1,0:T(2,128)(2,1)}, bf16[64,2,832]{2,1,0:T(2,128)(2,1)}, u32[]{:S(2)}, u32[]{:S(2)}) %collective-permute-start) | collective-permute-done | bytes 213024 | tf_op jit(solution)/shard_map/ppermute | solution.py:248
  82.2 0.3 collective-permute-done.1.next_2_ref
  82.5 1.9 %shard_map.75.refs_0_ = bf16[384,832]{1,0:T(8,128)(2,1)S(1)} custom-call(s32[384,1]{1,0:T(8,128)S(1)} %add_select_fusion.source_ref, bf16[64,2,832]{2,1,0:T(2,128)(2,1)} %all_to_all.15.own_ref, bf16[64,2,832]{2,1,0:T(2,128)(2,1)} %collective-permute-done.next_1_ref, bf16[64,2,832]{2,1,0:T(2,128)(2,1)} %collective-permute-done.1.next_2_ref), custom_call_target="tpu_custom_call" | custom-call | flops 20000000000 | bytes 1500000 | tf_op jit(solution)/shard_map/pallas_call | solution.py:178
  84.4 1.8 %shard_map.76 = (bf16[2,192,1024]{2,1,0:T(8,128)(2,1)S(1)}, f32[2,192,1024]{2,1,0:T(8,128)S(1)}) custom-call(bf16[384,832]{1,0:T(8,128)(2,1)S(1)} %shard_map.75.refs_0_, bf16[832,1024]{1,0:T(8,128)(2,1)S(1)} %multiply_convert_fusion.refs_1_, bf16[832,1024]{1,0:T(8,128)(2,1)S(1)} %collective-permute-done.2.refs_2_), custom_call_target="tpu_custom_call" | custom-call | flops 1300000000 | bytes 6000000 | tf_op jit(solution)/shard_map/pallas_call | solution.py:154
  86.2 2.4 %collective-permute-start.3 = (bf16[2,192,1024]{2,1,0:T(8,128)(2,1)S(1)}, bf16[2,192,1024]{2,1,0:T(8,128)(2,1)S(1)}, u32[]{:S(2)}, u32[]{:S(2)}) collective-permute-start(bf16[2,192,1024]{2,1,0:T(8,128)(2,1)S(1)} %get-tuple-element.14), channel_id=1, source_target_pairs={{0,1},{1,0},{2,3},{3,2},{4,5},{5,4},{6,7},{7,6},{8,9},{9,8},{10,11... | collective-permute-start | bytes 2359304 | tf_op jit(solution)/shard_map/ppermute | solution.py:258
  88.6 0.0 collective-permute-done.6.refs_2_
  88.6 0.4 collective-permute-done.7.refs_3_
  89.0 3.2 %shard_map.77 = (bf16[2,192,1024]{2,1,0:T(8,128)(2,1)S(1)}, f32[2,192,1024]{2,1,0:T(8,128)S(1)}) custom-call(bf16[384,832]{1,0:T(8,128)(2,1)S(1)} %shard_map.75.refs_0_, bf16[832,1024]{1,0:T(8,128)(2,1)} %collective-permute-done.5.refs_1_, bf16[384,1024]{1,0:T(8,128)(2,1)S(1)} %collective-permute-done.6.refs_2_, ...), custom_call_target="tpu_custom_call" | custom-call | flops 1300000000 | bytes 6000000 | tf_op jit(solution)/shard_map/pallas_call | solution.py:154
  92.2 3.1 %collective-permute-start.8 = (bf16[2,192,1024]{2,1,0:T(8,128)(2,1)S(1)}, bf16[2,192,1024]{2,1,0:T(8,128)(2,1)S(1)}, u32[]{:S(2)}, u32[]{:S(2)}) collective-permute-start(bf16[2,192,1024]{2,1,0:T(8,128)(2,1)S(1)} %get-tuple-element.16), channel_id=1, source_target_pairs={{0,1},{1,0},{2,3},{3,2},{4,5},{5,4},{6,7},{7,6},{8,9},{9,8},{10,11... | collective-permute-start | bytes 2359304 | tf_op jit(solution)/shard_map/ppermute | solution.py:258
  95.4 0.2 convert_add_fusion.1
  95.6 0.1 slice.70
  95.7 2.7 %collective-permute-start.4 = (bf16[2,96,1024]{2,1,0:T(8,128)(2,1)S(1)}, bf16[2,96,1024]{2,1,0:T(8,128)(2,1)S(1)}, u32[]{:S(2)}, u32[]{:S(2)}) collective-permute-start(bf16[2,96,1024]{2,1,0:T(8,128)(2,1)S(1)} %slice.70), channel_id=1, source_target_pairs={{0,2},{2,0},{4,6},{6,4},{8,10},{10,8},{12,14},{14,12},{1,3},{3,1},... | collective-permute-start | bytes 1179656 | tf_op jit(solution)/shard_map/ppermute | solution.py:260
  98.4 0.0 collective-permute-done.8
  98.4 0.2 convert_add_fusion
  98.7 2.0 %collective-permute-start.9 = (bf16[2,96,1024]{2,1,0:T(8,128)(2,1)S(1)}, bf16[2,96,1024]{2,1,0:T(8,128)(2,1)S(1)}, u32[]{:S(2)}, u32[]{:S(2)}) collective-permute-start(bf16[2,96,1024]{2,1,0:T(8,128)(2,1)S(1)} %slice.69), channel_id=1, source_target_pairs={{0,14},{2,4},{4,2},{6,8},{8,6},{10,12},{12,10},{14,0},{1,15},{3,5}... | collective-permute-start | bytes 1179656 | tf_op jit(solution)/shard_map/ppermute | solution.py:260
  100.7 7.6 %collective-permute-done.4 = bf16[2,96,1024]{2,1,0:T(8,128)(2,1)S(1)} collective-permute-done((bf16[2,96,1024]{2,1,0:T(8,128)(2,1)S(1)}, bf16[2,96,1024]{2,1,0:T(8,128)(2,1)S(1)}, u32[]{:S(2)}, u32[]{:S(2)}) %collective-permute-start.4) | collective-permute-done | bytes 393248 | tf_op jit(solution)/shard_map/ppermute | solution.py:260
  108.3 0.1 fusion.6
  108.4 2.6 %collective-permute-done.9 = bf16[2,96,1024]{2,1,0:T(8,128)(2,1)S(1)} collective-permute-done((bf16[2,96,1024]{2,1,0:T(8,128)(2,1)S(1)}, bf16[2,96,1024]{2,1,0:T(8,128)(2,1)S(1)}, u32[]{:S(2)}, u32[]{:S(2)}) %collective-permute-start.9) | collective-permute-done | bytes 393248 | tf_op jit(solution)/shard_map/ppermute | solution.py:260
  111.0 0.1 fusion.5
  111.1 0.9 pad_maximum_fusion
  112.0 12.7 %all-to-all-start.2 = ((bf16[16,24,1024]{2,1,0:T(8,128)(2,1)}), bf16[16,24,1024]{2,1,0:T(8,128)(2,1)S(1)}, u32[]{:S(2)}, u32[]{:S(2)}) async-start(bf16[16,24,1024]{2,1,0:T(8,128)(2,1)} %bitcast.3), calls=%async_computation.2 | async-start | bytes 1572864 | tf_op jit(solution)/shard_map/all_to_all | solution.py:263
  124.8 18.1 %all-to-all-done.2 = bf16[16,24,1024]{2,1,0:T(8,128)(2,1)S(1)} async-done(((bf16[16,24,1024]{2,1,0:T(8,128)(2,1)}), bf16[16,24,1024]{2,1,0:T(8,128)(2,1)S(1)}, u32[]{:S(2)}, u32[]{:S(2)}) %all-to-all-start.2) | async-done | bytes 786464 | tf_op jit(solution)/shard_map/all_to_all | solution.py:263
  142.9 0.1 reduce_sum.12
  143.0 8.1 %collective-permute-start.11 = (bf16[24,1024]{1,0:T(8,128)(2,1)S(1)}, bf16[24,1024]{1,0:T(8,128)(2,1)S(1)}, u32[]{:S(2)}, u32[]{:S(2)}) collective-permute-start(bf16[24,1024]{1,0:T(8,128)(2,1)S(1)} %reduce_sum.12), channel_id=1, source_target_pairs={{0,0},{1,1},{2,2},{3,3},{4,4},{5,21},{6,22},{7,23},{8,24},{9,25},{... | collective-permute-start | bytes 147464 | tf_op jit(solution)/shard_map/ppermute | solution.py:269
  151.1 2.2 %collective-permute-start.10 = (bf16[8,1024]{1,0:T(8,128)(2,1)S(1)}, bf16[8,1024]{1,0:T(8,128)(2,1)S(1)}, u32[]{:S(2)}, u32[]{:S(2)}) collective-permute-start(bf16[8,1024]{1,0:T(8,128)(2,1)S(1)} %slice_select_fusion.2), channel_id=1, source_target_pairs={{5,5},{10,42},{21,69},{26,106},{37,197},{42,234},{53,133},{58,170}... | collective-permute-start | bytes 49160 | tf_op jit(solution)/shard_map/ppermute | solution.py:270
  153.3 6.5 %collective-permute-done.10 = bf16[8,1024]{1,0:T(8,128)(2,1)S(1)} collective-permute-done((bf16[8,1024]{1,0:T(8,128)(2,1)S(1)}, bf16[8,1024]{1,0:T(8,128)(2,1)S(1)}, u32[]{:S(2)}, u32[]{:S(2)}) %collective-permute-start.10) | collective-permute-done | bytes 16416 | tf_op jit(solution)/shard_map/ppermute | solution.py:270
  159.8 0.6 pad_maximum_fusion.1
  (12 shorter events, 0.1 us)
Async XLA Ops:
  0.0 0.9 copy-start
  0.9 0.7 copy-start.1
  1.6 0.7 copy-start.2
  3.4 24.4 %all-to-all-start = ((bf16[64,2,896]{2,1,0:T(2,128)(2,1)}), bf16[64,2,896]{2,1,0:T(2,128)(2,1)}, u32[]{:S(2)}, u32[]{:S(2)}) async-start(bf16[64,2,896]{2,1,0:T(2,128)(2,1)} %shard_map.73), calls=%async_computation | async-start | bytes 458752 | tf_op jit(solution)/shard_map/all_to_all | solution.py:245
  18.0 9.8 %copy-start.3 = (bf16[128,128]{1,0:T(8,128)(2,1)S(1)}, bf16[128,128]{1,0:T(8,128)(2,1)}, u32[]{:S(2)}) copy-start(bf16[128,128]{1,0:T(8,128)(2,1)} %constant.114.clone.rows_ref) | copy-start | bytes 98308
  18.0 9.8 %copy-start.4 = (bf16[128,128]{1,0:T(8,128)(2,1)S(1)}, bf16[128,128]{1,0:T(8,128)(2,1)}, u32[]{:S(2)}) copy-start(bf16[128,128]{1,0:T(8,128)(2,1)} %constant.115.clone.lanes_ref) | copy-start | bytes 98308
  21.8 43.0 %collective-permute-start.2 = (bf16[832,1024]{1,0:T(8,128)(2,1)S(1)}, bf16[832,1024]{1,0:T(8,128)(2,1)S(1)}, u32[]{:S(2)}, u32[]{:S(2)}) collective-permute-start(bf16[832,1024]{1,0:T(8,128)(2,1)S(1)} %multiply_convert_fusion.refs_1_), channel_id=1, source_target_pairs={{0,192},{64,0},{128,64},{192,128},{1,193},{65,1},{129,65},{193,129... | collective-permute-start | bytes 5111816 | tf_op jit(solution)/shard_map/ppermute | solution.py:239
  24.0 43.1 %collective-permute-start.5 = (bf16[832,1024]{1,0:T(8,128)(2,1)S(1)}, bf16[832,1024]{1,0:T(8,128)(2,1)}, u32[]{:S(2)}, u32[]{:S(2)}) collective-permute-start(bf16[832,1024]{1,0:T(8,128)(2,1)S(1)} %multiply_convert_fusion.refs_1_), channel_id=1, source_target_pairs={{0,64},{64,128},{128,192},{192,0},{1,65},{65,129},{129,193},{193,1... | collective-permute-start | bytes 5111816 | tf_op jit(solution)/shard_map/ppermute | solution.py:236
  50.7 31.4 %collective-permute-start = (bf16[64,2,832]{2,1,0:T(2,128)(2,1)}, bf16[64,2,832]{2,1,0:T(2,128)(2,1)}, u32[]{:S(2)}, u32[]{:S(2)}) collective-permute-start(bf16[64,2,832]{2,1,0:T(2,128)(2,1)} %all_to_all.15.own_ref), channel_id=1, source_target_pairs={{0,512},{256,0},{512,256},{1,513},{257,1},{513,257},{2,514},{258,2... | collective-permute-start | bytes 638984 | tf_op jit(solution)/shard_map/ppermute | solution.py:248
  62.3 20.1 %collective-permute-start.1 = (bf16[64,2,832]{2,1,0:T(2,128)(2,1)}, bf16[64,2,832]{2,1,0:T(2,128)(2,1)}, u32[]{:S(2)}, u32[]{:S(2)}) collective-permute-start(bf16[64,2,832]{2,1,0:T(2,128)(2,1)} %all_to_all.15.own_ref), channel_id=1, source_target_pairs={{0,256},{256,512},{512,0},{1,257},{257,513},{513,1},{2,258},{258,5... | collective-permute-start | bytes 638984 | tf_op jit(solution)/shard_map/ppermute | solution.py:249
  64.9 24.1 %collective-permute-start.7 = (bf16[448,1024]{1,0:T(8,128)(2,1)S(1)}, bf16[448,1024]{1,0:T(8,128)(2,1)S(1)}, u32[]{:S(2)}, u32[]{:S(2)}) collective-permute-start(bf16[448,1024]{1,0:T(8,128)(2,1)S(1)} %slice.49), channel_id=1, source_target_pairs={{0,192},{64,0},{128,64},{192,128},{1,193},{65,1},{129,65},{193,129... | collective-permute-start | bytes 2752520 | tf_op jit(solution)/shard_map/ppermute | solution.py:239
  68.3 20.3 %collective-permute-start.6 = (bf16[384,1024]{1,0:T(8,128)(2,1)S(1)}, bf16[384,1024]{1,0:T(8,128)(2,1)S(1)}, u32[]{:S(2)}, u32[]{:S(2)}) collective-permute-start(bf16[384,1024]{1,0:T(8,128)(2,1)S(1)} %slice.48), channel_id=1, source_target_pairs={{0,64},{64,128},{128,192},{192,0},{1,65},{65,129},{129,193},{193,1... | collective-permute-start | bytes 2359304 | tf_op jit(solution)/shard_map/ppermute | solution.py:236
  86.2 9.2 %collective-permute-start.3 = (bf16[2,192,1024]{2,1,0:T(8,128)(2,1)S(1)}, bf16[2,192,1024]{2,1,0:T(8,128)(2,1)S(1)}, u32[]{:S(2)}, u32[]{:S(2)}) collective-permute-start(bf16[2,192,1024]{2,1,0:T(8,128)(2,1)S(1)} %get-tuple-element.14), channel_id=1, source_target_pairs={{0,1},{1,0},{2,3},{3,2},{4,5},{5,4},{6,7},{7,6},{8,9},{9,8},{10,11... | collective-permute-start | bytes 2359304 | tf_op jit(solution)/shard_map/ppermute | solution.py:258
  92.2 6.2 %collective-permute-start.8 = (bf16[2,192,1024]{2,1,0:T(8,128)(2,1)S(1)}, bf16[2,192,1024]{2,1,0:T(8,128)(2,1)S(1)}, u32[]{:S(2)}, u32[]{:S(2)}) collective-permute-start(bf16[2,192,1024]{2,1,0:T(8,128)(2,1)S(1)} %get-tuple-element.16), channel_id=1, source_target_pairs={{0,1},{1,0},{2,3},{3,2},{4,5},{5,4},{6,7},{7,6},{8,9},{9,8},{10,11... | collective-permute-start | bytes 2359304 | tf_op jit(solution)/shard_map/ppermute | solution.py:258
  95.7 12.6 %collective-permute-start.4 = (bf16[2,96,1024]{2,1,0:T(8,128)(2,1)S(1)}, bf16[2,96,1024]{2,1,0:T(8,128)(2,1)S(1)}, u32[]{:S(2)}, u32[]{:S(2)}) collective-permute-start(bf16[2,96,1024]{2,1,0:T(8,128)(2,1)S(1)} %slice.70), channel_id=1, source_target_pairs={{0,2},{2,0},{4,6},{6,4},{8,10},{10,8},{12,14},{14,12},{1,3},{3,1},... | collective-permute-start | bytes 1179656 | tf_op jit(solution)/shard_map/ppermute | solution.py:260
  98.7 12.3 %collective-permute-start.9 = (bf16[2,96,1024]{2,1,0:T(8,128)(2,1)S(1)}, bf16[2,96,1024]{2,1,0:T(8,128)(2,1)S(1)}, u32[]{:S(2)}, u32[]{:S(2)}) collective-permute-start(bf16[2,96,1024]{2,1,0:T(8,128)(2,1)S(1)} %slice.69), channel_id=1, source_target_pairs={{0,14},{2,4},{4,2},{6,8},{8,6},{10,12},{12,10},{14,0},{1,15},{3,5}... | collective-permute-start | bytes 1179656 | tf_op jit(solution)/shard_map/ppermute | solution.py:260
  112.0 30.8 %all-to-all-start.2 = ((bf16[16,24,1024]{2,1,0:T(8,128)(2,1)}), bf16[16,24,1024]{2,1,0:T(8,128)(2,1)S(1)}, u32[]{:S(2)}, u32[]{:S(2)}) async-start(bf16[16,24,1024]{2,1,0:T(8,128)(2,1)} %bitcast.3), calls=%async_computation.2 | async-start | bytes 1572864 | tf_op jit(solution)/shard_map/all_to_all | solution.py:263
  143.0 16.8 %collective-permute-start.11 = (bf16[24,1024]{1,0:T(8,128)(2,1)S(1)}, bf16[24,1024]{1,0:T(8,128)(2,1)S(1)}, u32[]{:S(2)}, u32[]{:S(2)}) collective-permute-start(bf16[24,1024]{1,0:T(8,128)(2,1)S(1)} %reduce_sum.12), channel_id=1, source_target_pairs={{0,0},{1,1},{2,2},{3,3},{4,4},{5,21},{6,22},{7,23},{8,24},{9,25},{... | collective-permute-start | bytes 147464 | tf_op jit(solution)/shard_map/ppermute | solution.py:269
  151.1 8.7 %collective-permute-start.10 = (bf16[8,1024]{1,0:T(8,128)(2,1)S(1)}, bf16[8,1024]{1,0:T(8,128)(2,1)S(1)}, u32[]{:S(2)}, u32[]{:S(2)}) collective-permute-start(bf16[8,1024]{1,0:T(8,128)(2,1)S(1)} %slice_select_fusion.2), channel_id=1, source_target_pairs={{5,5},{10,42},{21,69},{26,106},{37,197},{42,234},{53,133},{58,170}... | collective-permute-start | bytes 49160 | tf_op jit(solution)/shard_map/ppermute | solution.py:270

commit v8 on v7

--- a/solution.py
+++ b/solution.py
@@ -137,31 +137,37 @@
     return total
 
 
-def product_kernel(counts, acts_ref, *refs):
-    *pieces, other_ref, mine_ref = refs
-    start = 0
+def first_kernel(acts_ref, near_0_ref, near_1_ref, far_ref, other_ref, mine_ref, far_other_ref, far_mine_ref):
     acts = acts_ref[...]
-    for at, count in enumerate(counts):
-        product = accumulate(acts, pieces[start : start + count])
-        other_ref[at] = product[:192].astype(jnp.bfloat16)
-        mine_ref[at] = product[192:]
-        start += count
-
-
-def products(acts, weights):
-    flat = [piece for weight in weights for piece in weight]
-    counts = tuple(len(weight) for weight in weights)
-    return pl.pallas_call(
-        lambda *refs: product_kernel(counts, *refs),
-        out_shape=(
-            jax.ShapeDtypeStruct((2, 192, 1024), jnp.bfloat16),
-            jax.ShapeDtypeStruct((2, 192, 1024), jnp.float32),
+    for at, weight_ref in enumerate((near_0_ref, near_1_ref, far_ref)):
+        product = dot(acts, weight_ref[...])
+        if at < 2:
+            other_ref[at] = product[:192].astype(jnp.bfloat16)
+            mine_ref[at] = product[192:]
+        else:
+            far_other_ref[0] = product[:192].astype(jnp.bfloat16)
+            far_mine_ref[0] = product[192:]
+
+
+def last_kernel(acts_ref, top_ref, low_ref, far_other_in, far_mine_in, far_other_ref, far_mine_ref):
+    product = accumulate(acts_ref[...], (top_ref, low_ref))
+    far_other_ref[0] = far_other_in[0]
+    far_mine_ref[0] = far_mine_in[0]
+    far_other_ref[1] = product[:192].astype(jnp.bfloat16)
+    far_mine_ref[1] = product[192:]
+
+
+def products(kernel, shapes, operands, flops):
+    return pl.pallas_call(
+        kernel,
+        out_shape=tuple(
+            jax.ShapeDtypeStruct((count, 192, 1024), kind) for count in shapes for kind in (jnp.bfloat16, jnp.float32)
         ),
-        in_specs=[pl.BlockSpec(memory_space=pltpu.VMEM)] * (1 + len(flat)),
-        out_specs=(pl.BlockSpec(memory_space=pltpu.VMEM),) * 2,
+        in_specs=[pl.BlockSpec(memory_space=pltpu.VMEM)] * len(operands),
+        out_specs=(pl.BlockSpec(memory_space=pltpu.VMEM),) * (2 * len(shapes)),
         compiler_params=pltpu.CompilerParams(vmem_limit_bytes=32 * 1024 * 1024),
-        cost_estimate=pl.CostEstimate(flops=1_300_000_000, bytes_accessed=6_000_000, transcendentals=0),
-    )(acts, *flat)
+        cost_estimate=pl.CostEstimate(flops=flops, bytes_accessed=6_000_000, transcendentals=0),
+    )(*operands)
 
 
 def arrange_kernel(source_ref, own_ref, next_1_ref, next_2_ref, out_ref):
@@ -186,8 +192,9 @@
 
 
 def quantize_weight(weight_matrix, weight_exponent):
-    scaling = jnp.exp2(weight_exponent.astype(jnp.float32)).astype(jnp.bfloat16).astype(jnp.float32)[None, :]
-    clipped = jnp.clip(weight_matrix.astype(jnp.float32) / scaling, -7.5, 7.5)
+    coarse = (weight_exponent == -8)[None, :]
+    scaling = jnp.where(coarse, 2.0**-8, 2.0**-9)
+    clipped = jnp.clip(weight_matrix.astype(jnp.float32) * jnp.where(coarse, 2.0**8, 2.0**9), -7.5, 7.5)
     return (soft_round(clipped) * scaling).astype(jnp.bfloat16)
 
 
@@ -252,13 +259,20 @@
 
     y_pairs_near = [(y, y ^ 1) for y in range(8)]
     y_pairs_far = [(y, (y - 1) % 8 if y % 2 == 0 else (y + 1) % 8) for y in range(8)]
-    parts = []
-    for weights, y_pairs in ((((weight_0,), (weight_1,)), y_pairs_near), (((weight_3,), weight_2), y_pairs_far)):
-        other, own_rows = products(acts, weights)
-        from_core = lax.ppermute(other, "c", [(0, 1), (1, 0)])
-        mine = own_rows + from_core.astype(jnp.float32)
+    def over_core(other, own_rows):
+        return own_rows + lax.ppermute(other, "c", [(0, 1), (1, 0)]).astype(jnp.float32)
+
+    def over_y(mine, y_pairs):
         from_y = lax.ppermute(mine[:, :96].astype(jnp.bfloat16), ("yh", "yl"), y_pairs)
-        parts.append((mine[:, 96:] + from_y.astype(jnp.float32)).astype(jnp.bfloat16))
+        return (mine[:, 96:] + from_y.astype(jnp.float32)).astype(jnp.bfloat16)
+
+    other, own_rows, far_other, far_rows = products(
+        first_kernel, (2, 1), (acts, weight_0, weight_1, weight_3), 1_300_000_000
+    )
+    near = over_core(other, own_rows)
+    far_other, far_rows = products(last_kernel, (2,), (acts, *weight_2, far_other, far_rows), 1_300_000_000)
+    far = over_core(far_other, far_rows)
+    parts = [over_y(near, y_pairs_near), over_y(far, y_pairs_far)]
     sums = jnp.concatenate(parts, axis=0).reshape(16, 24, 1024)
     crossed = lax.all_to_all(sums, ("l", "yh"), split_axis=0, concat_axis=0, tiled=True)
     total = jnp.sum(crossed.astype(jnp.float32), axis=0).astype(jnp.bfloat16)

time: 161 us -> 160 us (level)
  the two profiles are of different devices: /device:TPU:21 before, /device:TPU:40 now
where the time goes in v8:
time: 160 us; the launch traced here: 159 us
  starting transfers between devices  75 us (47%)
  waiting for transfers between devices  43.5 us (27%)
  blocking collectives  19.4 us (12%)
  Pallas kernels  9.86 us (6%)
  other arithmetic  7.37 us (5%)
  local copies, waits for them, and re-layouts  3.64 us (2%)
    all_to_all x1, blocking collectives, shards(): lax.all_to_all(quantized, TENSOR, split_axis=0, concat_axis=0, tiled=True)  19.4 us
    all_to_all x1, waiting for transfers between devices, shards(): lax.all_to_all(sums, ('l', 'yh'), split_axis=0, concat_axis=0, tiled=True)  17.9 us
    all_to_all x1, starting transfers between devices, shards(): lax.all_to_all(sums, ('l', 'yh'), split_axis=0, concat_axis=0, tiled=True)  14.3 us
    all_to_all x1, starting transfers between devices, shards(): lax.all_to_all(packed, TENSOR, split_axis=0, concat_axis=0, tiled=True)  13.9 us
    ppermute x1, starting transfers between devices, shards(): next_1 = lax.ppermute(own, 'h', ring(3, -1))  11.8 us
    ppermute x2, waiting for transfers between devices, over_y(): lax.ppermute(mine[:, :96].astype(jnp.bfloat16), ('yh', 'yl'), y_pairs)  9.56 us
    ppermute x2, starting transfers between devices, to_left(): return lax.ppermute(rows, 'x', ring(4, -1))  9.18 us
    ppermute x1, waiting for transfers between devices, shards(): next_1 = lax.ppermute(own, 'h', ring(3, -1))  9.12 us
  transfers between devices with their start and end apart: 14, of which 7 were waited for; matrix products, arithmetic and copies ran while one was open for 4% of the time, Pallas kernels for 6%

profile of v8, /device:TPU:40, one launch (start us, length us, event | category | flops | bytes accessed | tf_op | source)
XLA Modules:
  0.0 159.1 jit_solution(10443988514713071575)
XLA Ops:
  0.0 0.9 copy-done
  0.9 0.7 copy-done.1
  1.6 0.7 copy-done.2
  2.3 1.1 shard_map.73
  3.4 13.9 %all-to-all-start = ((bf16[64,2,896]{2,1,0:T(2,128)(2,1)}), bf16[64,2,896]{2,1,0:T(2,128)(2,1)}, u32[]{:S(2)}, u32[]{:S(2)}) async-start(bf16[64,2,896]{2,1,0:T(2,128)(2,1)} %shard_map.73), calls=%async_computation | async-start | bytes 458752 | tf_op jit(solution)/shard_map/all_to_all | solution.py:252
  17.3 0.7 broadcast_select_fusion.1
  18.0 0.0 copy-start.4
  18.0 3.8 %multiply_convert_fusion.near_0_ref = bf16[832,1024]{1,0:T(8,128)(2,1)S(1)} fusion(bf16[832,1024]{1,0:T(8,128)(2,1)} %param.8, f32[1024]{0:T(1024)S(1)} %broadcast_select_fusion, f32[1024]{0:T(1024)S(1)} %get-tuple-element.21), kind=kLoop, calls=%fused_computation.1 | loop fusion | flops 20447232 | bytes 3416064 | tf_op jit(solution)/shard_map/convert_element_type | solution.py:198
  21.8 4.0 %collective-permute-start.2 = (bf16[832,1024]{1,0:T(8,128)(2,1)S(1)}, bf16[832,1024]{1,0:T(8,128)(2,1)S(1)}, u32[]{:S(2)}, u32[]{:S(2)}) collective-permute-start(bf16[832,1024]{1,0:T(8,128)(2,1)S(1)} %multiply_convert_fusion.near_0_ref), channel_id=1, source_target_pairs={{0,192},{64,0},{128,64},{192,128},{1,193},{65,1},{129,65},{193,129... | collective-permute-start | bytes 5111816 | tf_op jit(solution)/shard_map/ppermute | solution.py:246
  25.8 1.9 %collective-permute-start.3 = (bf16[832,1024]{1,0:T(8,128)(2,1)S(1)}, bf16[832,1024]{1,0:T(8,128)(2,1)}, u32[]{:S(2)}, u32[]{:S(2)}) collective-permute-start(bf16[832,1024]{1,0:T(8,128)(2,1)S(1)} %multiply_convert_fusion.near_0_ref), channel_id=1, source_target_pairs={{0,64},{64,128},{128,192},{192,0},{1,65},{65,129},{129,193},{193,1... | collective-permute-start | bytes 5111816 | tf_op jit(solution)/shard_map/ppermute | solution.py:243
  27.8 0.0 all-to-all-done.x_ref
  27.8 1.8 %shard_map.74 = bf16[64,2,832]{2,1,0:T(2,128)(2,1)S(1)} custom-call(bf16[64,2,896]{2,1,0:T(2,128)(2,1)} %all-to-all-done.x_ref, bf16[128,128]{1,0:T(8,128)(2,1)S(1)} %copy-done.3, bf16[128,128]{1,0:T(8,128)(2,1)S(1)} %copy-done.4), custom_call_target="tpu_custom_call" | custom-call | flops 2000000000 | bytes 1500000 | tf_op jit(solution)/shard_map/pallas_call | solution.py:120
  29.6 19.4 %all_to_all.15.own_ref = bf16[64,2,832]{2,1,0:T(2,128)(2,1)} all-to-all(bf16[64,2,832]{2,1,0:T(2,128)(2,1)S(1)} %shard_map.74), channel_id=1, replica_groups=mesh['h'=3,'x'=4,'l'=4,'yh'=4,'yl'=2,'c'=2] {'l','yh','yl','c'}, dimensions={0} | all-to-all | bytes 425984 | tf_op jit(solution)/shard_map/all_to_all | solution.py:254
  49.0 11.8 %collective-permute-start = (bf16[64,2,832]{2,1,0:T(2,128)(2,1)}, bf16[64,2,832]{2,1,0:T(2,128)(2,1)}, u32[]{:S(2)}, u32[]{:S(2)}) collective-permute-start(bf16[64,2,832]{2,1,0:T(2,128)(2,1)} %all_to_all.15.own_ref), channel_id=1, source_target_pairs={{0,512},{256,0},{512,256},{1,513},{257,1},{513,257},{2,514},{258,2... | collective-permute-start | bytes 638984 | tf_op jit(solution)/shard_map/ppermute | solution.py:255
  60.9 1.9 %collective-permute-start.1 = (bf16[64,2,832]{2,1,0:T(2,128)(2,1)}, bf16[64,2,832]{2,1,0:T(2,128)(2,1)}, u32[]{:S(2)}, u32[]{:S(2)}) collective-permute-start(bf16[64,2,832]{2,1,0:T(2,128)(2,1)} %all_to_all.15.own_ref), channel_id=1, source_target_pairs={{0,256},{256,512},{512,0},{1,257},{257,513},{513,1},{2,258},{258,5... | collective-permute-start | bytes 638984 | tf_op jit(solution)/shard_map/ppermute | solution.py:256
  62.8 0.5 add_select_fusion.source_ref
  63.4 0.0 collective-permute-done.2.near_1_ref
  63.4 0.1 slice.49
  63.5 5.1 %collective-permute-start.7 = (bf16[448,1024]{1,0:T(8,128)(2,1)S(1)}, bf16[448,1024]{1,0:T(8,128)(2,1)S(1)}, u32[]{:S(2)}, u32[]{:S(2)}) collective-permute-start(bf16[448,1024]{1,0:T(8,128)(2,1)S(1)} %slice.49), channel_id=1, source_target_pairs={{0,192},{64,0},{128,64},{192,128},{1,193},{65,1},{129,65},{193,129... | collective-permute-start | bytes 2752520 | tf_op jit(solution)/shard_map/ppermute | solution.py:246
  68.6 0.0 collective-permute-done.3.far_ref
  68.6 1.2 slice.48
  69.8 1.9 %collective-permute-start.6 = (bf16[384,1024]{1,0:T(8,128)(2,1)S(1)}, bf16[384,1024]{1,0:T(8,128)(2,1)S(1)}, u32[]{:S(2)}, u32[]{:S(2)}) collective-permute-start(bf16[384,1024]{1,0:T(8,128)(2,1)S(1)} %slice.48), channel_id=1, source_target_pairs={{0,64},{64,128},{128,192},{192,0},{1,65},{65,129},{129,193},{193,1... | collective-permute-start | bytes 2359304 | tf_op jit(solution)/shard_map/ppermute | solution.py:243
  71.7 9.1 %collective-permute-done.next_1_ref = bf16[64,2,832]{2,1,0:T(2,128)(2,1)} collective-permute-done((bf16[64,2,832]{2,1,0:T(2,128)(2,1)}, bf16[64,2,832]{2,1,0:T(2,128)(2,1)}, u32[]{:S(2)}, u32[]{:S(2)}) %collective-permute-start) | collective-permute-done | bytes 213024 | tf_op jit(solution)/shard_map/ppermute | solution.py:255
  80.8 0.5 collective-permute-done.1.next_2_ref
  81.4 1.9 %shard_map.75.acts_ref = bf16[384,832]{1,0:T(8,128)(2,1)S(1)} custom-call(s32[384,1]{1,0:T(8,128)S(1)} %add_select_fusion.source_ref, bf16[64,2,832]{2,1,0:T(2,128)(2,1)} %all_to_all.15.own_ref, bf16[64,2,832]{2,1,0:T(2,128)(2,1)} %collective-permute-done.next_1_ref, bf16[64,2,832]{2,1,0:T(2,128)(2,1)} %collective-permute-done.1.next_2_ref), custom_call_target="tpu_custom_call" | custom-call | flops 20000000000 | bytes 1500000 | tf_op jit(solution)/shard_map/pallas_call | solution.py:184
  83.3 4.0 %shard_map.76 = (bf16[2,192,1024]{2,1,0:T(8,128)(2,1)S(1)}, f32[2,192,1024]{2,1,0:T(8,128)S(1)}, bf16[1,192,1024]{2,1,0:T(8,128)(2,1)S(1)}, f32[1,192,1024]{2,1,0:T(8,128)S(1)}) custom-call(bf16[384,832]{1,0:T(8,128)(2,1)S(1)} %shard_map.75.acts_ref, bf16[832,1024]{1,0:T(8,128)(2,1)S(1)} %multiply_convert_fusion.near_0_ref, ...), custom_call_target="tpu_custom_call" | custom-call | flops 1300000000 | bytes 6000000 | tf_op jit(solution)/shard_map/pallas_call | solution.py:161
  87.3 1.9 %collective-permute-start.4 = (bf16[2,192,1024]{2,1,0:T(8,128)(2,1)S(1)}, bf16[2,192,1024]{2,1,0:T(8,128)(2,1)S(1)}, u32[]{:S(2)}, u32[]{:S(2)}) collective-permute-start(bf16[2,192,1024]{2,1,0:T(8,128)(2,1)S(1)} %get-tuple-element.16), channel_id=1, source_target_pairs={{0,1},{1,0},{2,3},{3,2},{4,5},{5,4},{6,7},{7,6},{8,9},{9,8},{10,11... | collective-permute-start | bytes 2359304 | tf_op jit(solution)/shard_map/ppermute | solution.py:263
  89.3 2.6 %collective-permute-done.6.top_ref = bf16[384,1024]{1,0:T(8,128)(2,1)S(1)} collective-permute-done((bf16[384,1024]{1,0:T(8,128)(2,1)S(1)}, bf16[384,1024]{1,0:T(8,128)(2,1)S(1)}, u32[]{:S(2)}, u32[]{:S(2)}) %collective-permute-start.6) | collective-permute-done | bytes 786464 | tf_op jit(solution)/shard_map/ppermute | solution.py:243
  91.9 1.0 shard_map.77
  92.9 1.9 %collective-permute-start.8 = (bf16[2,192,1024]{2,1,0:T(8,128)(2,1)S(1)}, bf16[2,192,1024]{2,1,0:T(8,128)(2,1)S(1)}, u32[]{:S(2)}, u32[]{:S(2)}) collective-permute-start(bf16[2,192,1024]{2,1,0:T(8,128)(2,1)S(1)} %get-tuple-element.20), channel_id=1, source_target_pairs={{0,1},{1,0},{2,3},{3,2},{4,5},{5,4},{6,7},{7,6},{8,9},{9,8},{10,11... | collective-permute-start | bytes 2359304 | tf_op jit(solution)/shard_map/ppermute | solution.py:263
  94.8 0.2 convert_add_fusion.1
  95.1 0.1 slice.70
  95.1 2.7 %collective-permute-start.5 = (bf16[2,96,1024]{2,1,0:T(8,128)(2,1)S(1)}, bf16[2,96,1024]{2,1,0:T(8,128)(2,1)S(1)}, u32[]{:S(2)}, u32[]{:S(2)}) collective-permute-start(bf16[2,96,1024]{2,1,0:T(8,128)(2,1)S(1)} %slice.70), channel_id=1, source_target_pairs={{0,2},{2,0},{4,6},{6,4},{8,10},{10,8},{12,14},{14,12},{1,3},{3,1},... | collective-permute-start | bytes 1179656 | tf_op jit(solution)/shard_map/ppermute | solution.py:266
  97.8 0.0 collective-permute-done.8
  97.9 0.2 convert_add_fusion
  98.1 3.5 %collective-permute-start.9 = (bf16[2,96,1024]{2,1,0:T(8,128)(2,1)S(1)}, bf16[2,96,1024]{2,1,0:T(8,128)(2,1)S(1)}, u32[]{:S(2)}, u32[]{:S(2)}) collective-permute-start(bf16[2,96,1024]{2,1,0:T(8,128)(2,1)S(1)} %slice.69), channel_id=1, source_target_pairs={{0,14},{2,4},{4,2},{6,8},{8,6},{10,12},{12,10},{14,0},{1,15},{3,5}... | collective-permute-start | bytes 1179656 | tf_op jit(solution)/shard_map/ppermute | solution.py:266
  101.6 6.9 %collective-permute-done.5 = bf16[2,96,1024]{2,1,0:T(8,128)(2,1)S(1)} collective-permute-done((bf16[2,96,1024]{2,1,0:T(8,128)(2,1)S(1)}, bf16[2,96,1024]{2,1,0:T(8,128)(2,1)S(1)}, u32[]{:S(2)}, u32[]{:S(2)}) %collective-permute-start.5) | collective-permute-done | bytes 393248 | tf_op jit(solution)/shard_map/ppermute | solution.py:266
  108.5 0.1 fusion.6
  108.6 2.6 %collective-permute-done.9 = bf16[2,96,1024]{2,1,0:T(8,128)(2,1)S(1)} collective-permute-done((bf16[2,96,1024]{2,1,0:T(8,128)(2,1)S(1)}, bf16[2,96,1024]{2,1,0:T(8,128)(2,1)S(1)}, u32[]{:S(2)}, u32[]{:S(2)}) %collective-permute-start.9) | collective-permute-done | bytes 393248 | tf_op jit(solution)/shard_map/ppermute | solution.py:266
  111.3 0.1 fusion.5
  111.4 1.0 pad_maximum_fusion
  112.3 14.3 %all-to-all-start.2 = ((bf16[16,24,1024]{2,1,0:T(8,128)(2,1)}), bf16[16,24,1024]{2,1,0:T(8,128)(2,1)S(1)}, u32[]{:S(2)}, u32[]{:S(2)}) async-start(bf16[16,24,1024]{2,1,0:T(8,128)(2,1)} %bitcast.3), calls=%async_computation.2 | async-start | bytes 1572864 | tf_op jit(solution)/shard_map/all_to_all | solution.py:277
  126.6 17.9 %all-to-all-done.2 = bf16[16,24,1024]{2,1,0:T(8,128)(2,1)S(1)} async-done(((bf16[16,24,1024]{2,1,0:T(8,128)(2,1)}), bf16[16,24,1024]{2,1,0:T(8,128)(2,1)S(1)}, u32[]{:S(2)}, u32[]{:S(2)}) %all-to-all-start.2) | async-done | bytes 786464 | tf_op jit(solution)/shard_map/all_to_all | solution.py:277
  144.5 0.1 reduce_sum.12
  144.6 4.0 %collective-permute-start.11 = (bf16[24,1024]{1,0:T(8,128)(2,1)S(1)}, bf16[24,1024]{1,0:T(8,128)(2,1)S(1)}, u32[]{:S(2)}, u32[]{:S(2)}) collective-permute-start(bf16[24,1024]{1,0:T(8,128)(2,1)S(1)} %reduce_sum.12), channel_id=1, source_target_pairs={{0,0},{1,1},{2,2},{3,3},{4,4},{5,21},{6,22},{7,23},{8,24},{9,25},{... | collective-permute-start | bytes 147464 | tf_op jit(solution)/shard_map/ppermute | solution.py:283
  148.6 6.0 %collective-permute-start.10 = (bf16[8,1024]{1,0:T(8,128)(2,1)S(1)}, bf16[8,1024]{1,0:T(8,128)(2,1)S(1)}, u32[]{:S(2)}, u32[]{:S(2)}) collective-permute-start(bf16[8,1024]{1,0:T(8,128)(2,1)S(1)} %slice_select_fusion.2), channel_id=1, source_target_pairs={{5,5},{10,42},{21,69},{26,106},{37,197},{42,234},{53,133},{58,170}... | collective-permute-start | bytes 49160 | tf_op jit(solution)/shard_map/ppermute | solution.py:284
  154.7 3.8 %collective-permute-done.10 = bf16[8,1024]{1,0:T(8,128)(2,1)S(1)} collective-permute-done((bf16[8,1024]{1,0:T(8,128)(2,1)S(1)}, bf16[8,1024]{1,0:T(8,128)(2,1)S(1)}, u32[]{:S(2)}, u32[]{:S(2)}) %collective-permute-start.10) | collective-permute-done | bytes 16416 | tf_op jit(solution)/shard_map/ppermute | solution.py:284
  158.5 0.6 pad_maximum_fusion.1
  (13 shorter events, 0.1 us)
Async XLA Ops:
  0.0 0.9 copy-start
  0.9 0.7 copy-start.1
  1.6 0.7 copy-start.2
  3.4 24.4 %all-to-all-start = ((bf16[64,2,896]{2,1,0:T(2,128)(2,1)}), bf16[64,2,896]{2,1,0:T(2,128)(2,1)}, u32[]{:S(2)}, u32[]{:S(2)}) async-start(bf16[64,2,896]{2,1,0:T(2,128)(2,1)} %shard_map.73), calls=%async_computation | async-start | bytes 458752 | tf_op jit(solution)/shard_map/all_to_all | solution.py:252
  18.0 9.8 %copy-start.3 = (bf16[128,128]{1,0:T(8,128)(2,1)S(1)}, bf16[128,128]{1,0:T(8,128)(2,1)}, u32[]{:S(2)}) copy-start(bf16[128,128]{1,0:T(8,128)(2,1)} %constant.122.clone.rows_ref) | copy-start | bytes 98308
  18.0 9.8 %copy-start.4 = (bf16[128,128]{1,0:T(8,128)(2,1)S(1)}, bf16[128,128]{1,0:T(8,128)(2,1)}, u32[]{:S(2)}) copy-start(bf16[128,128]{1,0:T(8,128)(2,1)} %constant.123.clone.lanes_ref) | copy-start | bytes 98308
  21.8 41.6 %collective-permute-start.2 = (bf16[832,1024]{1,0:T(8,128)(2,1)S(1)}, bf16[832,1024]{1,0:T(8,128)(2,1)S(1)}, u32[]{:S(2)}, u32[]{:S(2)}) collective-permute-start(bf16[832,1024]{1,0:T(8,128)(2,1)S(1)} %multiply_convert_fusion.near_0_ref), channel_id=1, source_target_pairs={{0,192},{64,0},{128,64},{192,128},{1,193},{65,1},{129,65},{193,129... | collective-permute-start | bytes 5111816 | tf_op jit(solution)/shard_map/ppermute | solution.py:246
  25.8 42.8 %collective-permute-start.3 = (bf16[832,1024]{1,0:T(8,128)(2,1)S(1)}, bf16[832,1024]{1,0:T(8,128)(2,1)}, u32[]{:S(2)}, u32[]{:S(2)}) collective-permute-start(bf16[832,1024]{1,0:T(8,128)(2,1)S(1)} %multiply_convert_fusion.near_0_ref), channel_id=1, source_target_pairs={{0,64},{64,128},{128,192},{192,0},{1,65},{65,129},{129,193},{193,1... | collective-permute-start | bytes 5111816 | tf_op jit(solution)/shard_map/ppermute | solution.py:243
  49.0 31.8 %collective-permute-start = (bf16[64,2,832]{2,1,0:T(2,128)(2,1)}, bf16[64,2,832]{2,1,0:T(2,128)(2,1)}, u32[]{:S(2)}, u32[]{:S(2)}) collective-permute-start(bf16[64,2,832]{2,1,0:T(2,128)(2,1)} %all_to_all.15.own_ref), channel_id=1, source_target_pairs={{0,512},{256,0},{512,256},{1,513},{257,1},{513,257},{2,514},{258,2... | collective-permute-start | bytes 638984 | tf_op jit(solution)/shard_map/ppermute | solution.py:255
  60.9 20.5 %collective-permute-start.1 = (bf16[64,2,832]{2,1,0:T(2,128)(2,1)}, bf16[64,2,832]{2,1,0:T(2,128)(2,1)}, u32[]{:S(2)}, u32[]{:S(2)}) collective-permute-start(bf16[64,2,832]{2,1,0:T(2,128)(2,1)} %all_to_all.15.own_ref), channel_id=1, source_target_pairs={{0,256},{256,512},{512,0},{1,257},{257,513},{513,1},{2,258},{258,5... | collective-permute-start | bytes 638984 | tf_op jit(solution)/shard_map/ppermute | solution.py:256
  63.5 28.4 %collective-permute-start.7 = (bf16[448,1024]{1,0:T(8,128)(2,1)S(1)}, bf16[448,1024]{1,0:T(8,128)(2,1)S(1)}, u32[]{:S(2)}, u32[]{:S(2)}) collective-permute-start(bf16[448,1024]{1,0:T(8,128)(2,1)S(1)} %slice.49), channel_id=1, source_target_pairs={{0,192},{64,0},{128,64},{192,128},{1,193},{65,1},{129,65},{193,129... | collective-permute-start | bytes 2752520 | tf_op jit(solution)/shard_map/ppermute | solution.py:246
  69.8 22.1 %collective-permute-start.6 = (bf16[384,1024]{1,0:T(8,128)(2,1)S(1)}, bf16[384,1024]{1,0:T(8,128)(2,1)S(1)}, u32[]{:S(2)}, u32[]{:S(2)}) collective-permute-start(bf16[384,1024]{1,0:T(8,128)(2,1)S(1)} %slice.48), channel_id=1, source_target_pairs={{0,64},{64,128},{128,192},{192,0},{1,65},{65,129},{129,193},{193,1... | collective-permute-start | bytes 2359304 | tf_op jit(solution)/shard_map/ppermute | solution.py:243
  87.3 7.5 %collective-permute-start.4 = (bf16[2,192,1024]{2,1,0:T(8,128)(2,1)S(1)}, bf16[2,192,1024]{2,1,0:T(8,128)(2,1)S(1)}, u32[]{:S(2)}, u32[]{:S(2)}) collective-permute-start(bf16[2,192,1024]{2,1,0:T(8,128)(2,1)S(1)} %get-tuple-element.16), channel_id=1, source_target_pairs={{0,1},{1,0},{2,3},{3,2},{4,5},{5,4},{6,7},{7,6},{8,9},{9,8},{10,11... | collective-permute-start | bytes 2359304 | tf_op jit(solution)/shard_map/ppermute | solution.py:263
  92.9 4.9 %collective-permute-start.8 = (bf16[2,192,1024]{2,1,0:T(8,128)(2,1)S(1)}, bf16[2,192,1024]{2,1,0:T(8,128)(2,1)S(1)}, u32[]{:S(2)}, u32[]{:S(2)}) collective-permute-start(bf16[2,192,1024]{2,1,0:T(8,128)(2,1)S(1)} %get-tuple-element.20), channel_id=1, source_target_pairs={{0,1},{1,0},{2,3},{3,2},{4,5},{5,4},{6,7},{7,6},{8,9},{9,8},{10,11... | collective-permute-start | bytes 2359304 | tf_op jit(solution)/shard_map/ppermute | solution.py:263
  95.1 13.4 %collective-permute-start.5 = (bf16[2,96,1024]{2,1,0:T(8,128)(2,1)S(1)}, bf16[2,96,1024]{2,1,0:T(8,128)(2,1)S(1)}, u32[]{:S(2)}, u32[]{:S(2)}) collective-permute-start(bf16[2,96,1024]{2,1,0:T(8,128)(2,1)S(1)} %slice.70), channel_id=1, source_target_pairs={{0,2},{2,0},{4,6},{6,4},{8,10},{10,8},{12,14},{14,12},{1,3},{3,1},... | collective-permute-start | bytes 1179656 | tf_op jit(solution)/shard_map/ppermute | solution.py:266
  98.1 13.1 %collective-permute-start.9 = (bf16[2,96,1024]{2,1,0:T(8,128)(2,1)S(1)}, bf16[2,96,1024]{2,1,0:T(8,128)(2,1)S(1)}, u32[]{:S(2)}, u32[]{:S(2)}) collective-permute-start(bf16[2,96,1024]{2,1,0:T(8,128)(2,1)S(1)} %slice.69), channel_id=1, source_target_pairs={{0,14},{2,4},{4,2},{6,8},{8,6},{10,12},{12,10},{14,0},{1,15},{3,5}... | collective-permute-start | bytes 1179656 | tf_op jit(solution)/shard_map/ppermute | solution.py:266
  112.3 32.1 %all-to-all-start.2 = ((bf16[16,24,1024]{2,1,0:T(8,128)(2,1)}), bf16[16,24,1024]{2,1,0:T(8,128)(2,1)S(1)}, u32[]{:S(2)}, u32[]{:S(2)}) async-start(bf16[16,24,1024]{2,1,0:T(8,128)(2,1)} %bitcast.3), calls=%async_computation.2 | async-start | bytes 1572864 | tf_op jit(solution)/shard_map/all_to_all | solution.py:277
  144.6 13.9 %collective-permute-start.11 = (bf16[24,1024]{1,0:T(8,128)(2,1)S(1)}, bf16[24,1024]{1,0:T(8,128)(2,1)S(1)}, u32[]{:S(2)}, u32[]{:S(2)}) collective-permute-start(bf16[24,1024]{1,0:T(8,128)(2,1)S(1)} %reduce_sum.12), channel_id=1, source_target_pairs={{0,0},{1,1},{2,2},{3,3},{4,4},{5,21},{6,22},{7,23},{8,24},{9,25},{... | collective-permute-start | bytes 147464 | tf_op jit(solution)/shard_map/ppermute | solution.py:283
  148.6 9.8 %collective-permute-start.10 = (bf16[8,1024]{1,0:T(8,128)(2,1)S(1)}, bf16[8,1024]{1,0:T(8,128)(2,1)S(1)}, u32[]{:S(2)}, u32[]{:S(2)}) collective-permute-start(bf16[8,1024]{1,0:T(8,128)(2,1)S(1)} %slice_select_fusion.2), channel_id=1, source_target_pairs={{5,5},{10,42},{21,69},{26,106},{37,197},{42,234},{53,133},{58,170}... | collective-permute-start | bytes 49160 | tf_op jit(solution)/shard_map/ppermute | solution.py:284

commit v9 on v8

--- a/solution.py
+++ b/solution.py
@@ -123,7 +123,7 @@
         in_specs=[pl.BlockSpec(memory_space=pltpu.VMEM)] * 3,
         out_specs=pl.BlockSpec(memory_space=pltpu.VMEM),
         compiler_params=pltpu.CompilerParams(vmem_limit_bytes=24 * 1024 * 1024),
-        cost_estimate=pl.CostEstimate(flops=2_000_000_000, bytes_accessed=1_500_000, transcendentals=0),
+        cost_estimate=pl.CostEstimate(flops=20_000_000_000, bytes_accessed=1_500_000, transcendentals=0),
     )(arrived, jnp.asarray(np.kron(walsh(64), np.eye(2)), jnp.bfloat16), jnp.asarray(lanes, jnp.bfloat16))
 
 
@@ -135,6 +135,20 @@
         total = term if total is None else total + term
         start = stop
     return total
+
+
+def take_rows(weight, start, stop):
+    def kernel(weight_ref, out_ref):
+        out_ref[...] = weight_ref[start:stop]
+
+    return pl.pallas_call(
+        kernel,
+        out_shape=jax.ShapeDtypeStruct((stop - start, 1024), jnp.bfloat16),
+        in_specs=[pl.BlockSpec(memory_space=pltpu.VMEM)],
+        out_specs=pl.BlockSpec(memory_space=pltpu.VMEM),
+        compiler_params=pltpu.CompilerParams(vmem_limit_bytes=8 * 1024 * 1024),
+        cost_estimate=pl.CostEstimate(flops=20_000_000_000, bytes_accessed=1_700_000, transcendentals=0),
+    )(weight)
 
 
 def first_kernel(acts_ref, near_0_ref, near_1_ref, far_ref, other_ref, mine_ref, far_other_ref, far_mine_ref):
@@ -170,25 +184,25 @@
     )(*operands)
 
 
-def arrange_kernel(source_ref, own_ref, next_1_ref, next_2_ref, out_ref):
+def arrange_kernel(source_ref, rows_ref, out_ref):
     column = lax.broadcasted_iota(jnp.int32, (384, 128), 1)
     source = source_ref[...]
     total = None
-    for at, rows_ref in enumerate((own_ref, next_1_ref, next_2_ref)):
-        term = dot(ones_where(source == column + 128 * at), rows_ref[...].reshape(128, 832))
+    for at in range(3):
+        term = dot(ones_where(source == column + 128 * at), rows_ref[at].reshape(128, 832))
         total = term if total is None else total + term
     out_ref[...] = total.astype(jnp.bfloat16)
 
 
-def arrange(source, own, next_1, next_2):
+def arrange(source, rows):
     return pl.pallas_call(
         arrange_kernel,
         out_shape=jax.ShapeDtypeStruct((384, 832), jnp.bfloat16),
-        in_specs=[pl.BlockSpec(memory_space=pltpu.VMEM)] * 4,
+        in_specs=[pl.BlockSpec(memory_space=pltpu.VMEM)] * 2,
         out_specs=pl.BlockSpec(memory_space=pltpu.VMEM),
         compiler_params=pltpu.CompilerParams(vmem_limit_bytes=16 * 1024 * 1024),
         cost_estimate=pl.CostEstimate(flops=20000000000, bytes_accessed=1_500_000, transcendentals=0),
-    )(source, own, next_1, next_2)
+    )(source, rows)
 
 
 def quantize_weight(weight_matrix, weight_exponent):
@@ -224,7 +238,7 @@
     return pairs
 
 
-def row_order(h, x, y_low, c):
+def row_order(x, y_low, c):
     at = lax.broadcasted_iota(jnp.int32, (384, 1), 0)
     core = jnp.where(at < 192, 1 - c, c)
     rest = at % 192
@@ -232,11 +246,11 @@
     rest = rest % 96
     y = 2 * (rest // 24) + parity
     row = (2 * y + core) * 24 + rest % 24
-    return (row - 128 * ((h + x) % 3) + 384) % 384
+    return row % 128 + 128 * ((row // 128 - x + 6) % 3)
 
 
 def shards(hidden, down_weight, act_exponent, clip_index, weight_exponent):
-    h, x, y_low, c = (lax.axis_index(name) for name in ("h", "x", "yl", "c"))
+    x, y_low, c = (lax.axis_index(name) for name in ("x", "yl", "c"))
     y_high = lax.axis_index("yh")
 
     def to_right(rows):
@@ -252,10 +266,11 @@
     arrived = lax.all_to_all(packed, TENSOR, split_axis=0, concat_axis=0, tiled=True)
     quantized = rotate_and_quantize(arrived)
     own = lax.all_to_all(quantized, TENSOR, split_axis=0, concat_axis=0, tiled=True)
-    next_1 = lax.ppermute(own, "h", ring(3, -1))
-    next_2 = lax.ppermute(own, "h", ring(3, 1))
-    weight_2 = (to_right(weight_3[:SPLIT]), to_left(weight_1[SPLIT:]))
-    acts = arrange(row_order(h, x, y_low, c), own, next_1, next_2)
+    rows = lax.all_to_all(
+        jnp.broadcast_to(own[None], (3, 64, 2, 832)), "h", split_axis=0, concat_axis=0, tiled=True
+    )
+    weight_2 = (to_right(take_rows(weight_3, 0, SPLIT)), to_left(take_rows(weight_1, SPLIT, 832)))
+    acts = arrange(row_order(x, y_low, c), rows)
 
     y_pairs_near = [(y, y ^ 1) for y in range(8)]
     y_pairs_far = [(y, (y - 1) % 8 if y % 2 == 0 else (y + 1) % 8) for y in range(8)]

time: 160 us -> 173 us (1.081)
  waiting for transfers between devices: 43.5 us -> 67.9 us
  blocking collectives: 19.4 us -> 0 us
  Pallas kernels: 9.86 us -> 14.7 us
  local copies, waits for them, and re-layouts: 3.64 us -> 6.16 us
    all_to_all x0 -> x2, starting transfers between devices: none -> 21.9 us  [the longest x1 11.2 us: shards(): lax.all_to_all(jnp.broadcast_to(own[None], (3, 64, 2, 832)), 'h', split_a...]
    ppermute x2, waiting for transfers between devices: 2.65 us -> 22.4 us  [to_right(): return lax.ppermute(rows, 'x', ring(4, 1))]
    all_to_all x1 -> x0, blocking collectives: 19.4 us -> none  [shards(): lax.all_to_all(quantized, TENSOR, split_axis=0, concat_axis=0, tiled=True)]
    ppermute x2 -> x0, starting transfers between devices: 13.8 us -> none  [the longest x1 11.8 us: shards(): next_1 = lax.ppermute(own, 'h', ring(3, -1))]
    ppermute x2 -> x0, waiting for transfers between devices: 9.63 us -> none  [the longest x1 9.12 us: shards(): next_1 = lax.ppermute(own, 'h', ring(3, -1))]
    all_to_all x0 -> x2, waiting for transfers between devices: none -> 7.07 us  [the longest x1 5.42 us: shards(): lax.all_to_all(quantized, TENSOR, split_axis=0, concat_axis=0, tiled=True)]
    all_to_all x1, starting transfers between devices: 14.3 us -> 10.2 us  [shards(): lax.all_to_all(sums, ('l', 'yh'), split_axis=0, concat_axis=0, tiled=True)]
    ppermute x1, waiting for transfers between devices: 3.78 us -> 7.46 us  [shards(): lax.ppermute(jnp.where(early, total[:8], total[16:]), ('x', 'l', 'yh', 'y...]
  transfers between devices with their start and end apart: 14 -> 14, of which waited for: 7 -> 10; matrix products, arithmetic and copies ran while one was open for 4% -> 5% of each run, Pallas kernels for 6% -> 8%
where the time goes in v9:
time: 173 us; the launch traced here: 172 us
  starting transfers between devices  74.4 us (43%)
  waiting for transfers between devices  67.9 us (39%)
  Pallas kernels  14.7 us (8%)
  other arithmetic  8.24 us (5%)
  local copies, waits for them, and re-layouts  6.16 us (4%)
    ppermute x2, waiting for transfers between devices, to_right(): return lax.ppermute(rows, 'x', ring(4, 1))  22.4 us
    all_to_all x1, waiting for transfers between devices, shards(): lax.all_to_all(sums, ('l', 'yh'), split_axis=0, concat_axis=0, tiled=True)  18.1 us
    all_to_all x1, starting transfers between devices, shards(): lax.all_to_all(packed, TENSOR, split_axis=0, concat_axis=0, tiled=True)  13.9 us
    all_to_all x1, starting transfers between devices, shards(): lax.all_to_all(jnp.broadcast_to(own[None], (3, 64, 2, 832)), 'h', split_a...  11.2 us
    ppermute x2, waiting for transfers between devices, over_y(): lax.ppermute(mine[:, :96].astype(jnp.bfloat16), ('yh', 'yl'), y_pairs)  11.1 us
    all_to_all x1, starting transfers between devices, shards(): lax.all_to_all(quantized, TENSOR, split_axis=0, concat_axis=0, tiled=True)  10.7 us
    all_to_all x1, starting transfers between devices, shards(): lax.all_to_all(sums, ('l', 'yh'), split_axis=0, concat_axis=0, tiled=True)  10.2 us
    ppermute x2, starting transfers between devices, to_left(): return lax.ppermute(rows, 'x', ring(4, -1))  9.27 us
  transfers between devices with their start and end apart: 14, of which 10 were waited for; matrix products, arithmetic and copies ran while one was open for 5% of the time, Pallas kernels for 8%

profile of v9, /device:TPU:40, one launch (start us, length us, event | category | flops | bytes accessed | tf_op | source)
XLA Modules:
  0.0 171.6 jit_solution(11951807069073015834)
XLA Ops:
  0.0 0.9 copy-done.1
  0.9 0.7 copy-done.3
  1.6 0.7 copy-done.4
  2.3 1.1 shard_map.73
  3.4 13.9 %all-to-all-start = ((bf16[64,2,896]{2,1,0:T(2,128)(2,1)}), bf16[64,2,896]{2,1,0:T(2,128)(2,1)}, u32[]{:S(2)}, u32[]{:S(2)}) async-start(bf16[64,2,896]{2,1,0:T(2,128)(2,1)} %shard_map.73), calls=%async_computation | async-start | bytes 458752 | tf_op jit(solution)/shard_map/all_to_all | solution.py:266
  17.3 0.7 broadcast_select_fusion.1
  18.0 0.0 copy-start.6
  18.0 3.8 %multiply_convert_fusion.near_0_ref = bf16[832,1024]{1,0:T(8,128)(2,1)S(1)} fusion(bf16[832,1024]{1,0:T(8,128)(2,1)} %param.8, f32[1024]{0:T(1024)S(1)} %broadcast_select_fusion, f32[1024]{0:T(1024)S(1)} %get-tuple-element.21), kind=kLoop, calls=%fused_computation.1 | loop fusion | flops 20447232 | bytes 3416064 | tf_op jit(solution)/shard_map/convert_element_type | solution.py:212
  21.8 4.0 %collective-permute-start = (bf16[832,1024]{1,0:T(8,128)(2,1)S(1)}, bf16[832,1024]{1,0:T(8,128)(2,1)S(1)}, u32[]{:S(2)}, u32[]{:S(2)}) collective-permute-start(bf16[832,1024]{1,0:T(8,128)(2,1)S(1)} %multiply_convert_fusion.near_0_ref), channel_id=1, source_target_pairs={{0,192},{64,0},{128,64},{192,128},{1,193},{65,1},{129,65},{193,129... | collective-permute-start | bytes 5111816 | tf_op jit(solution)/shard_map/ppermute | solution.py:260
  25.9 0.2 all-to-all-done.x_ref
  26.1 1.8 %shard_map.74 = bf16[64,2,832]{2,1,0:T(2,128)(2,1)S(1)} custom-call(bf16[64,2,896]{2,1,0:T(2,128)(2,1)} %all-to-all-done.x_ref, bf16[128,128]{1,0:T(8,128)(2,1)S(1)} %copy-done.5, bf16[128,128]{1,0:T(8,128)(2,1)S(1)} %copy-done.6), custom_call_target="tpu_custom_call" | custom-call | flops 20000000000 | bytes 1500000 | tf_op jit(solution)/shard_map/pallas_call | solution.py:120
  27.9 0.7 copy-done
  28.6 10.7 %all-to-all-start.1 = ((bf16[64,2,832]{2,1,0:T(2,128)(2,1)}), bf16[64,2,832]{2,1,0:T(2,128)(2,1)}, u32[]{:S(2)}, u32[]{:S(2)}) async-start(bf16[64,2,832]{2,1,0:T(2,128)(2,1)} %copy-done), calls=%async_computation.1 | async-start | bytes 458752 | tf_op jit(solution)/shard_map/all_to_all | solution.py:268
  39.3 1.9 %collective-permute-start.1 = (bf16[832,1024]{1,0:T(8,128)(2,1)S(1)}, bf16[832,1024]{1,0:T(8,128)(2,1)}, u32[]{:S(2)}, u32[]{:S(2)}) collective-permute-start(bf16[832,1024]{1,0:T(8,128)(2,1)S(1)} %multiply_convert_fusion.near_0_ref), channel_id=1, source_target_pairs={{0,64},{64,128},{128,192},{192,0},{1,65},{65,129},{129,193},{193,1... | collective-permute-start | bytes 5111816 | tf_op jit(solution)/shard_map/ppermute | solution.py:257
  41.2 1.4 fusion.13.source_ref
  42.6 5.4 %all-to-all-done.1 = bf16[64,2,832]{2,1,0:T(2,128)(2,1)} async-done(((bf16[64,2,832]{2,1,0:T(2,128)(2,1)}), bf16[64,2,832]{2,1,0:T(2,128)(2,1)}, u32[]{:S(2)}, u32[]{:S(2)}) %all-to-all-start.1) | async-done | bytes 213024 | tf_op jit(solution)/shard_map/all_to_all | solution.py:268
  48.0 2.2 %broadcast_in_dim.42 = bf16[3,64,2,832]{3,2,1,0:T(2,128)(2,1)} broadcast(bf16[64,2,832]{2,1,0:T(2,128)(2,1)} %all-to-all-done.1), dimensions={1,2,3} | broadcast | bytes 851968 | tf_op jit(solution)/shard_map/broadcast_in_dim | solution.py:270
  50.2 11.2 %all-to-all-start.2 = ((bf16[3,64,2,832]{3,2,1,0:T(2,128)(2,1)}), bf16[3,64,2,832]{3,2,1,0:T(2,128)(2,1)}, u32[]{:S(2)}, u32[]{:S(2)}) async-start(bf16[3,64,2,832]{3,2,1,0:T(2,128)(2,1)} %broadcast_in_dim.42), calls=%async_computation.2 | async-start | bytes 1376256 | tf_op jit(solution)/shard_map/all_to_all | solution.py:269
  61.4 1.6 collective-permute-done.near_1_ref.weight_ref
  63.0 1.0 shard_map.78
  63.9 5.2 %collective-permute-start.5 = (bf16[448,1024]{1,0:T(8,128)(2,1)}, bf16[448,1024]{1,0:T(8,128)(2,1)}, u32[]{:S(2)}, u32[]{:S(2)}) collective-permute-start(bf16[448,1024]{1,0:T(8,128)(2,1)} %shard_map.78), channel_id=1, source_target_pairs={{0,192},{64,0},{128,64},{192,128},{1,193},{65,1},{129,65},{193,129... | collective-permute-start | bytes 2752520 | tf_op jit(solution)/shard_map/ppermute | solution.py:260
  69.2 12.6 %collective-permute-done.1.far_ref.weight_ref = bf16[832,1024]{1,0:T(8,128)(2,1)} collective-permute-done((bf16[832,1024]{1,0:T(8,128)(2,1)S(1)}, bf16[832,1024]{1,0:T(8,128)(2,1)}, u32[]{:S(2)}, u32[]{:S(2)}) %collective-permute-start.1) | collective-permute-done | bytes 1703968 | tf_op jit(solution)/shard_map/ppermute | solution.py:257
  81.8 2.4 %shard_map.77 = bf16[384,1024]{1,0:T(8,128)(2,1)} custom-call(bf16[832,1024]{1,0:T(8,128)(2,1)} %collective-permute-done.1.far_ref.weight_ref), custom_call_target="tpu_custom_call" | custom-call | flops 20000000000 | bytes 1700000 | tf_op jit(solution)/shard_map/pallas_call | solution.py:144
  84.1 1.9 %collective-permute-start.4 = (bf16[384,1024]{1,0:T(8,128)(2,1)}, bf16[384,1024]{1,0:T(8,128)(2,1)}, u32[]{:S(2)}, u32[]{:S(2)}) collective-permute-start(bf16[384,1024]{1,0:T(8,128)(2,1)} %shard_map.77), channel_id=1, source_target_pairs={{0,64},{64,128},{128,192},{192,0},{1,65},{65,129},{129,193},{193,1... | collective-permute-start | bytes 2359304 | tf_op jit(solution)/shard_map/ppermute | solution.py:257
  86.1 1.6 all-to-all-done.2.rows_ref
  87.7 0.9 copy-done.2
  88.6 1.8 %shard_map.75.acts_ref = bf16[384,832]{1,0:T(8,128)(2,1)S(1)} custom-call(s32[384,1]{1,0:T(8,128)S(1)} %copy-done.2, bf16[3,64,2,832]{3,2,1,0:T(2,128)(2,1)} %all-to-all-done.2.rows_ref), custom_call_target="tpu_custom_call" | custom-call | flops 20000000000 | bytes 1500000 | tf_op jit(solution)/shard_map/pallas_call | solution.py:198
  90.5 4.0 %shard_map.76 = (bf16[2,192,1024]{2,1,0:T(8,128)(2,1)S(1)}, f32[2,192,1024]{2,1,0:T(8,128)S(1)}, bf16[1,192,1024]{2,1,0:T(8,128)(2,1)S(1)}, f32[1,192,1024]{2,1,0:T(8,128)S(1)}) custom-call(bf16[384,832]{1,0:T(8,128)(2,1)S(1)} %shard_map.75.acts_ref, bf16[832,1024]{1,0:T(8,128)(2,1)S(1)} %multiply_convert_fusion.near_0_ref, ...), custom_call_target="tpu_custom_call" | custom-call | flops 1300000000 | bytes 6000000 | tf_op jit(solution)/shard_map/pallas_call | solution.py:175
  94.5 1.9 %collective-permute-start.2 = (bf16[2,192,1024]{2,1,0:T(8,128)(2,1)S(1)}, bf16[2,192,1024]{2,1,0:T(8,128)(2,1)S(1)}, u32[]{:S(2)}, u32[]{:S(2)}) collective-permute-start(bf16[2,192,1024]{2,1,0:T(8,128)(2,1)S(1)} %get-tuple-element.16), channel_id=1, source_target_pairs={{0,1},{1,0},{2,3},{3,2},{4,5},{5,4},{6,7},{7,6},{8,9},{9,8},{10,11... | collective-permute-start | bytes 2359304 | tf_op jit(solution)/shard_map/ppermute | solution.py:278
  96.5 9.8 %collective-permute-done.4.top_ref = bf16[384,1024]{1,0:T(8,128)(2,1)} collective-permute-done((bf16[384,1024]{1,0:T(8,128)(2,1)}, bf16[384,1024]{1,0:T(8,128)(2,1)}, u32[]{:S(2)}, u32[]{:S(2)}) %collective-permute-start.4) | collective-permute-done | bytes 786464 | tf_op jit(solution)/shard_map/ppermute | solution.py:257
  106.3 2.5 %shard_map.79 = (bf16[2,192,1024]{2,1,0:T(8,128)(2,1)S(1)}, f32[2,192,1024]{2,1,0:T(8,128)S(1)}) custom-call(bf16[384,832]{1,0:T(8,128)(2,1)S(1)} %shard_map.75.acts_ref, bf16[384,1024]{1,0:T(8,128)(2,1)} %collective-permute-done.4.top_ref, bf16[448,1024]{1,0:T(8,128)(2,1)} %collective-permute-done.5.low_ref, ...), custom_call_target="tpu_custom_call" | custom-call | flops 1300000000 | bytes 6000000 | tf_op jit(solution)/shard_map/pallas_call | solution.py:175
  108.8 1.9 %collective-permute-start.6 = (bf16[2,192,1024]{2,1,0:T(8,128)(2,1)S(1)}, bf16[2,192,1024]{2,1,0:T(8,128)(2,1)S(1)}, u32[]{:S(2)}, u32[]{:S(2)}) collective-permute-start(bf16[2,192,1024]{2,1,0:T(8,128)(2,1)S(1)} %get-tuple-element.20), channel_id=1, source_target_pairs={{0,1},{1,0},{2,3},{3,2},{4,5},{5,4},{6,7},{7,6},{8,9},{9,8},{10,11... | collective-permute-start | bytes 2359304 | tf_op jit(solution)/shard_map/ppermute | solution.py:278
  110.7 0.2 convert_add_fusion.1
  111.0 3.4 %collective-permute-start.3 = (bf16[2,96,1024]{2,1,0:T(8,128)(2,1)S(1)}, bf16[2,96,1024]{2,1,0:T(8,128)(2,1)S(1)}, u32[]{:S(2)}, u32[]{:S(2)}) collective-permute-start(bf16[2,96,1024]{2,1,0:T(8,128)(2,1)S(1)} %slice.60), channel_id=1, source_target_pairs={{0,2},{2,0},{4,6},{6,4},{8,10},{10,8},{12,14},{14,12},{1,3},{3,1},... | collective-permute-start | bytes 1179656 | tf_op jit(solution)/shard_map/ppermute | solution.py:281
  114.4 0.2 convert_add_fusion
  114.7 1.9 %collective-permute-start.7 = (bf16[2,96,1024]{2,1,0:T(8,128)(2,1)S(1)}, bf16[2,96,1024]{2,1,0:T(8,128)(2,1)S(1)}, u32[]{:S(2)}, u32[]{:S(2)}) collective-permute-start(bf16[2,96,1024]{2,1,0:T(8,128)(2,1)S(1)} %slice.59), channel_id=1, source_target_pairs={{0,14},{2,4},{4,2},{6,8},{8,6},{10,12},{12,10},{14,0},{1,15},{3,5}... | collective-permute-start | bytes 1179656 | tf_op jit(solution)/shard_map/ppermute | solution.py:281
  116.6 7.8 %collective-permute-done.3 = bf16[2,96,1024]{2,1,0:T(8,128)(2,1)S(1)} collective-permute-done((bf16[2,96,1024]{2,1,0:T(8,128)(2,1)S(1)}, bf16[2,96,1024]{2,1,0:T(8,128)(2,1)S(1)}, u32[]{:S(2)}, u32[]{:S(2)}) %collective-permute-start.3) | collective-permute-done | bytes 393248 | tf_op jit(solution)/shard_map/ppermute | solution.py:281
  124.4 0.1 fusion.6
  124.5 3.3 %collective-permute-done.7 = bf16[2,96,1024]{2,1,0:T(8,128)(2,1)S(1)} collective-permute-done((bf16[2,96,1024]{2,1,0:T(8,128)(2,1)S(1)}, bf16[2,96,1024]{2,1,0:T(8,128)(2,1)S(1)}, u32[]{:S(2)}, u32[]{:S(2)}) %collective-permute-start.7) | collective-permute-done | bytes 393248 | tf_op jit(solution)/shard_map/ppermute | solution.py:281
  127.8 0.1 fusion.5
  127.9 1.0 pad_maximum_fusion
  128.9 10.2 %all-to-all-start.3 = ((bf16[16,24,1024]{2,1,0:T(8,128)(2,1)}), bf16[16,24,1024]{2,1,0:T(8,128)(2,1)S(1)}, u32[]{:S(2)}, u32[]{:S(2)}) async-start(bf16[16,24,1024]{2,1,0:T(8,128)(2,1)} %bitcast.3), calls=%async_computation.3 | async-start | bytes 1572864 | tf_op jit(solution)/shard_map/all_to_all | solution.py:292
  139.0 18.1 %all-to-all-done.3 = bf16[16,24,1024]{2,1,0:T(8,128)(2,1)S(1)} async-done(((bf16[16,24,1024]{2,1,0:T(8,128)(2,1)}), bf16[16,24,1024]{2,1,0:T(8,128)(2,1)S(1)}, u32[]{:S(2)}, u32[]{:S(2)}) %all-to-all-start.3) | async-done | bytes 786464 | tf_op jit(solution)/shard_map/all_to_all | solution.py:292
  157.2 0.1 reduce_sum.12
  157.3 3.9 %collective-permute-start.9 = (bf16[24,1024]{1,0:T(8,128)(2,1)S(1)}, bf16[24,1024]{1,0:T(8,128)(2,1)S(1)}, u32[]{:S(2)}, u32[]{:S(2)}) collective-permute-start(bf16[24,1024]{1,0:T(8,128)(2,1)S(1)} %reduce_sum.12), channel_id=1, source_target_pairs={{0,0},{1,1},{2,2},{3,3},{4,4},{5,21},{6,22},{7,23},{8,24},{9,25},{... | collective-permute-start | bytes 147464 | tf_op jit(solution)/shard_map/ppermute | solution.py:298
  161.2 2.3 %collective-permute-start.8 = (bf16[8,1024]{1,0:T(8,128)(2,1)S(1)}, bf16[8,1024]{1,0:T(8,128)(2,1)S(1)}, u32[]{:S(2)}, u32[]{:S(2)}) collective-permute-start(bf16[8,1024]{1,0:T(8,128)(2,1)S(1)} %slice_select_fusion.2), channel_id=1, source_target_pairs={{5,5},{10,42},{21,69},{26,106},{37,197},{42,234},{53,133},{58,170}... | collective-permute-start | bytes 49160 | tf_op jit(solution)/shard_map/ppermute | solution.py:299
  163.5 7.5 %collective-permute-done.8 = bf16[8,1024]{1,0:T(8,128)(2,1)S(1)} collective-permute-done((bf16[8,1024]{1,0:T(8,128)(2,1)S(1)}, bf16[8,1024]{1,0:T(8,128)(2,1)S(1)}, u32[]{:S(2)}, u32[]{:S(2)}) %collective-permute-start.8) | collective-permute-done | bytes 16416 | tf_op jit(solution)/shard_map/ppermute | solution.py:299
  171.0 0.6 pad_maximum_fusion.1
  (17 shorter events, 0.1 us)
Async XLA Ops:
  0.0 0.9 copy-start.1
  0.9 0.7 copy-start.3
  1.6 0.7 copy-start.4
  3.4 22.7 %all-to-all-start = ((bf16[64,2,896]{2,1,0:T(2,128)(2,1)}), bf16[64,2,896]{2,1,0:T(2,128)(2,1)}, u32[]{:S(2)}, u32[]{:S(2)}) async-start(bf16[64,2,896]{2,1,0:T(2,128)(2,1)} %shard_map.73), calls=%async_computation | async-start | bytes 458752 | tf_op jit(solution)/shard_map/all_to_all | solution.py:266
  18.0 8.1 %copy-start.5 = (bf16[128,128]{1,0:T(8,128)(2,1)S(1)}, bf16[128,128]{1,0:T(8,128)(2,1)}, u32[]{:S(2)}) copy-start(bf16[128,128]{1,0:T(8,128)(2,1)} %constant.129.clone.rows_ref) | copy-start | bytes 98308
  18.0 8.1 %copy-start.6 = (bf16[128,128]{1,0:T(8,128)(2,1)S(1)}, bf16[128,128]{1,0:T(8,128)(2,1)}, u32[]{:S(2)}) copy-start(bf16[128,128]{1,0:T(8,128)(2,1)} %constant.130.clone.lanes_ref) | copy-start | bytes 98308
  21.8 41.2 %collective-permute-start = (bf16[832,1024]{1,0:T(8,128)(2,1)S(1)}, bf16[832,1024]{1,0:T(8,128)(2,1)S(1)}, u32[]{:S(2)}, u32[]{:S(2)}) collective-permute-start(bf16[832,1024]{1,0:T(8,128)(2,1)S(1)} %multiply_convert_fusion.near_0_ref), channel_id=1, source_target_pairs={{0,192},{64,0},{128,64},{192,128},{1,193},{65,1},{129,65},{193,129... | collective-permute-start | bytes 5111816 | tf_op jit(solution)/shard_map/ppermute | solution.py:260
  27.9 0.7 copy-start
  28.6 19.4 %all-to-all-start.1 = ((bf16[64,2,832]{2,1,0:T(2,128)(2,1)}), bf16[64,2,832]{2,1,0:T(2,128)(2,1)}, u32[]{:S(2)}, u32[]{:S(2)}) async-start(bf16[64,2,832]{2,1,0:T(2,128)(2,1)} %copy-done), calls=%async_computation.1 | async-start | bytes 458752 | tf_op jit(solution)/shard_map/all_to_all | solution.py:268
  39.3 42.5 %collective-permute-start.1 = (bf16[832,1024]{1,0:T(8,128)(2,1)S(1)}, bf16[832,1024]{1,0:T(8,128)(2,1)}, u32[]{:S(2)}, u32[]{:S(2)}) collective-permute-start(bf16[832,1024]{1,0:T(8,128)(2,1)S(1)} %multiply_convert_fusion.near_0_ref), channel_id=1, source_target_pairs={{0,64},{64,128},{128,192},{192,0},{1,65},{65,129},{129,193},{193,1... | collective-permute-start | bytes 5111816 | tf_op jit(solution)/shard_map/ppermute | solution.py:257
  50.2 37.5 %all-to-all-start.2 = ((bf16[3,64,2,832]{3,2,1,0:T(2,128)(2,1)}), bf16[3,64,2,832]{3,2,1,0:T(2,128)(2,1)}, u32[]{:S(2)}, u32[]{:S(2)}) async-start(bf16[3,64,2,832]{3,2,1,0:T(2,128)(2,1)} %broadcast_in_dim.42), calls=%async_computation.2 | async-start | bytes 1376256 | tf_op jit(solution)/shard_map/all_to_all | solution.py:269
  63.9 42.4 %collective-permute-start.5 = (bf16[448,1024]{1,0:T(8,128)(2,1)}, bf16[448,1024]{1,0:T(8,128)(2,1)}, u32[]{:S(2)}, u32[]{:S(2)}) collective-permute-start(bf16[448,1024]{1,0:T(8,128)(2,1)} %shard_map.78), channel_id=1, source_target_pairs={{0,192},{64,0},{128,64},{192,128},{1,193},{65,1},{129,65},{193,129... | collective-permute-start | bytes 2752520 | tf_op jit(solution)/shard_map/ppermute | solution.py:260
  84.1 22.2 %collective-permute-start.4 = (bf16[384,1024]{1,0:T(8,128)(2,1)}, bf16[384,1024]{1,0:T(8,128)(2,1)}, u32[]{:S(2)}, u32[]{:S(2)}) collective-permute-start(bf16[384,1024]{1,0:T(8,128)(2,1)} %shard_map.77), channel_id=1, source_target_pairs={{0,64},{64,128},{128,192},{192,0},{1,65},{65,129},{129,193},{193,1... | collective-permute-start | bytes 2359304 | tf_op jit(solution)/shard_map/ppermute | solution.py:257
  87.7 0.9 copy-start.2
  94.5 16.2 %collective-permute-start.2 = (bf16[2,192,1024]{2,1,0:T(8,128)(2,1)S(1)}, bf16[2,192,1024]{2,1,0:T(8,128)(2,1)S(1)}, u32[]{:S(2)}, u32[]{:S(2)}) collective-permute-start(bf16[2,192,1024]{2,1,0:T(8,128)(2,1)S(1)} %get-tuple-element.16), channel_id=1, source_target_pairs={{0,1},{1,0},{2,3},{3,2},{4,5},{5,4},{6,7},{7,6},{8,9},{9,8},{10,11... | collective-permute-start | bytes 2359304 | tf_op jit(solution)/shard_map/ppermute | solution.py:278
  108.8 5.6 %collective-permute-start.6 = (bf16[2,192,1024]{2,1,0:T(8,128)(2,1)S(1)}, bf16[2,192,1024]{2,1,0:T(8,128)(2,1)S(1)}, u32[]{:S(2)}, u32[]{:S(2)}) collective-permute-start(bf16[2,192,1024]{2,1,0:T(8,128)(2,1)S(1)} %get-tuple-element.20), channel_id=1, source_target_pairs={{0,1},{1,0},{2,3},{3,2},{4,5},{5,4},{6,7},{7,6},{8,9},{9,8},{10,11... | collective-permute-start | bytes 2359304 | tf_op jit(solution)/shard_map/ppermute | solution.py:278
  111.0 13.4 %collective-permute-start.3 = (bf16[2,96,1024]{2,1,0:T(8,128)(2,1)S(1)}, bf16[2,96,1024]{2,1,0:T(8,128)(2,1)S(1)}, u32[]{:S(2)}, u32[]{:S(2)}) collective-permute-start(bf16[2,96,1024]{2,1,0:T(8,128)(2,1)S(1)} %slice.60), channel_id=1, source_target_pairs={{0,2},{2,0},{4,6},{6,4},{8,10},{10,8},{12,14},{14,12},{1,3},{3,1},... | collective-permute-start | bytes 1179656 | tf_op jit(solution)/shard_map/ppermute | solution.py:281
  114.7 13.1 %collective-permute-start.7 = (bf16[2,96,1024]{2,1,0:T(8,128)(2,1)S(1)}, bf16[2,96,1024]{2,1,0:T(8,128)(2,1)S(1)}, u32[]{:S(2)}, u32[]{:S(2)}) collective-permute-start(bf16[2,96,1024]{2,1,0:T(8,128)(2,1)S(1)} %slice.59), channel_id=1, source_target_pairs={{0,14},{2,4},{4,2},{6,8},{8,6},{10,12},{12,10},{14,0},{1,15},{3,5}... | collective-permute-start | bytes 1179656 | tf_op jit(solution)/shard_map/ppermute | solution.py:281
  128.9 28.3 %all-to-all-start.3 = ((bf16[16,24,1024]{2,1,0:T(8,128)(2,1)}), bf16[16,24,1024]{2,1,0:T(8,128)(2,1)S(1)}, u32[]{:S(2)}, u32[]{:S(2)}) async-start(bf16[16,24,1024]{2,1,0:T(8,128)(2,1)} %bitcast.3), calls=%async_computation.3 | async-start | bytes 1572864 | tf_op jit(solution)/shard_map/all_to_all | solution.py:292
  157.3 13.7 %collective-permute-start.9 = (bf16[24,1024]{1,0:T(8,128)(2,1)S(1)}, bf16[24,1024]{1,0:T(8,128)(2,1)S(1)}, u32[]{:S(2)}, u32[]{:S(2)}) collective-permute-start(bf16[24,1024]{1,0:T(8,128)(2,1)S(1)} %reduce_sum.12), channel_id=1, source_target_pairs={{0,0},{1,1},{2,2},{3,3},{4,4},{5,21},{6,22},{7,23},{8,24},{9,25},{... | collective-permute-start | bytes 147464 | tf_op jit(solution)/shard_map/ppermute | solution.py:298
  161.2 9.8 %collective-permute-start.8 = (bf16[8,1024]{1,0:T(8,128)(2,1)S(1)}, bf16[8,1024]{1,0:T(8,128)(2,1)S(1)}, u32[]{:S(2)}, u32[]{:S(2)}) collective-permute-start(bf16[8,1024]{1,0:T(8,128)(2,1)S(1)} %slice_select_fusion.2), channel_id=1, source_target_pairs={{5,5},{10,42},{21,69},{26,106},{37,197},{42,234},{53,133},{58,170}... | collective-permute-start | bytes 49160 | tf_op jit(solution)/shard_map/ppermute | solution.py:299
